TPU v7x, 32 devices: a whole 2x2x4 slice. The times are simulated.
32 devices in a mesh: row: 4 (over y, x), col: 8 (over z, core).
Axes of the slice: x: 2, y: 2, z: 4, core: 2. Of those that a mesh axis runs over, the one named last changes fastest.
Arguments:
- layer_stack: bfloat16 [8, 8192, 2048], P(None, ('row', 'col')), may hold values from -6 to 6
- mix_coeffs: float32 [8192, 4, 8], P(('row', 'col')), may hold values from -3 to 3
- prefix: int32 [8], P('row'), may hold values from 0 to 1024
- ln_gain: float32 [4, 2048], replicated, may hold values from 0.5 to 1.5
- ln_bias: float32 [4, 2048], replicated, may hold values from -0.3 to 0.3
- qkv_weight: bfloat16 [3, 2048, 2048], P(None, 'row', 'col'), may hold values from -0.125 to 0.125
- qkv_bias: float32 [3, 2048], P(None, 'col'), may hold values from -0.15 to 0.15
- out_weight: bfloat16 [2048, 2048], P('col', 'row'), may hold values from -3 to 3
- out_bias: float32 [2048], replicated, may hold values from -0.6 to 0.6
- up_weight: bfloat16 [2048, 8192], P('row', 'col'), may hold values from -0.125 to 0.125
- up_bias: float32 [8192], P('col'), may hold values from -1.5 to 1.5
- down_weight: bfloat16 [8192, 2048], P('col', 'row'), may hold values from -0.0625 to 0.0625
- down_bias: float32 [2048], replicated, may hold values from -1.5 to 1.5
- mix_gain: float32 [2048], replicated, may hold values from 0.5 to 1.5
- mix_in: float32 [2048, 36], replicated, may hold values from -0.125 to 0.125
- mix_out: float32 [36, 36], replicated, may hold values from -1 to 1
- out_grad: bfloat16 [8192, 2048], P(('row', 'col')), may hold values from -6 to 6
- coeff_grad: float32 [8192, 36], P(('row', 'col')), may hold values from -6 to 6
Outputs:
- layer_out: float32 [8192, 2048], P(('row', 'col'))
- coeff_out: float32 [8192, 36], P(('row', 'col'))
- stack_grad: float32 [8, 8192, 2048], P(None, ('row', 'col'))
- coeffs_grad: float32 [8192, 4, 8], P(('row', 'col'))
- ln_gain_grad: float32 [4, 2048], replicated
- ln_bias_grad: float32 [4, 2048], replicated
- qkv_weight_grad: float32 [3, 2048, 2048], P(None, 'row', 'col')
- qkv_bias_grad: float32 [3, 2048], P(None, 'col')
- out_weight_grad: float32 [2048, 2048], P('col', 'row')
- out_bias_grad: float32 [2048], replicated
- up_weight_grad: float32 [2048, 8192], P('row', 'col')
- up_bias_grad: float32 [8192], P('col')
- down_weight_grad: float32 [8192, 2048], P('col', 'row')
- down_bias_grad: float32 [2048], replicated
- mix_gain_grad: float32 [2048], replicated
- mix_in_grad: float32 [2048, 36], replicated
- mix_out_grad: float32 [36, 36], replicated
Inputs may be any that keep to these rules, and one draw needn't show every extreme that they name: prefix[b] leading tokens of sequence b see each other in both directions; the rest see only earlier tokens and that prefix.
All inputs are finite; a program needn't handle non-finite values.
Results may differ from a plain program's by a relative error of at most 0.039.
Values may be sent and summed in bfloat16 or wider, within the bound.
No kernel may reach another device: no remote copies, remote signals or barrier semaphores. Data moves between devices by JAX's collectives and lax.ppermute only.
A program may use at most 384 MiB of HBM per device.

v0:
```python
import jax
import jax.numpy as jnp
from jax import lax
from jax.sharding import PartitionSpec as P

HD = 128
ROT = 32
LEN = 1024


eps_layer = 1e-05
eps_rms = 1e-06
finest = lax.Precision.HIGHEST


def layer_norm(values, norm_gain, norm_bias):
    centred = values - jnp.mean(values, axis=-1, keepdims=True)
    spread = jnp.mean(centred * centred, axis=-1, keepdims=True)
    return centred * lax.rsqrt(spread + eps_layer) * norm_gain + norm_bias


def front(layer_stack, mix_coeffs, ln_gain, ln_bias):
    streams = jnp.einsum("tsj,jtd->tsd", mix_coeffs, layer_stack, precision=finest)
    return (layer_norm(streams[:, :3], ln_gain[:3], ln_bias[:3]), streams[:, 3])


def middle(hidden, ln_gain, ln_bias):
    return layer_norm(hidden, ln_gain[3], ln_bias[3])


def mixing(layer_out, mix_gain, mix_in, mix_out):
    scaled = (
        layer_out
        * lax.rsqrt(jnp.mean(layer_out * layer_out, axis=-1, keepdims=True) + eps_rms)
        * mix_gain
    )
    middle_act = jax.nn.gelu(
        jnp.dot(scaled, mix_in, precision=finest, preferred_element_type=jnp.float32),
        approximate=False,
    )
    return jnp.dot(middle_act, mix_out, precision=finest, preferred_element_type=jnp.float32)


def erf_gelu(values):
    return jax.nn.gelu(values, approximate=False)


def rotary(seq_length):
    half_rot = ROT // 2
    inv_freq = 10000.0 ** (-(jnp.arange(half_rot, dtype=jnp.float32) * 2.0) / ROT)
    angles = jnp.arange(seq_length, dtype=jnp.float32)[:, None] * inv_freq[None, :]
    angles = jnp.concatenate([angles, angles], axis=1)
    return (jnp.cos(angles), jnp.sin(angles))


def rotate(values, cos_table, sine_table):
    half_rot = ROT // 2
    turned = jnp.concatenate([-values[..., half_rot:ROT], values[..., :half_rot]], axis=-1)
    rotated = values[..., :ROT] * cos_table[:, None, :] + turned * sine_table[:, None, :]
    return jnp.concatenate([rotated, values[..., ROT:]], axis=-1)


def tokens_col(values):
    return lax.all_gather(values, "col", axis=0, tiled=True)


def split_features(values):
    return lax.all_to_all(values, "row", split_axis=2, concat_axis=0, tiled=True)


def join_features(values):
    return lax.all_to_all(values, "row", split_axis=0, concat_axis=2, tiled=True)


def tokens_row(values):
    return lax.all_gather(values, "row", axis=0, tiled=True)


def blocks_col(values):
    return lax.all_gather(values, "col", axis=1, tiled=True)


def sum_row(term_fn, shard_rows):
    return lax.psum_scatter(
        term_fn(jnp.int32(0), shard_rows * lax.axis_size("row")).astype(jnp.bfloat16),
        "row",
        scatter_dimension=0,
        tiled=True,
    ).astype(jnp.float32)


def sum_col(term_fn, shard_rows):
    return lax.psum_scatter(
        term_fn(jnp.int32(0), shard_rows * lax.axis_size("col")).astype(jnp.bfloat16),
        "col",
        scatter_dimension=0,
        tiled=True,
    ).astype(jnp.float32)


def col_major(values, row_count, col_count):
    block_rows = values.shape[0] // (row_count * col_count)
    shaped = values.reshape((row_count, col_count, block_rows) + values.shape[1:])
    return shaped


def scores_of(queries, key_rows, prefix_len):
    positions = jnp.arange(queries.shape[0], dtype=jnp.int32)
    allowed = (positions[None, :] <= positions[:, None]) | (positions[None, :] < prefix_len)
    raw_scores = jnp.einsum(
        "qhd,khd->hqk", queries, key_rows, preferred_element_type=jnp.float32
    ) * HD ** (-0.5)
    return jnp.where(allowed[None], raw_scores, -1e30)


def attend(block_items):
    queries, key_rows, value_rows, prefix_len = block_items
    raw_scores = scores_of(queries, key_rows, prefix_len)
    row_max = jnp.max(raw_scores, axis=-1, keepdims=True)
    exp_scores = jnp.exp(raw_scores - row_max)
    exp_total = jnp.sum(exp_scores, axis=-1, keepdims=True)
    probs_low = (exp_scores / exp_total).astype(jnp.bfloat16)
    head_rows = jnp.einsum(
        "hqk,khd->qhd", probs_low, value_rows, preferred_element_type=jnp.float32
    )
    return (head_rows, row_max + jnp.log(exp_total))


def attend_back(block_items):
    queries, key_rows, value_rows, log_total, grad_rows, prefix_len = block_items
    score_scale = HD ** (-0.5)
    probs_full = jnp.exp(scores_of(queries, key_rows, prefix_len) - log_total)
    grad_probs = jnp.einsum(
        "qhd,khd->hqk", grad_rows, value_rows, preferred_element_type=jnp.float32
    )
    grad_value = jnp.einsum(
        "hqk,qhd->khd",
        probs_full.astype(jnp.bfloat16),
        grad_rows,
        preferred_element_type=jnp.float32,
    )
    row_inner = jnp.sum(grad_probs * probs_full, axis=-1, keepdims=True)
    grad_scores = (probs_full * (grad_probs - row_inner)).astype(jnp.bfloat16)
    grad_query = (
        jnp.einsum("hqk,khd->qhd", grad_scores, key_rows, preferred_element_type=jnp.float32)
        * score_scale
    )
    grad_key = (
        jnp.einsum("hqk,qhd->khd", grad_scores, queries, preferred_element_type=jnp.float32)
        * score_scale
    )
    return (grad_query, grad_key, grad_value)


def on_device(
    layer_stack,
    mix_coeffs,
    prefix,
    ln_gain,
    ln_bias,
    qkv_weight,
    qkv_bias,
    out_weight,
    out_bias,
    up_weight,
    up_bias,
    down_weight,
    down_bias,
    mix_gain,
    mix_in,
    mix_out,
    out_grad,
    coeff_grad,
):
    row_count = lax.axis_size("row")
    col_count = lax.axis_size("col")
    row_index = lax.axis_index("row")
    col_index = lax.axis_index("col")
    local_tokens = layer_stack.shape[1]
    row_tokens = local_tokens * col_count
    col_tokens = local_tokens * row_count
    head_width = qkv_bias.shape[1]
    feat_block = qkv_weight.shape[1]
    head_shape = (prefix.shape[0], LEN, head_width // HD, HD)
    cos_table, sine_table = rotary(LEN)
    out_bias_block = lax.dynamic_slice_in_dim(out_bias, row_index * feat_block, feat_block, 0)
    down_bias_block = lax.dynamic_slice_in_dim(down_bias, row_index * feat_block, feat_block, 0)
    (normed, residual), front_pull = jax.vjp(
        front, layer_stack.astype(jnp.float32), mix_coeffs, ln_gain, ln_bias
    )
    normed_rows = tokens_col(normed.astype(jnp.bfloat16))
    normed_all = split_features(normed_rows)

    def qkv_term(start, count):
        return jnp.einsum(
            "tsd,sde->tse", normed_all, qkv_weight, preferred_element_type=jnp.float32
        )

    projected = sum_row(qkv_term, row_tokens) + qkv_bias
    query_rot = rotate(projected[:, 0].reshape(head_shape), cos_table, sine_table).astype(
        jnp.bfloat16
    )
    key_rot = rotate(projected[:, 1].reshape(head_shape), cos_table, sine_table).astype(
        jnp.bfloat16
    )
    value_rows = projected[:, 2].reshape(head_shape).astype(jnp.bfloat16)
    head_rows, log_total = lax.map(attend, (query_rot, key_rot, value_rows, prefix))
    head_out = head_rows.reshape(row_tokens, head_width).astype(jnp.bfloat16)
    head_all = tokens_row(head_out)

    def attn_term(start, count):
        picked = col_major(head_all, row_count, col_count)
        return jnp.einsum(
            "akte,ed->katd", picked, out_weight, preferred_element_type=jnp.float32
        ).reshape(count, feat_block)

    attn_block = (sum_col(attn_term, col_tokens) + out_bias_block).astype(jnp.bfloat16)
    attn_out = join_features(attn_block[:, None, :])[:, 0]
    hidden = residual + attn_out.astype(jnp.float32)
    normed2, middle_pull = jax.vjp(middle, hidden, ln_gain, ln_bias)
    normed2_rows = tokens_col(normed2.astype(jnp.bfloat16))
    normed2_all = split_features(normed2_rows[:, None, :])[:, 0]

    def up_term(start, count):
        return jnp.dot(normed2_all, up_weight, preferred_element_type=jnp.float32)

    up_pre = sum_row(up_term, row_tokens) + up_bias
    act_full, gelu_pull = jax.vjp(erf_gelu, up_pre)
    act_out = act_full.astype(jnp.bfloat16)
    act_all = tokens_row(act_out)

    def down_term(start, count):
        picked = col_major(act_all, row_count, col_count)
        return jnp.einsum(
            "aktf,fd->katd", picked, down_weight, preferred_element_type=jnp.float32
        ).reshape(count, feat_block)

    down_block = (sum_col(down_term, col_tokens) + down_bias_block).astype(jnp.bfloat16)
    down_out = join_features(down_block[:, None, :])[:, 0]
    layer_out = hidden + down_out.astype(jnp.float32)
    coeff_out, mixing_pull = jax.vjp(mixing, layer_out, mix_gain, mix_in, mix_out)
    grad_layer, mix_gain_part, mix_in_part, mix_out_part = mixing_pull(coeff_grad)
    grad_layer = grad_layer + out_grad.astype(jnp.float32)
    grad_down = grad_layer.astype(jnp.bfloat16)
    down_bias_part = jnp.sum(grad_down.astype(jnp.float32), axis=0)
    down_split = split_features(grad_down[:, None, :]).reshape(row_count, local_tokens, feat_block)
    grad_down_all = blocks_col(down_split).reshape(row_tokens * row_count, feat_block)
    down_weight_grad = jnp.einsum(
        "tf,td->fd", act_all, grad_down_all, preferred_element_type=jnp.float32
    )

    def act_term(start, count):
        return jnp.einsum(
            "td,fd->tf", grad_down_all, down_weight, preferred_element_type=jnp.float32
        )

    grad_act = sum_row(act_term, row_tokens)
    grad_up = gelu_pull(grad_act)[0].astype(jnp.bfloat16)
    up_bias_part = jnp.sum(grad_up.astype(jnp.float32), axis=0)
    grad_up_all = tokens_row(grad_up)
    up_weight_grad = jnp.einsum(
        "td,tf->df", normed2_all, grad_up_all, preferred_element_type=jnp.float32
    )

    def normed2_term(start, count):
        picked = col_major(grad_up_all, row_count, col_count)
        return jnp.einsum(
            "aktf,df->katd", picked, up_weight, preferred_element_type=jnp.float32
        ).reshape(count, feat_block)

    grad_normed2_block = sum_col(normed2_term, col_tokens).astype(jnp.bfloat16)
    grad_normed2 = join_features(grad_normed2_block[:, None, :])[:, 0]
    grad_hidden, gain_late, bias_late = middle_pull(grad_normed2.astype(jnp.float32))
    grad_hidden = grad_hidden + grad_layer
    grad_attn = grad_hidden.astype(jnp.bfloat16)
    out_bias_part = jnp.sum(grad_attn.astype(jnp.float32), axis=0)
    attn_split = split_features(grad_attn[:, None, :]).reshape(row_count, local_tokens, feat_block)
    grad_attn_all = blocks_col(attn_split).reshape(row_tokens * row_count, feat_block)
    out_weight_grad = jnp.einsum(
        "te,td->ed", head_all, grad_attn_all, preferred_element_type=jnp.float32
    )

    def heads_term(start, count):
        return jnp.einsum(
            "td,ed->te", grad_attn_all, out_weight, preferred_element_type=jnp.float32
        )

    grad_heads = sum_row(heads_term, row_tokens).astype(jnp.bfloat16)
    grad_query, grad_key, grad_value = lax.map(
        attend_back,
        (query_rot, key_rot, value_rows, log_total, grad_heads.reshape(head_shape), prefix),
    )
    grad_query = rotate(grad_query, cos_table, -sine_table)
    grad_key = rotate(grad_key, cos_table, -sine_table)
    grad_projected = (
        jnp.stack([grad_query, grad_key, grad_value], axis=2)
        .reshape(row_tokens, 3, head_width)
        .astype(jnp.bfloat16)
    )
    qkv_bias_part = jnp.sum(grad_projected.astype(jnp.float32), axis=0)
    grad_projected_all = tokens_row(grad_projected)
    qkv_weight_grad = jnp.einsum(
        "tsd,tse->sde", normed_all, grad_projected_all, preferred_element_type=jnp.float32
    )

    def normed_term(start, count):
        picked = col_major(grad_projected_all, row_count, col_count)
        return jnp.einsum(
            "aktse,sde->katsd", picked, qkv_weight, preferred_element_type=jnp.float32
        ).reshape(count, 3, feat_block)

    grad_normed = join_features(sum_col(normed_term, col_tokens).astype(jnp.bfloat16))
    stack_grad, coeffs_grad, gain_early, bias_early = front_pull(
        (grad_normed.astype(jnp.float32), grad_hidden)
    )
    up_width = up_bias.shape[0]
    up_pad = lax.dynamic_update_slice(
        jnp.zeros((up_width * col_count,), jnp.float32), up_bias_part, (col_index * up_width,)
    )
    qkv_pad = lax.dynamic_update_slice(
        jnp.zeros((3, head_width * col_count), jnp.float32),
        qkv_bias_part,
        (jnp.int32(0), col_index * head_width),
    )
    summed = lax.psum(
        (
            gain_early + gain_late,
            bias_early + bias_late,
            mix_gain_part,
            mix_in_part,
            mix_out_part,
            out_bias_part,
            down_bias_part,
            up_pad,
            qkv_pad,
        ),
        ("row", "col"),
    )
    up_bias_grad = lax.dynamic_slice_in_dim(summed[7], col_index * up_width, up_width, 0)
    qkv_bias_grad = lax.dynamic_slice_in_dim(summed[8], col_index * head_width, head_width, 1)
    return (
        layer_out,
        coeff_out,
        stack_grad,
        coeffs_grad,
        summed[0],
        summed[1],
        qkv_weight_grad,
        qkv_bias_grad,
        out_weight_grad,
        summed[5],
        up_weight_grad,
        up_bias_grad,
        down_weight_grad,
        summed[6],
        summed[2],
        summed[3],
        summed[4],
    )


def solution(mesh):
    in_specs = (
        P(None, ("row", "col"), None),
        P(("row", "col"), None, None),
        P("row"),
        P(),
        P(),
        P(None, "row", "col"),
        P(None, "col"),
        P("col", "row"),
        P(),
        P("row", "col"),
        P("col"),
        P("col", "row"),
        P(),
        P(),
        P(),
        P(),
        P(("row", "col"), None),
        P(("row", "col"), None),
    )
    out_specs = (
        P(("row", "col"), None),
        P(("row", "col"), None),
        P(None, ("row", "col"), None),
        P(("row", "col"), None, None),
        P(),
        P(),
        P(None, "row", "col"),
        P(None, "col"),
        P("col", "row"),
        P(),
        P("row", "col"),
        P("col"),
        P("col", "row"),
        P(),
        P(),
        P(),
        P(),
    )
    return jax.shard_map(
        on_device, mesh=mesh, in_specs=in_specs, out_specs=out_specs, check_vma=False
    )
```

profile of v0, /device:TPU:0, one launch (start us, length us, event | category | flops | bytes accessed | tf_op | source)
XLA Modules:
  0.0 3649.5 jit_solution(6101477330911539510)
XLA Ops:
  39.4 222.7 %all-gather.11.cloned.1.call-done = bf16[2048,3,2048]{2,0,1:T(8,128)(2,1)} async-done(((bf16[256,3,2048]{2,0,1:T(8,128)(2,1)}), bf16[2048,3,2048]{2,0,1:T(8,128)(2,1)}) %all-gather.11.cloned.1.call-update) | async-done | bytes 25165840 | tf_op jit(solution)/shard_map/all_gather | solution.py:64
  262.1 53.8 %copy.375 = bf16[2048,3,2048]{0,1,2:T(4,128)(2,1)} copy(bf16[2048,3,2048]{2,0,1:T(8,128)(2,1)} %all-gather.11.cloned.1.call-done) | data formatting | bytes 50331648 | tf_op jit(solution)/shard_map/all_gather | solution.py:64
  315.9 369.3 %all_to_all.99 = bf16[2048,3,2048]{0,1,2:T(4,128)(2,1)S(1)} all-to-all(bf16[2048,3,2048]{0,1,2:T(4,128)(2,1)} %copy.375), channel_id=1, replica_groups=mesh['row'=4,'col'=8] {'row'}, dimensions={2} | all-to-all | bytes 50331648 | tf_op jit(solution)/shard_map/all_to_all | solution.py:68
  685.2 35.0 copy.376
  720.2 33.2 copy.377
  772.2 113.2 %reduce-scatter.9.cloned.1.call-done = bf16[2048,3,256]{2,0,1:T(8,128)(2,1)} async-done(((bf16[8192,3,256]{2,0,1:T(8,128)(2,1)}), bf16[2048,3,256]{2,0,1:T(8,128)(2,1)}) %reduce-scatter.9.cloned.1.call-update) | async-done | bytes 3145744 | tf_op jit(solution)/shard_map/reduce_scatter | solution.py:84
  949.0 39.6 %while.28 = (s32[]{:T(128)}, bf16[2,1024,2,128]{1,3,2,0:T(8,128)(2,1)}, f32[2,2,1024,1]{2,1,3,0:T(2,128)S(1)}, bf16[2,1024,2,128]{3,2,1,0:T(2,128)(2,1)}, s32[2]...) while((s32[]{:T(128)}, ...), condition=%wide.region_6.7_spmd.clone, body=%wide.region_3.6_spmd.sunk.clone | while | flops 1101003776 | bytes 76091064 | solution.py:207
  992.5 52.8 %all-gather.13.cloned.1.call-done = bf16[8192,256]{1,0:T(8,128)(2,1)} async-done(((bf16[2048,256]{1,0:T(8,128)(2,1)}), bf16[8192,256]{1,0:T(8,128)(2,1)}) %all-gather.13.cloned.1.call-update) | async-done | bytes 4194320 | tf_op jit(solution)/shard_map/all_gather | solution.py:76
  1061.6 89.0 %reduce-scatter.11.cloned.1.call-done = bf16[1024,512]{1,0:T(8,128)(2,1)} async-done(((bf16[8192,512]{1,0:T(8,128)(2,1)}), bf16[1024,512]{1,0:T(8,128)(2,1)}) %reduce-scatter.11.cloned.1.call-update) | async-done | bytes 1048592 | tf_op jit(solution)/shard_map/reduce_scatter | solution.py:93
  1183.8 81.8 %all-gather.15.cloned.1.call-done = bf16[2048,2048]{1,0:T(8,128)(2,1)} async-done(((bf16[256,2048]{1,0:T(8,128)(2,1)}), bf16[2048,2048]{1,0:T(8,128)(2,1)}) %all-gather.15.cloned.1.call-update) | async-done | bytes 8388624 | tf_op jit(solution)/shard_map/all_gather | solution.py:64
  1265.5 39.3 %copy.394 = bf16[2048,1,2048]{0,1,2:T(2,128)(2,1)} copy(bf16[2048,1,2048]{2,0,1:T(8,128)(2,1)} %bitcast.322) | data formatting | bytes 16777216 | tf_op jit(solution)/shard_map/broadcast_in_dim | solution.py:222
  1304.9 51.0 %reduce.9 = bf16[2048,2048]{1,0:T(8,128)(2,1)} reduce(bf16[2048,1,2048]{2,1,0:T(2,128)(2,1)} %bitcast.305, bf16[]{:T(256)} %broadcast.353), dimensions={1}, to_apply=%bitcast.190.reduce_sub_computation | reduce | bytes 16777218
  1365.8 101.5 %all_to_all.100 = bf16[4,2,524288]{2,1,0:T(2,128)(2,1)} all-to-all(bf16[4,2,524288]{2,1,0:T(2,128)(2,1)} %reshape.410), channel_id=1, replica_groups=mesh['row'=4,'col'=8] {'row'}, dimensions={0} | all-to-all | bytes 16777216 | tf_op jit(solution)/shard_map/all_to_all | solution.py:68
  1519.6 151.0 %reduce-scatter.13.cloned.1.call-done = bf16[2048,1024]{1,0:T(8,128)(2,1)} async-done(((bf16[8192,1024]{1,0:T(8,128)(2,1)}), bf16[2048,1024]{1,0:T(8,128)(2,1)}) %reduce-scatter.13.cloned.1.call-update) | async-done | bytes 4194320 | tf_op jit(solution)/shard_map/reduce_scatter | solution.py:84
  1670.6 20.7 multiply_convert_fusion.1
  1691.6 157.3 %all-gather.17.cloned.1.call-done = bf16[8192,1024]{1,0:T(8,128)(2,1)} async-done(((bf16[2048,1024]{1,0:T(8,128)(2,1)}), bf16[8192,1024]{1,0:T(8,128)(2,1)}) %all-gather.17.cloned.1.call-update) | async-done | bytes 16777232 | tf_op jit(solution)/shard_map/all_gather | solution.py:76
  1874.1 89.0 %reduce-scatter.15.cloned.1.call-done = bf16[1024,512]{1,0:T(8,128)(2,1)} async-done(((bf16[8192,512]{1,0:T(8,128)(2,1)}), bf16[1024,512]{1,0:T(8,128)(2,1)}) %reduce-scatter.15.cloned.1.call-update) | async-done | bytes 1048592 | tf_op jit(solution)/shard_map/reduce_scatter | solution.py:93
  2028.5 17.9 all_to_all.101
  2053.6 82.1 %all-gather.23.cloned.1.call-done = bf16[4,2048,1,512]{1,3,0,2:T(8,128)(2,1)} async-done(((bf16[4,256,1,512]{1,3,0,2:T(8,128)(2,1)}), bf16[4,2048,1,512]{1,3,0,2:T(8,128)(2,1)}) %all-gather.23.cloned.1.call-update) | async-done | bytes 8388624 | tf_op jit(solution)/shard_map/all_gather | solution.py:80
  2163.2 152.2 %reduce-scatter.17.cloned.1.call-done = bf16[2048,1024]{1,0:T(8,128)(2,1)} async-done(((bf16[8192,1024]{1,0:T(8,128)(2,1)}), bf16[2048,1024]{1,0:T(8,128)(2,1)}) %reduce-scatter.17.cloned.1.call-update) | async-done | bytes 4194320 | tf_op jit(solution)/shard_map/reduce_scatter | solution.py:84
  2325.5 157.5 %all-gather.19.cloned.1.call-done = bf16[8192,1024]{1,0:T(8,128)(2,1)} async-done(((bf16[2048,1024]{1,0:T(8,128)(2,1)}), bf16[8192,1024]{1,0:T(8,128)(2,1)}) %all-gather.19.cloned.1.call-update) | async-done | bytes 16777232 | tf_op jit(solution)/shard_map/all_gather | solution.py:76
  2507.5 89.8 %reduce-scatter.19.cloned.1.call-done = bf16[1024,512]{1,0:T(8,128)(2,1)} async-done(((bf16[8192,512]{1,0:T(8,128)(2,1)}), bf16[1024,512]{1,0:T(8,128)(2,1)}) %reduce-scatter.19.cloned.1.call-update) | async-done | bytes 1048592 | tf_op jit(solution)/shard_map/reduce_scatter | solution.py:93
  2660.2 82.4 %all-gather.25.cloned.1.call-done = bf16[4,2048,1,512]{1,3,0,2:T(8,128)(2,1)} async-done(((bf16[4,256,1,512]{1,3,0,2:T(8,128)(2,1)}), bf16[4,2048,1,512]{1,3,0,2:T(8,128)(2,1)}) %all-gather.25.cloned.1.call-update) | async-done | bytes 8388624 | tf_op jit(solution)/shard_map/all_gather | solution.py:80
  2762.4 50.6 %reduce-scatter.21.cloned.1.call-done = bf16[2048,256]{1,0:T(8,128)(2,1)} async-done(((bf16[8192,256]{1,0:T(8,128)(2,1)}), bf16[2048,256]{1,0:T(8,128)(2,1)}) %reduce-scatter.21.cloned.1.call-update) | async-done | bytes 1048592 | tf_op jit(solution)/shard_map/reduce_scatter | solution.py:84
  2815.2 37.6 %while.29 = (s32[]{:T(128)}, f32[2,1024,2,128]{1,3,2,0:T(8,128)}, f32[2,1024,2,128]{1,3,2,0:T(8,128)}, bf16[2,1024,2,128]{1,3,2,0:T(8,128)(2,1)}, bf16[2,1024,2,...) while((s32[]{:T(128)}, f32[2,1024,2,128]{1,3,2,0:T(8,128)}, ...), condition=%wide.region_21.22_spmd.clone, body=%wide.region_19.21_spmd.sunk.clone | while | flops 2718432256 | bytes 92862128 | solution.py:289
  2869.4 122.6 %all-gather.21.cloned.1.call-done = bf16[8192,3,256]{2,0,1:T(8,128)(2,1)} async-done(((bf16[2048,3,256]{2,0,1:T(8,128)(2,1)}), bf16[8192,3,256]{2,0,1:T(8,128)(2,1)}) %all-gather.21.cloned.1.call-update) | async-done | bytes 12582928 | tf_op jit(solution)/shard_map/all_gather | solution.py:76
  3007.5 20.5 copy.414
  3028.1 247.2 %reduce-scatter.23.cloned.1.call-done = bf16[1024,3,512]{2,0,1:T(8,128)(2,1)} async-done(((bf16[8192,3,512]{2,0,1:T(8,128)(2,1)}), bf16[1024,3,512]{2,0,1:T(8,128)(2,1)}) %reduce-scatter.23.cloned.1.call-update) | async-done | bytes 3145744 | tf_op jit(solution)/shard_map/reduce_scatter | solution.py:93
  3292.9 39.5 %all-to-all-done.7 = bf16[1024,3,512]{2,1,0:T(4,128)(2,1)} async-done(((bf16[1024,3,512]{2,1,0:T(4,128)(2,1)}), bf16[1024,3,512]{2,1,0:T(4,128)(2,1)}, u32[]{:S(2)}, u32[]{:S(2)}) %all-to-all-start.7) | async-done | bytes 3145760 | tf_op jit(solution)/shard_map/all_to_all | solution.py:72
  3444.0 23.3 fusion.65
  3467.3 20.0 convolution_bitcast_fusion
  3508.5 124.2 %all-reduce.10.cloned.1.call-done = f32[2048,36]{0,1:T(8,128)} async-done(((f32[2048,36]{0,1:T(8,128)}), f32[2048,36]{0,1:T(8,128)}) %all-reduce.10.cloned.1.call-update) | async-done | bytes 294928 | tf_op jit(solution)/shard_map/psum | solution.py:325
  (429 shorter events, 743.2 us)
Async XLA Ops:
  7.2 1841.7 %copy-start = (bf16[1024,512]{1,0:T(8,128)(2,1)S(1)}, bf16[1024,512]{1,0:T(8,128)(2,1)}, u32[]{:S(2)}) copy-start(bf16[1024,512]{1,0:T(8,128)(2,1)} %param.33) | copy-start | bytes 3145732
  7.2 254.9 %all-gather.11.cloned.1.call-start = ((), (), s32[]{:S(2)}) async-start(), calls=%async_computation.16 | async-start | bytes 28311552 | tf_op jit(solution)/shard_map/all_gather | solution.py:64
  39.4 846.0 %reduce-scatter.9.cloned.1.call-start = ((), (), s32[]{:S(2)}) async-start(), calls=%async_computation.17 | async-start | bytes 15728640 | tf_op jit(solution)/shard_map/reduce_scatter | solution.py:84
  767.7 277.6 %all-gather.13.cloned.1.call-start = ((), (), s32[]{:S(2)}) async-start(), calls=%async_computation.18 | async-start | bytes 5242880 | tf_op jit(solution)/shard_map/all_gather | solution.py:76
  992.5 158.1 %reduce-scatter.11.cloned.1.call-start = ((), (), s32[]{:S(2)}) async-start(), calls=%async_computation.19 | async-start | bytes 9437184 | tf_op jit(solution)/shard_map/reduce_scatter | solution.py:93
  1155.9 16.1 all-to-all-start.1
  1160.2 105.4 %all-gather.15.cloned.1.call-start = ((), (), s32[]{:S(2)}) async-start(), calls=%async_computation.20 | async-start | bytes 9437184 | tf_op jit(solution)/shard_map/all_gather | solution.py:64
  1183.7 486.9 %reduce-scatter.13.cloned.1.call-start = ((), (), s32[]{:S(2)}) async-start(), calls=%async_computation.21 | async-start | bytes 20971520 | tf_op jit(solution)/shard_map/reduce_scatter | solution.py:84
  1519.5 329.4 %all-gather.17.cloned.1.call-start = ((), (), s32[]{:S(2)}) async-start(), calls=%async_computation.22 | async-start | bytes 20971520 | tf_op jit(solution)/shard_map/all_gather | solution.py:76
  1691.3 271.8 %reduce-scatter.15.cloned.1.call-start = ((), (), s32[]{:S(2)}) async-start(), calls=%async_computation.23 | async-start | bytes 9437184 | tf_op jit(solution)/shard_map/reduce_scatter | solution.py:93
  1972.5 16.1 all-to-all-start.3
  1976.7 159.0 %all-gather.23.cloned.1.call-start = ((), (), s32[]{:S(2)}) async-start(), calls=%async_computation.31 | async-start | bytes 9437184 | tf_op jit(solution)/shard_map/all_gather | solution.py:80
  2053.1 262.3 %reduce-scatter.17.cloned.1.call-start = ((), (), s32[]{:S(2)}) async-start(), calls=%async_computation.24 | async-start | bytes 20971520 | tf_op jit(solution)/shard_map/reduce_scatter | solution.py:84
  2163.2 319.8 %all-gather.19.cloned.1.call-start = ((), (), s32[]{:S(2)}) async-start(), calls=%async_computation.25 | async-start | bytes 20971520 | tf_op jit(solution)/shard_map/all_gather | solution.py:76
  2315.4 167.6 %copy-start.73 = (bf16[512,1024]{1,0:T(8,128)(2,1)S(1)}, bf16[512,1024]{1,0:T(8,128)(2,1)}, u32[]{:S(2)}) copy-start(bf16[512,1024]{1,0:T(8,128)(2,1)} %param.31) | copy-start | bytes 3145732
  2325.5 271.8 %reduce-scatter.19.cloned.1.call-start = ((), (), s32[]{:S(2)}) async-start(), calls=%async_computation.26 | async-start | bytes 9437184 | tf_op jit(solution)/shard_map/reduce_scatter | solution.py:93
  2601.9 15.3 all-to-all-start.5
  2605.5 137.1 %all-gather.25.cloned.1.call-start = ((), (), s32[]{:S(2)}) async-start(), calls=%async_computation.32 | async-start | bytes 9437184 | tf_op jit(solution)/shard_map/all_gather | solution.py:80
  2660.2 152.8 %reduce-scatter.21.cloned.1.call-start = ((), (), s32[]{:S(2)}) async-start(), calls=%async_computation.27 | async-start | bytes 5242880 | tf_op jit(solution)/shard_map/reduce_scatter | solution.py:84
  2762.0 230.0 %all-gather.21.cloned.1.call-start = ((), (), s32[]{:S(2)}) async-start(), calls=%async_computation.28 | async-start | bytes 15728640 | tf_op jit(solution)/shard_map/all_gather | solution.py:76
  2869.3 406.0 %reduce-scatter.23.cloned.1.call-start = ((), (), s32[]{:S(2)}) async-start(), calls=%async_computation.29 | async-start | bytes 28311552 | tf_op jit(solution)/shard_map/reduce_scatter | solution.py:93
  3028.0 258.9 %copy-start.48 = (f32[256,36]{0,1:T(8,128)S(1)}, f32[256,36]{0,1:T(8,128)}, u32[]{:S(2)}) copy-start(f32[256,36]{0,1:T(8,128)} %param.39) | copy-start | bytes 110596
  3028.0 258.9 %copy-start.52 = (f32[256,36]{0,1:T(8,128)S(1)}, f32[256,36]{0,1:T(8,128)}, u32[]{:S(2)}) copy-start(f32[256,36]{0,1:T(8,128)} %copy-done.51) | copy-start | bytes 110596
  3028.0 259.8 %copy-start.14 = (f32[256,2048]{1,0:T(8,128)S(1)}, f32[256,2048]{1,0:T(8,128)}, u32[]{:S(2)}) copy-start(f32[256,2048]{1,0:T(8,128)} %copy-done.13) | copy-start | bytes 6291460
  3028.1 259.7 %copy-start.50 = (f32[256,36]{0,1:T(8,128)S(1)}, f32[256,36]{0,1:T(8,128)}, u32[]{:S(2)}) copy-start(f32[256,36]{0,1:T(8,128)} %copy-done.49) | copy-start | bytes 110596
  3028.1 259.7 %copy-start.61 = (f32[2048]{0:T(1024)S(1)}, f32[2048]{0:T(1024)}, u32[]{:S(2)}) copy-start(f32[2048]{0:T(1024)} %param.35) | copy-start | bytes 24580
  3028.1 259.7 %copy-start.71 = (f32[256]{0:T(256)S(1)}, f32[256]{0:T(256)}, u32[]{:S(2)}) copy-start(f32[256]{0:T(256)} %copy-done.70) | copy-start | bytes 3076
  3028.1 262.2 %copy-start.67 = (f32[1024]{0:T(1024)S(1)}, f32[1024]{0:T(1024)}, u32[]{:S(2)}) copy-start(f32[1024]{0:T(1024)} %get-tuple-element.404) | copy-start | bytes 12292
  3028.1 262.4 %copy-start.58 = (f32[4,512]{1,0:T(4,128)S(1)}, f32[4,512]{1,0:T(4,128)}, u32[]{:S(2)}) copy-start(f32[4,512]{1,0:T(4,128)} %get-tuple-element.358) | copy-start | bytes 24580
  3282.0 50.4 %all-to-all-start.7 = ((bf16[1024,3,512]{2,1,0:T(4,128)(2,1)}), bf16[1024,3,512]{2,1,0:T(4,128)(2,1)}, u32[]{:S(2)}, u32[]{:S(2)}) async-start(bf16[1024,3,512]{2,1,0:T(4,128)(2,1)} %copy.415), calls=%async_computation.15 | async-start | bytes 8388608 | tf_op jit(solution)/shard_map/all_to_all | solution.py:72
  3286.9 219.1 %all-reduce.12.cloned.1.call-start = ((), (), s32[]{:S(2)}) async-start(), calls=%async_computation.33 | async-start | bytes 352256 | tf_op jit(solution)/shard_map/psum | solution.py:325
  3374.4 258.3 %all-reduce.10.cloned.1.call-start = ((), (), s32[]{:S(2)}) async-start(), calls=%async_computation.30 | async-start | bytes 655360 | tf_op jit(solution)/shard_map/psum | solution.py:325
  (73 other events, 2121.8 us)
Sparse Core Ops, SparseCore 0:
  39.5 222.5 all-gather.10
  767.8 117.4 reduce-scatter.8
  992.6 52.6 all-gather.12
  1060.9 89.5 reduce-scatter.10
  1183.8 81.6 all-gather.14
  1519.6 150.8 reduce-scatter.12
  1691.4 157.3 all-gather.16
  1873.4 89.5 reduce-scatter.14
  2053.2 82.4 all-gather.22
  2163.3 152.0 reduce-scatter.16
  2325.6 157.3 all-gather.18
  2507.6 89.5 reduce-scatter.18
  2660.3 82.3 all-gather.24
  2762.1 50.8 reduce-scatter.20
  2869.4 122.4 all-gather.20
  3028.1 247.1 reduce-scatter.22
  3374.5 125.4 all-reduce.11
  3505.8 126.8 all-reduce.9
where the time goes:
time: 3670 us; the launch traced here: 3650 us
  waiting for transfers between devices  2130 us (58%)
  blocking collectives  505 us (14%)
  local copies, waits for them, and re-layouts  499 us (14%)
  matrix products  276 us (8%)
  other arithmetic  208 us (6%)
    reduce_scatter x4, waiting for transfers between devices, sum_col(): lax.psum_scatter(term_fn(jnp.int32(0), shard_rows * lax.axis_size('col'))...  515 us
    all_to_all x4, blocking collectives, split_features(): lax.all_to_all(values, 'row', split_axis=2, concat_axis=0, tiled=True)  505 us
    all_gather x4, waiting for transfers between devices, tokens_row(): return lax.all_gather(values, 'row', axis=0, tiled=True)  490 us
    reduce_scatter x4, waiting for transfers between devices, sum_row(): lax.psum_scatter(term_fn(jnp.int32(0), shard_rows * lax.axis_size('row'))...  467 us
    all_gather x2, waiting for transfers between devices, tokens_col(): return lax.all_gather(values, 'col', axis=0, tiled=True)  304 us
    all_gather x2, waiting for transfers between devices, blocks_col(): return lax.all_gather(values, 'col', axis=1, tiled=True)  165 us
    unnamed x189, local copies, waits for them, and re-layouts  136 us
    psum x2, waiting for transfers between devices, on_device(): lax.psum((gain_early + gain_late, bias_early + bias_late, mix_gain_part,...  124 us
  transfers between devices with their start and end apart: 22, of which 21 were waited for; matrix products, arithmetic and copies ran while one was open for 4% of the time, Pallas kernels for 0%

commit v1 on v0

v1 whole, which is shorter than its diff:
```python
import functools

import jax
import jax.numpy as jnp
from jax import lax
from jax.experimental import pallas as pl
from jax.experimental.pallas import tpu as pltpu
from jax.sharding import Mesh, PartitionSpec as P

HD = 128
ROT = 32
LEN = 1024
EPS_LAYER = 1e-05
EPS_RMS = 1e-06
BF = jnp.bfloat16
F32 = jnp.float32
FINEST = lax.Precision.HIGHEST
LOG2E = 1.4426950408889634
SCALE = HD**-0.5
VMEM_CAP = 56 * 1024 * 1024
ALL = ("row", "zh", "zl", "core")

NN = (((1,), (0,)), ((), ()))
NT = (((1,), (1,)), ((), ()))
TN = (((0,), (0,)), ((), ()))


def dot(a, b, dims, precision=None):
    return lax.dot_general(a, b, dims, precision=precision, preferred_element_type=F32)


def params():
    return pltpu.CompilerParams(vmem_limit_bytes=VMEM_CAP)


def cost(flops, arrays, extra=0):
    moved = sum(int(a.size) * a.dtype.itemsize for a in arrays)
    return pl.CostEstimate(flops=int(flops), bytes_accessed=int(moved), transcendentals=int(extra))


def sds(shape, dtype):
    return jax.ShapeDtypeStruct(shape, dtype)


def mix_stream(stack_ref, coeffs, s, rows):
    total = None
    for j in range(8):
        term = coeffs[:, 8 * s + j : 8 * s + j + 1] * stack_ref[j, rows, :].astype(F32)
        total = term if total is None else total + term
    return total


def centre(values):
    centred = values - jnp.mean(values, axis=-1, keepdims=True)
    spread = jnp.mean(centred * centred, axis=-1, keepdims=True)
    return centred, lax.rsqrt(spread + EPS_LAYER)


def front_kernel(stack_ref, mix_ref, gain_ref, bias_ref, q_ref, k_ref, v_ref, res_ref):
    chunk = 16

    def step(i, carry):
        rows = pl.ds(pl.multiple_of(i * chunk, chunk), chunk)
        coeffs = mix_ref[rows, :]
        for s, out_ref in enumerate((q_ref, k_ref, v_ref)):
            centred, rstd = centre(mix_stream(stack_ref, coeffs, s, rows))
            out_ref[rows, :] = (
                centred * rstd * gain_ref[s : s + 1, :] + bias_ref[s : s + 1, :]
            ).astype(BF)
        res_ref[rows, :] = mix_stream(stack_ref, coeffs, 3, rows)
        return carry

    lax.fori_loop(0, stack_ref.shape[1] // chunk, step, 0)


def front(stack, mix, gain, bias):
    n_in, tokens, width = stack.shape
    tile = 64
    row_block = lambda i: (i, 0)
    outs = [sds((tokens, width), BF)] * 3 + [sds((tokens, width), F32)]
    return pl.pallas_call(
        front_kernel,
        grid=(tokens // tile,),
        in_specs=[
            pl.BlockSpec((n_in, tile, width), lambda i: (0, i, 0)),
            pl.BlockSpec((tile, mix.shape[1]), row_block),
            pl.BlockSpec(gain.shape, lambda i: (0, 0)),
            pl.BlockSpec(bias.shape, lambda i: (0, 0)),
        ],
        out_specs=[pl.BlockSpec((tile, width), row_block)] * 4,
        out_shape=outs,
        compiler_params=params(),
        cost_estimate=cost(70 * tokens * width, [stack, *outs]),
        name="front",
    )(stack, mix, gain, bias)


def front_back_kernel(pieces, *refs):
    grads = [refs[s * pieces : (s + 1) * pieces] for s in range(3)]
    hid_ref, stack_ref, mix_ref, gain_ref = refs[3 * pieces : 3 * pieces + 4]
    stack_out, coeff_out, gain_out, bias_out, held = refs[3 * pieces + 4 :]
    chunk = 16
    width = hid_ref.shape[1]

    @pl.when(pl.program_id(0) == 0)
    def _():
        gain_out[...] = jnp.zeros_like(gain_out)
        bias_out[...] = jnp.zeros_like(bias_out)

    def step(i, carry):
        rows = pl.ds(pl.multiple_of(i * chunk, chunk), chunk)
        coeffs = mix_ref[rows, :]
        for s in range(3):
            centred, rstd = centre(mix_stream(stack_ref, coeffs, s, rows))
            hat = centred * rstd
            grad = grads[s][0][rows, :].astype(F32)
            for piece in grads[s][1:]:
                grad = grad + piece[rows, :].astype(F32)
            grad = grad.astype(BF).astype(F32)
            gain_out[8 * s : 8 * s + 8, :] += jnp.sum(
                (grad * hat).reshape(chunk // 8, 8, width), axis=0
            )
            bias_out[8 * s : 8 * s + 8, :] += jnp.sum(grad.reshape(chunk // 8, 8, width), axis=0)
            scaled = grad * gain_ref[s : s + 1, :]
            held[s] = rstd * (
                scaled
                - jnp.mean(scaled, axis=-1, keepdims=True)
                - hat * jnp.mean(scaled * hat, axis=-1, keepdims=True)
            )
        held[3] = hid_ref[rows, :]
        lanes = lax.broadcasted_iota(jnp.int32, (chunk, mix_ref.shape[1]), 1)
        gathered = jnp.zeros((chunk, mix_ref.shape[1]), F32)
        for j in range(8):
            given = stack_ref[j, rows, :].astype(F32)
            total = None
            for s in range(4):
                grad = held[s]
                term = coeffs[:, 8 * s + j : 8 * s + j + 1] * grad
                total = term if total is None else total + term
                inner = jnp.sum(grad * given, axis=-1, keepdims=True)
                gathered = jnp.where(lanes == 8 * s + j, inner, gathered)
            stack_out[j, rows, :] = total
        coeff_out[rows, :] = gathered
        return carry

    lax.fori_loop(0, hid_ref.shape[0] // chunk, step, 0)


def front_back(grad_pieces, grad_hidden, stack, mix, gain):
    n_in, tokens, width = stack.shape
    tile = 32
    pieces = len(grad_pieces[0])
    row_block = lambda i: (i, 0)
    fixed = lambda i: (0, 0)
    outs = [
        sds(stack.shape, F32),
        sds(mix.shape, F32),
        sds((24, width), F32),
        sds((24, width), F32),
    ]
    flat = [piece for group in grad_pieces for piece in group]
    return pl.pallas_call(
        functools.partial(front_back_kernel, pieces),
        grid=(tokens // tile,),
        in_specs=[pl.BlockSpec((tile, width), row_block)] * (3 * pieces + 1)
        + [
            pl.BlockSpec((n_in, tile, width), lambda i: (0, i, 0)),
            pl.BlockSpec((tile, mix.shape[1]), row_block),
            pl.BlockSpec(gain.shape, fixed),
        ],
        out_specs=[
            pl.BlockSpec((n_in, tile, width), lambda i: (0, i, 0)),
            pl.BlockSpec((tile, mix.shape[1]), row_block),
            pl.BlockSpec((24, width), fixed),
            pl.BlockSpec((24, width), fixed),
        ],
        out_shape=outs,
        scratch_shapes=[pltpu.VMEM((4, 16, width), F32)],
        compiler_params=params(),
        cost_estimate=cost(250 * tokens * width, [stack, grad_hidden, *flat, *outs]),
        name="front_back",
    )(*flat, grad_hidden, stack, mix, gain)


def turn(values, cos_table, sine_table):
    lanes = lax.broadcasted_iota(jnp.int32, values.shape, 1)
    half = ROT // 2
    swapped = jnp.where(
        lanes < half, pltpu.roll(values, HD - half, 1), pltpu.roll(values, half, 1)
    )
    return values * cos_table + swapped * sine_table


def proj_kernel(blocks, rotary, *refs):
    x_refs = refs[:blocks]
    if rotary:
        weight_ref, bias_ref, cos_ref, sine_ref, out_ref = refs[blocks:]
    else:
        weight_ref, bias_ref, out_ref = refs[blocks:]
    rows = x_refs[0].shape[0]
    for b, x_ref in enumerate(x_refs):
        here = slice(b * rows, (b + 1) * rows)
        total = dot(x_ref[...], weight_ref[...], NN) + bias_ref[...]
        if not rotary:
            out_ref[here, :] = total.astype(BF)
            continue
        for h in range(total.shape[1] // HD):
            heads = slice(h * HD, (h + 1) * HD)
            out_ref[here, heads] = turn(
                total[:, heads], cos_ref[here, :], sine_ref[here, :]
            ).astype(BF)


def proj(x_blocks, weight, part, bias, tables=None):
    blocks = len(x_blocks)
    rows, width = x_blocks[0].shape
    cols = bias.shape[1]
    out = sds((blocks * rows, cols), BF)
    whole = lambda a: pl.BlockSpec(a.shape, lambda i: (0, 0))
    rest = [bias] + list(tables or ())
    return pl.pallas_call(
        functools.partial(proj_kernel, blocks, tables is not None),
        grid=(1,),
        in_specs=[whole(x) for x in x_blocks]
        + [pl.BlockSpec((width, cols), lambda i: (0, part))]
        + [whole(a) for a in rest],
        out_specs=whole(out),
        out_shape=out,
        compiler_params=params(),
        cost_estimate=cost(2 * blocks * rows * width * cols, [*x_blocks, bias, out]),
        name="proj",
    )(*x_blocks, weight, *rest)


def unproj_kernel(halves, *refs):
    a_refs, weight_refs, outs = refs[:halves], refs[halves : 2 * halves], refs[2 * halves :]
    rows = outs[0].shape[0]
    for b, out_ref in enumerate(outs):
        total = None
        for a_ref, weight_ref in zip(a_refs, weight_refs):
            term = dot(a_ref[b * rows : (b + 1) * rows, :], weight_ref[...], NT)
            total = term if total is None else total + term
        out_ref[...] = total.astype(BF)


def unproj(parts, weights, part, blocks):
    halves = len(parts)
    tokens, cols = parts[0].shape
    width = weights[0].shape[0]
    tile = min(width, 512)
    outs = [sds((tokens // blocks, width), BF)] * blocks
    return pl.pallas_call(
        functools.partial(unproj_kernel, halves),
        grid=(width // tile,),
        in_specs=[pl.BlockSpec((tokens, cols), lambda i: (0, 0))] * halves
        + [pl.BlockSpec((tile, cols), lambda i: (i, part))] * halves,
        out_specs=[pl.BlockSpec((tokens // blocks, tile), lambda i: (0, i))] * blocks,
        out_shape=outs,
        compiler_params=params(),
        cost_estimate=cost(2 * halves * tokens * cols * width, [*parts, *outs]),
        name="unproj",
    )(*parts, *weights)


def masked_scores(scalars, keys, query, block, blocks):
    rows = query.shape[0]
    raw = dot(keys, query, NT)
    lanes = lax.broadcasted_iota(jnp.int32, (1, rows), 1)
    limit = jnp.maximum(lanes + scalars[block], scalars[blocks] - 1)
    places = lax.broadcasted_iota(jnp.int32, (rows, rows), 0)
    kept = []
    for b in range(blocks):
        allowed = places <= limit - scalars[b]
        kept.append(jnp.where(allowed, raw[b * rows : (b + 1) * rows, :], -1e30))
    return jnp.concatenate(kept, axis=0)


def attend_kernel(blocks, scalars, q_ref, k_ref, v_ref, out_ref, log_ref):
    rows = q_ref.shape[0] // blocks
    factor = SCALE * LOG2E
    for b in range(blocks):
        here = slice(b * rows, (b + 1) * rows)
        scores = masked_scores(scalars, k_ref[...], q_ref[here, :], b, blocks)
        top = jnp.max(scores, axis=0, keepdims=True)
        probs = jnp.exp2((scores - top) * factor)
        total = jnp.sum(probs, axis=0, keepdims=True)
        mixed = dot(v_ref[...], probs.astype(BF), TN) / total
        out_ref[here, :] = mixed.T.astype(BF)
        log_ref[0, :, here] = top * factor + jnp.log2(total)


def attend(scalars, query, key, value, blocks):
    tokens, cols = query.shape
    heads = cols // HD
    head_block = pl.BlockSpec((tokens, HD), lambda h: (0, h))
    outs = [sds((tokens, cols), BF), sds((heads, 1, tokens), F32)]
    return pl.pallas_call(
        functools.partial(attend_kernel, blocks),
        grid=(heads,),
        in_specs=[pl.BlockSpec(memory_space=pltpu.SMEM)] + [head_block] * 3,
        out_specs=[head_block, pl.BlockSpec((1, 1, tokens), lambda h: (h, 0, 0))],
        out_shape=outs,
        compiler_params=params(),
        cost_estimate=cost(8 * heads * tokens * tokens * HD, [query, key, value, *outs]),
        name="attend",
    )(scalars, query, key, value)


def attend_back_kernel(
    blocks, scalars, q_ref, k_ref, v_ref, g_ref, log_ref, cos_ref, sine_ref,
    gq_ref, gk_ref, gv_ref, sums_ref, key_acc, value_acc,
):
    rows = q_ref.shape[0] // blocks
    factor = SCALE * LOG2E
    sums = []
    query_sum = jnp.zeros((1, HD), F32)
    for b in range(blocks):
        here = slice(b * rows, (b + 1) * rows)
        query, grad = q_ref[here, :], g_ref[here, :]
        scores = masked_scores(scalars, k_ref[...], query, b, blocks)
        probs = jnp.exp2(scores * factor - log_ref[0, :, here])
        grad_probs = dot(v_ref[...], grad, NT)
        inner = jnp.sum(probs * grad_probs, axis=0, keepdims=True)
        grad_scores = (probs * (grad_probs - inner)).astype(BF)
        key_term = dot(grad_scores, query, NN)
        value_term = dot(probs.astype(BF), grad, NN)
        if b == 0:
            key_acc[...] = key_term
            value_acc[...] = value_term
        else:
            key_acc[...] += key_term
            value_acc[...] += value_term
        grad_query = dot(k_ref[...], grad_scores, TN).T * SCALE
        low = turn(grad_query, cos_ref[here, :], -sine_ref[here, :]).astype(BF)
        gq_ref[here, :] = low
        query_sum = query_sum + jnp.sum(low.astype(F32), axis=0, keepdims=True)
    low_key = turn(key_acc[...] * SCALE, cos_ref[...], -sine_ref[...]).astype(BF)
    gk_ref[...] = low_key
    low_value = value_acc[...].astype(BF)
    gv_ref[...] = low_value
    sums_ref[0, 0:1, :] = query_sum
    sums_ref[0, 1:2, :] = jnp.sum(low_key.astype(F32), axis=0, keepdims=True)
    sums_ref[0, 2:3, :] = jnp.sum(low_value.astype(F32), axis=0, keepdims=True)


def attend_back(scalars, query, key, value, grad, log_total, tables, blocks):
    tokens, cols = query.shape
    heads = cols // HD
    head_block = pl.BlockSpec((tokens, HD), lambda h: (0, h))
    fixed = pl.BlockSpec((tokens, HD), lambda h: (0, 0))
    outs = [sds((tokens, cols), BF)] * 3 + [sds((heads, 8, HD), F32)]
    return pl.pallas_call(
        functools.partial(attend_back_kernel, blocks),
        grid=(heads,),
        in_specs=[pl.BlockSpec(memory_space=pltpu.SMEM)]
        + [head_block] * 4
        + [pl.BlockSpec((1, 1, tokens), lambda h: (h, 0, 0)), fixed, fixed],
        out_specs=[head_block] * 3 + [pl.BlockSpec((1, 8, HD), lambda h: (h, 0, 0))],
        out_shape=outs,
        scratch_shapes=[pltpu.VMEM((tokens, HD), F32)] * 2,
        compiler_params=params(),
        cost_estimate=cost(16 * heads * tokens * tokens * HD, [query, key, value, grad, *outs]),
        name="attend_back",
    )(scalars, query, key, value, grad, log_total, *tables)


def total_of(refs, rows=slice(None)):
    total = refs[0][rows, :].astype(F32)
    for ref in refs[1:]:
        total = total + ref[rows, :].astype(F32)
    return total


def middle_kernel(pieces, *refs):
    parts = refs[:pieces]
    res_ref, out_bias_ref, gain_ref, bias_ref, hid_ref, norm_ref = refs[pieces:]
    attn = (total_of(parts) + out_bias_ref[...]).astype(BF)
    hidden = res_ref[...] + attn.astype(F32)
    hid_ref[...] = hidden
    centred, rstd = centre(hidden)
    norm_ref[...] = (centred * rstd * gain_ref[3:4, :] + bias_ref[3:4, :]).astype(BF)


def middle(parts, residual, out_bias, gain, bias):
    tokens, width = residual.shape
    tile = 64
    block = pl.BlockSpec((tile, width), lambda i: (i, 0))
    whole = lambda a: pl.BlockSpec(a.shape, lambda i: (0, 0))
    outs = [sds((tokens, width), F32), sds((tokens, width), BF)]
    return pl.pallas_call(
        functools.partial(middle_kernel, len(parts)),
        grid=(tokens // tile,),
        in_specs=[block] * (len(parts) + 1) + [whole(out_bias), whole(gain), whole(bias)],
        out_specs=[block] * 2,
        out_shape=outs,
        compiler_params=params(),
        cost_estimate=cost(20 * tokens * width, [*parts, residual, *outs]),
        name="middle",
    )(*parts, residual, out_bias, gain, bias)


def middle_back_kernel(pieces, *refs):
    parts = refs[:pieces]
    hid_ref, layer_ref, gain_ref = refs[pieces : pieces + 3]
    grad_ref, low_ref, sums_ref = refs[pieces + 3 :]
    grad = total_of(parts).astype(BF).astype(F32)
    centred, rstd = centre(hid_ref[...])
    hat = centred * rstd
    scaled = grad * gain_ref[3:4, :]
    grad_hidden = layer_ref[...] + rstd * (
        scaled
        - jnp.mean(scaled, axis=-1, keepdims=True)
        - hat * jnp.mean(scaled * hat, axis=-1, keepdims=True)
    )
    grad_ref[...] = grad_hidden
    low = grad_hidden.astype(BF)
    low_ref[...] = low

    @pl.when(pl.program_id(0) == 0)
    def _():
        sums_ref[...] = jnp.zeros_like(sums_ref)

    sums_ref[0:1, :] += jnp.sum(grad * hat, axis=0, keepdims=True)
    sums_ref[1:2, :] += jnp.sum(grad, axis=0, keepdims=True)
    sums_ref[2:3, :] += jnp.sum(low.astype(F32), axis=0, keepdims=True)


def middle_back(parts, hidden, grad_layer, gain):
    tokens, width = hidden.shape
    tile = 64
    block = pl.BlockSpec((tile, width), lambda i: (i, 0))
    outs = [sds((tokens, width), F32), sds((tokens, width), BF), sds((8, width), F32)]
    return pl.pallas_call(
        functools.partial(middle_back_kernel, len(parts)),
        grid=(tokens // tile,),
        in_specs=[block] * (len(parts) + 2) + [pl.BlockSpec(gain.shape, lambda i: (0, 0))],
        out_specs=[block] * 2 + [pl.BlockSpec((8, width), lambda i: (0, 0))],
        out_shape=outs,
        compiler_params=params(),
        cost_estimate=cost(30 * tokens * width, [*parts, hidden, grad_layer, *outs]),
        name="middle_back",
    )(*parts, hidden, grad_layer, gain)


def gelu_pair(values):
    tail = 0.5 * (1.0 + lax.erf(values * (0.5**0.5)))
    slope = tail + values * jnp.exp2(values * values * (-0.5 * LOG2E)) * 0.3989422804014327
    return values * tail, slope


def feed_kernel(blocks, back, *refs):
    x_refs = refs[:blocks]
    if back:
        first_ref, second_ref, slope_ref = refs[blocks : blocks + 3]
        act_ref, sums_ref = refs[blocks + 3 : blocks + 5]
    else:
        first_ref, second_ref, bias_ref = refs[blocks : blocks + 3]
        act_ref, slope_ref = refs[blocks + 3 : blocks + 5]
    outs = refs[blocks + 5 : 2 * blocks + 5]
    acc = refs[2 * blocks + 5]
    rows = x_refs[0].shape[0]
    step, last = pl.program_id(0), pl.num_programs(0) - 1
    total = None
    for b, x_ref in enumerate(x_refs):
        here = slice(b * rows, (b + 1) * rows)
        up = dot(x_ref[...], first_ref[...], NN)
        if back:
            low = (up * slope_ref[here, :].astype(F32)).astype(BF)
            part = jnp.sum(low.astype(F32), axis=0, keepdims=True)
            total = part if total is None else total + part
        else:
            act, slope = gelu_pair(up + bias_ref[...])
            low = act.astype(BF)
            slope_ref[here, :] = slope.astype(BF)
        act_ref[here, :] = low
        term = dot(low, second_ref[...], NT)

        @pl.when(step == 0)
        def _():
            acc[here, :] = term

        @pl.when(step > 0)
        def _():
            acc[here, :] += term

    if back:
        sums_ref[...] = total

    @pl.when(step == last)
    def _():
        for b, out_ref in enumerate(outs):
            out_ref[...] = acc[b * rows : (b + 1) * rows, :].astype(BF)


def feed(x_blocks, first, second, extra, back):
    blocks = len(x_blocks)
    rows, width = x_blocks[0].shape
    tokens = blocks * rows
    hidden = first.shape[1]
    tile = 256
    whole = pl.BlockSpec((rows, width), lambda i: (0, 0))
    weight = pl.BlockSpec((width, tile), lambda i: (0, i))
    line = pl.BlockSpec((1, tile), lambda i: (0, i))
    column = pl.BlockSpec((tokens, tile), lambda i: (0, i))
    outs = [
        sds((tokens, hidden), BF),
        sds((1, hidden), F32) if back else sds((tokens, hidden), BF),
    ] + [sds((rows, width), BF)] * blocks
    return pl.pallas_call(
        functools.partial(feed_kernel, blocks, back),
        grid=(hidden // tile,),
        in_specs=[whole] * blocks + [weight, weight, column if back else line],
        out_specs=[column, line if back else column] + [whole] * blocks,
        out_shape=outs,
        scratch_shapes=[pltpu.VMEM((tokens, width), F32)],
        compiler_params=params(),
        cost_estimate=cost(4 * tokens * width * hidden, [*x_blocks, first, second, extra, *outs]),
        name="feed_back" if back else "feed",
    )(*x_blocks, first, second, extra)


def mixing_kernel(pieces, *refs):
    parts = refs[:pieces]
    hid_ref, down_bias_ref, gain_ref, in_ref, out_w_ref, og_ref, cg_ref = refs[
        pieces : pieces + 7
    ]
    layer_ref, coeff_ref, grad_ref, low_ref, sums_ref, in_grad_ref, out_grad_ref = refs[
        pieces + 7 :
    ]
    down = (total_of(parts) + down_bias_ref[...]).astype(BF)
    layer = hid_ref[...] + down.astype(F32)
    layer_ref[...] = layer
    rms = lax.rsqrt(jnp.mean(layer * layer, axis=-1, keepdims=True) + EPS_RMS)
    unit = layer * rms
    gain = gain_ref[...]
    scaled = unit * gain
    act, slope = gelu_pair(dot(scaled, in_ref[...], NN, FINEST))
    coeff_ref[...] = dot(act, out_w_ref[...], NN, FINEST)
    coeff_grad = cg_ref[...]
    grad_pre = dot(coeff_grad, out_w_ref[...], NT, FINEST) * slope
    grad_scaled = dot(grad_pre, in_ref[...], NT, FINEST)
    grad_unit = grad_scaled * gain
    grad_layer = (
        rms * (grad_unit - unit * jnp.mean(grad_unit * unit, axis=-1, keepdims=True))
        + og_ref[...].astype(F32)
    )
    grad_ref[...] = grad_layer
    low = grad_layer.astype(BF)
    low_ref[...] = low

    @pl.when(pl.program_id(0) == 0)
    def _():
        sums_ref[...] = jnp.zeros_like(sums_ref)
        in_grad_ref[...] = jnp.zeros_like(in_grad_ref)
        out_grad_ref[...] = jnp.zeros_like(out_grad_ref)

    sums_ref[0:1, :] += jnp.sum(low.astype(F32), axis=0, keepdims=True)
    sums_ref[1:2, :] += jnp.sum(grad_scaled * unit, axis=0, keepdims=True)
    in_grad_ref[...] += dot(grad_pre, scaled, TN, FINEST)
    out_grad_ref[...] += dot(act, coeff_grad, TN, FINEST)


def mixing(parts, hidden, down_bias, gain, mix_in, mix_out, out_grad, coeff_grad):
    tokens, width = hidden.shape
    tile = 128
    block = pl.BlockSpec((tile, width), lambda i: (i, 0))
    whole = lambda a: pl.BlockSpec(a.shape, lambda i: (0, 0))
    narrow = pl.BlockSpec((tile, coeff_grad.shape[1]), lambda i: (i, 0))
    outs = [
        sds((tokens, width), F32),
        sds(coeff_grad.shape, F32),
        sds((tokens, width), F32),
        sds((tokens, width), BF),
        sds((8, width), F32),
        sds((mix_in.shape[1], width), F32),
        sds(mix_out.shape, F32),
    ]
    return pl.pallas_call(
        functools.partial(mixing_kernel, len(parts)),
        grid=(tokens // tile,),
        in_specs=[block] * (len(parts) + 1)
        + [whole(a) for a in (down_bias, gain, mix_in, mix_out)]
        + [block, narrow],
        out_specs=[block, narrow, block, block] + [whole(a) for a in outs[4:]],
        out_shape=outs,
        compiler_params=params(),
        cost_estimate=cost(3000 * tokens * width, [*parts, hidden, out_grad, *outs]),
        name="mixing",
    )(*parts, hidden, down_bias, gain, mix_in, mix_out, out_grad, coeff_grad)


def swap(values, axis, bits):
    size = lax.axis_size(axis)
    return lax.ppermute(values, axis, [(i, i ^ bits) for i in range(size)])


def gather_tokens(values):
    blocks = []
    for k in range(lax.axis_size("zl")):
        held = swap(values, "zl", k) if k else values
        blocks += [held, swap(held, "core", 1)]
    return blocks


def scatter_tokens(blocks):
    terms = [blocks[0], swap(blocks[1], "core", 1)]
    for k in range(1, lax.axis_size("zl")):
        other = swap(blocks[2 * k + 1], "core", 1)
        chip_sum = (blocks[2 * k].astype(F32) + other.astype(F32)).astype(BF)
        terms.append(swap(chip_sum, "zl", k))
    return terms


def halves_of(values):
    return [values] + [swap(values, "zh", h) for h in range(1, lax.axis_size("zh"))]


def sum_everywhere(values):
    for axis in ("core", "zl", "row", "zh"):
        bit = 1
        while bit < lax.axis_size(axis):
            values = values + swap(values, axis, bit)
            bit *= 2
    return values


def sum_groups(values, axes):
    for axis in axes:
        bit = 1
        while bit < lax.axis_size(axis):
            values = values + swap(values, axis, bit)
            bit *= 2
    return values


def gather_weight(values):
    return lax.all_gather(values, "row", axis=0, tiled=True)


def scatter_weight(grad, halves):
    mine = lax.psum_scatter(grad, "row", scatter_dimension=0, tiled=True)
    cols = grad.shape[1] // halves
    total = mine[:, :cols].astype(F32)
    for h in range(1, halves):
        total = total + swap(mine[:, h * cols : (h + 1) * cols], "zh", h).astype(F32)
    return total


def on_device(
    layer_stack, mix_coeffs, prefix, ln_gain, ln_bias, qkv_weight, qkv_bias, out_weight,
    out_bias, up_weight, up_bias, down_weight, down_bias, mix_gain, mix_in, mix_out, out_grad,
    coeff_grad,
):
    tokens, width = layer_stack.shape[1:]
    halves = lax.axis_size("zh")
    group = lax.axis_size("zl") * 2
    cols = qkv_bias.shape[1]
    feats = qkv_weight.shape[1]
    place = lax.axis_index("zl") * 2 + lax.axis_index("core")

    attn_local = jnp.concatenate(
        [qkv_weight[s] for s in range(3)] + [out_weight.T], axis=1
    )
    attn_halves = halves_of(attn_local)
    up_local = jnp.concatenate(halves_of(up_weight), axis=1)
    down_local = jnp.concatenate(halves_of(down_weight.T), axis=1)
    attn_full = [gather_weight(w) for w in attn_halves]
    up_full = gather_weight(up_local)
    down_full = gather_weight(down_local)
    qkv_biases = halves_of(qkv_bias)
    up_bias_full = jnp.concatenate(halves_of(up_bias.reshape(1, -1)), axis=1)

    bases = (place ^ jnp.arange(group, dtype=jnp.int32)) * tokens
    prefix_here = lax.dynamic_slice_in_dim(prefix, lax.axis_index("zh"), 1, 0)
    scalars = jnp.concatenate([bases, prefix_here])
    positions = (bases[:, None] + jnp.arange(tokens, dtype=jnp.int32)[None, :]).reshape(-1)
    inv_freq = 10000.0 ** (-(jnp.arange(ROT // 2, dtype=F32) * 2.0) / ROT)
    angles = positions.astype(F32)[:, None] * inv_freq[None, :]
    cos_half, sine_half = jnp.cos(angles), jnp.sin(angles)
    rest = jnp.zeros((positions.shape[0], HD - ROT), F32)
    tables = (
        jnp.concatenate([cos_half, cos_half, rest + 1.0], axis=1),
        jnp.concatenate([-sine_half, sine_half, rest], axis=1),
    )

    mix_flat = mix_coeffs.reshape(tokens, -1)
    *normed, residual = front(layer_stack, mix_flat, ln_gain, ln_bias)
    normed_all = [gather_tokens(n) for n in normed]
    q, k, v, head, log_total = [], [], [], [], []
    for h in range(halves):
        bias = [qkv_biases[h][s : s + 1] for s in range(3)]
        q.append(proj(normed_all[0], attn_full[h], 0, bias[0], tables))
        k.append(proj(normed_all[1], attn_full[h], 1, bias[1], tables))
        v.append(proj(normed_all[2], attn_full[h], 2, bias[2]))
        out, log = attend(scalars, q[h], k[h], v[h], group)
        head.append(out)
        log_total.append(log)
    attn_terms = scatter_tokens(unproj(head, attn_full, 3, group))
    hidden, normed2 = middle(attn_terms, residual, out_bias.reshape(1, -1), ln_gain, ln_bias)
    normed2_all = gather_tokens(normed2)
    act, slope, *down_parts = feed(normed2_all, up_full, down_full, up_bias_full, False)
    down_terms = scatter_tokens(down_parts)
    layer_out, coeff_out, grad_layer, grad_down, mix_sums, mix_in_part, mix_out_part = mixing(
        down_terms, hidden, down_bias.reshape(1, -1), mix_gain.reshape(1, -1), mix_in, mix_out,
        out_grad, coeff_grad,
    )

    grad_down_all = gather_tokens(grad_down)
    grad_up, up_bias_part, *norm2_parts = feed(grad_down_all, down_full, up_full, slope, True)
    down_grad = scatter_weight(
        dot(jnp.concatenate(grad_down_all, axis=0), act, TN).astype(BF), halves
    ).T
    norm2_terms = scatter_tokens(norm2_parts)
    up_grad = scatter_weight(
        dot(jnp.concatenate(normed2_all, axis=0), grad_up, TN).astype(BF), halves
    )
    grad_hidden, grad_attn, mid_sums = middle_back(norm2_terms, hidden, grad_layer, ln_gain)
    grad_attn_all = gather_tokens(grad_attn)
    no_bias = jnp.zeros((1, cols), F32)
    grads = [[], [], []]
    bias_sums = []
    for h in range(halves):
        grad_heads = proj(grad_attn_all, attn_full[h], 3, no_bias)
        *parts, sums = attend_back(
            scalars, q[h], k[h], v[h], grad_heads, log_total[h], tables, group
        )
        for s in range(3):
            grads[s].append(parts[s])
        bias_sums.append(sums[:, :3].transpose(1, 0, 2).reshape(3, cols))
    norm_terms = [scatter_tokens(unproj(grads[s], attn_full, s, group)) for s in range(3)]
    grad_attn_cat = jnp.concatenate(grad_attn_all, axis=0)
    wide = [
        dot(jnp.concatenate(normed_all[s], axis=0), jnp.concatenate(grads[s], axis=1), TN)
        for s in range(3)
    ] + [dot(grad_attn_cat, jnp.concatenate(head, axis=1), TN)]
    attn_grad = scatter_weight(
        jnp.concatenate(
            [w[:, h * cols : (h + 1) * cols] for h in range(halves) for w in wide], axis=1
        ).astype(BF),
        halves,
    )
    qkv_grad = attn_grad[:, : 3 * cols].reshape(feats, 3, cols).transpose(1, 0, 2)
    out_w_grad = attn_grad[:, 3 * cols :].T
    stack_grad, coeffs_grad, gain_part, bias_part = front_back(
        norm_terms, grad_hidden, layer_stack, mix_flat, ln_gain
    )

    up_half = up_bias.shape[0]
    up_bias_grad = up_bias_part[0, :up_half]
    qkv_bias_grad = bias_sums[0]
    for h in range(1, halves):
        up_bias_grad = up_bias_grad + swap(
            up_bias_part[0, h * up_half : (h + 1) * up_half], "zh", h
        )
        qkv_bias_grad = qkv_bias_grad + swap(bias_sums[h], "zh", h)
    up_bias_grad = sum_groups(up_bias_grad, ("row",))
    qkv_bias_grad = sum_groups(qkv_bias_grad, ("row",))
    early = sum_everywhere(jnp.concatenate([mix_in_part, mix_sums[:2]], axis=0))
    mix_in_grad = early[: mix_in_part.shape[0]].T
    down_bias_grad, mix_gain_grad = early[-2], early[-1]
    mix_out_grad = sum_everywhere(mix_out_part)
    late = sum_everywhere(
        jnp.concatenate(
            [
                gain_part.reshape(3, 8, width).sum(axis=1),
                mid_sums[0:1],
                bias_part.reshape(3, 8, width).sum(axis=1),
                mid_sums[1:3],
            ],
            axis=0,
        )
    )
    return (
        layer_out,
        coeff_out,
        stack_grad,
        coeffs_grad.reshape(mix_coeffs.shape),
        late[0:4],
        late[4:8],
        qkv_grad,
        qkv_bias_grad,
        out_w_grad,
        late[8],
        up_grad,
        up_bias_grad,
        down_grad,
        down_bias_grad,
        mix_gain_grad,
        mix_in_grad,
        mix_out_grad,
    )


def solution(mesh):
    rows, cols = mesh.shape["row"], mesh.shape["col"]
    col = ("zh", "zl", "core")

    def run(*args):
        seqs = args[2].shape[0] // rows
        fine = Mesh(mesh.devices.reshape(rows, seqs, cols // (2 * seqs), 2), ALL)
        in_specs = (
            P(None, ALL, None),
            P(ALL, None, None),
            P("row"),
            P(),
            P(),
            P(None, "row", col),
            P(None, col),
            P(col, "row"),
            P(),
            P("row", col),
            P(col),
            P(col, "row"),
            P(),
            P(),
            P(),
            P(),
            P(ALL, None),
            P(ALL, None),
        )
        out_specs = (
            P(ALL, None),
            P(ALL, None),
            P(None, ALL, None),
            P(ALL, None, None),
            P(),
            P(),
            P(None, "row", col),
            P(None, col),
            P(col, "row"),
            P(),
            P("row", col),
            P(col),
            P(col, "row"),
            P(),
            P(),
            P(),
            P(),
        )
        return jax.shard_map(
            on_device, mesh=fine, in_specs=in_specs, out_specs=out_specs, check_vma=False
        )(*args)

    return run
```

time: 3670 us -> 1030 us (0.28)
  waiting for transfers between devices: 2130 us -> 573 us
  blocking collectives: 505 us -> 0 us
  local copies, waits for them, and re-layouts: 499 us -> 40.8 us
  Pallas kernels: 0 us -> 272 us
  matrix products: 276 us -> 41.8 us
  other arithmetic: 208 us -> 25 us
    reduce_scatter x8 -> x3, waiting for transfers between devices: 982 us -> 0.01 us  [scatter_weight(): mine = lax.psum_scatter(grad, 'row', scatter_dimension=0, tiled=True)]
    all_gather x8 -> x4, waiting for transfers between devices: 959 us -> 0.06 us  [gather_weight(): return lax.all_gather(values, 'row', axis=0, tiled=True)]
    ppermute x0 -> x65, waiting for transfers between devices: none -> 573 us  [swap(): return lax.ppermute(values, axis, [(i, i ^ bits) for i in range(size)])]
    all_to_all x4 -> x0, blocking collectives: 505 us -> none  [split_features(): lax.all_to_all(values, 'row', split_axis=2, concat_axis=0, tiled=True)]
    pallas_call x0 -> x23, Pallas kernels: none -> 272 us  [the longest x2 109 us: feed(): pl.pallas_call(functools.partial(feed_kernel, blocks, back), grid=(hidden...]
    dot_general x35 -> x6, matrix products: 276 us -> 41.8 us  [dot(): lax.dot_general(a, b, dims, precision=precision, preferred_element_type=F32)]
    psum x2 -> x0, waiting for transfers between devices: 124 us -> none  [on_device(): lax.psum((gain_early + gain_late, bias_early + bias_late, mix_gain_part,...]
    unnamed x189 -> x156, local copies, waits for them, and re-layouts: 136 us -> 22 us
  transfers between devices with their start and end apart: 22 -> 72, of which waited for: 21 -> 33; matrix products, arithmetic and copies ran while one was open for 4% -> 8% of each run, Pallas kernels for 0% -> 20%
where the time goes in v1:
time: 1030 us; the launch traced here: 1020 us
  waiting for transfers between devices  573 us (56%)
  Pallas kernels  272 us (26%)
  starting transfers between devices  48.8 us (5%)
  matrix products  41.8 us (4%)
  local copies, waits for them, and re-layouts  40.8 us (4%)
  other arithmetic  25 us (2%)
  between operations  15.5 us (2%)
    ppermute x65, waiting for transfers between devices, swap(): return lax.ppermute(values, axis, [(i, i ^ bits) for i in range(size)])  573 us
    pallas_call x2, Pallas kernels, feed(): pl.pallas_call(functools.partial(feed_kernel, blocks, back), grid=(hidden...  109 us
    ppermute x65, starting transfers between devices, swap(): return lax.ppermute(values, axis, [(i, i ^ bits) for i in range(size)])  48.5 us
    dot_general x6, matrix products, dot(): lax.dot_general(a, b, dims, precision=precision, preferred_element_type=F32)  41.8 us
    pallas_call x8, Pallas kernels, proj(): pl.pallas_call(functools.partial(proj_kernel, blocks, tables is not None)...  39.6 us
    pallas_call x1, Pallas kernels, front_back(): pl.pallas_call(functools.partial(front_back_kernel, pieces), grid=(tokens...  28.2 us
    pallas_call x4, Pallas kernels, unproj(): pl.pallas_call(functools.partial(unproj_kernel, halves), grid=(width // t...  22.7 us
    unnamed x156, local copies, waits for them, and re-layouts  22 us
  transfers between devices with their start and end apart: 72, of which 33 were waited for; matrix products, arithmetic and copies ran while one was open for 8% of the time, Pallas kernels for 20%

profile of v1, /device:TPU:0, one launch (start us, length us, event | category | flops | bytes accessed | tf_op | source)
XLA Modules:
  0.0 1017.5 jit_solution(3039474592427048308)
XLA Ops:
  14.9 45.8 %collective-permute-done.9 = bf16[512,1024]{1,0:T(8,128)(2,1)S(1)} collective-permute-done((bf16[512,1024]{1,0:T(8,128)(2,1)}, bf16[512,1024]{1,0:T(8,128)(2,1)S(1)}, u32[]{:S(2)}, u32[]{:S(2)}) %collective-permute-start.9) | collective-permute-done | bytes 1048608 | tf_op jit(solution)/shard_map/ppermute | solution.py:594
  62.4 47.7 %collective-permute-done.18 = bf16[512,1024]{1,0:T(8,128)(2,1)S(1)} collective-permute-done((bf16[512,1024]{1,0:T(8,128)(2,1)S(1)}, bf16[512,1024]{1,0:T(8,128)(2,1)S(1)}, u32[]{:S(2)}, u32[]{:S(2)}) %collective-permute-start.18) | collective-permute-done | bytes 1048608 | tf_op jit(solution)/shard_map/ppermute | solution.py:594
  111.8 46.8 %collective-permute-done.17 = bf16[512,1024]{1,0:T(8,128)(2,1)S(1)} collective-permute-done((bf16[512,1024]{1,0:T(8,128)(2,1)S(1)}, bf16[512,1024]{1,0:T(8,128)(2,1)S(1)}, u32[]{:S(2)}, u32[]{:S(2)}) %collective-permute-start.17) | collective-permute-done | bytes 1048608 | tf_op jit(solution)/shard_map/ppermute | solution.py:594
  160.9 12.8 %front.1 = (bf16[256,2048]{1,0:T(8,128)(2,1)}, bf16[256,2048]{1,0:T(8,128)(2,1)}, bf16[256,2048]{1,0:T(8,128)(2,1)}, f32[256,2048]{1,0:T(8,128)}) custom-call(bf16[8,256,2048]{2,1,0:T(8,128)(2,1)} %refs_10_.1, f32[256,32]{1,0:T(8,128)} %copy.54.mix_ref.refs_11_, f32[4,2048]{1,0:T(4,128)} %refs_12_.1, f32[4,2048]{1,0:T(4,128)} %refs_6_.2), custom_call_target="tpu_custom_call" | custom-call | flops 36700160 | bytes 13631488 | tf_op jit(solution)/shard_map/front/pallas_call | solution.py:81
  178.0 22.0 %collective-permute-done.1.refs_2_ = bf16[256,2048]{1,0:T(8,128)(2,1)S(1)} collective-permute-done((bf16[256,2048]{1,0:T(8,128)(2,1)}, bf16[256,2048]{1,0:T(8,128)(2,1)S(1)}, u32[]{:S(2)}, u32[]{:S(2)}) %collective-permute-start.1) | collective-permute-done | bytes 1048608 | tf_op jit(solution)/shard_map/ppermute | solution.py:594
  200.9 40.8 %collective-permute-done.10 = f32[3,256]{1,0:T(4,128)S(1)} collective-permute-done((f32[3,256]{1,0:T(4,128)S(1)}, f32[3,256]{1,0:T(4,128)S(1)}, u32[]{:S(2)}, u32[]{:S(2)}) %collective-permute-start.10) | collective-permute-done | bytes 3104 | tf_op jit(solution)/shard_map/ppermute | solution.py:594
  254.0 5.9 proj.9.k_ref
  264.4 8.2 attend.2
  287.5 8.1 attend.3
  307.3 23.9 %collective-permute-done.13.refs_2_ = bf16[256,2048]{1,0:T(8,128)(2,1)S(1)} collective-permute-done((bf16[256,2048]{1,0:T(8,128)(2,1)S(1)}, bf16[256,2048]{1,0:T(8,128)(2,1)S(1)}, u32[]{:S(2)}, u32[]{:S(2)}) %collective-permute-start.13) | collective-permute-done | bytes 1048608 | tf_op jit(solution)/shard_map/ppermute | solution.py:594
  338.6 23.5 %collective-permute-done.15.refs_2_ = bf16[256,2048]{1,0:T(8,128)(2,1)S(1)} collective-permute-done((bf16[256,2048]{1,0:T(8,128)(2,1)}, bf16[256,2048]{1,0:T(8,128)(2,1)S(1)}, u32[]{:S(2)}, u32[]{:S(2)}) %collective-permute-start.15) | collective-permute-done | bytes 1048608 | tf_op jit(solution)/shard_map/ppermute | solution.py:594
  368.6 55.3 %feed.1 = (bf16[1024,2048]{1,0:T(8,128)(2,1)}, bf16[1024,2048]{1,0:T(8,128)(2,1)}, bf16[256,2048]{1,0:T(8,128)(2,1)}, bf16[256,2048]{1,0:T(8,128)(2,1)}, bf16[25...) custom-call(bf16[256,2048]{1,0:T(8,128)(2,1)} %get-tuple-element.87.refs_0_, bf16[256,2048]{1,0:T(8,128)(2,1)} %copy-done.59, ...), custom_call_target="tpu_custom_call" | custom-call | flops 17179869184 | bytes 33562624 | tf_op jit(solution)/shard_map/feed/pallas_call | solution.py:509
  431.8 21.9 %collective-permute-done.22.refs_2_ = bf16[256,2048]{1,0:T(8,128)(2,1)S(1)} collective-permute-done((bf16[256,2048]{1,0:T(8,128)(2,1)S(1)}, bf16[256,2048]{1,0:T(8,128)(2,1)S(1)}, u32[]{:S(2)}, u32[]{:S(2)}) %collective-permute-start.22) | collective-permute-done | bytes 1048608 | tf_op jit(solution)/shard_map/ppermute | solution.py:594
  454.7 10.9 %mixing.1 = (f32[256,2048]{1,0:T(8,128)}, f32[256,36]{1,0:T(8,128)}, f32[256,2048]{1,0:T(8,128)}, bf16[256,2048]{1,0:T(8,128)(2,1)}, f32[8,2048]{1,0:T(8,128)}, /*index=5*/f32[36,2048]{1,0:T(8,128)}, f32[36,36]{1,0:T(8,128)}) custom-call(bf16[256,2048]{1,0:T(8,128)(2,1)} %get-tuple-element.88.refs_0_, bf16[256,2048]{1,0:T(8,128)(2,1)} %copy-done.28, ...), custom_call_target="tpu_custom_call" | custom-call | flops 1572864000 | bytes 11936832 | tf_op jit(solution)/shard_map/mixing/pallas_call | solution.py:578
  466.9 23.4 %collective-permute-done.24.refs_2_ = bf16[256,2048]{1,0:T(8,128)(2,1)S(1)} collective-permute-done((bf16[256,2048]{1,0:T(8,128)(2,1)}, bf16[256,2048]{1,0:T(8,128)(2,1)S(1)}, u32[]{:S(2)}, u32[]{:S(2)}) %collective-permute-start.24) | collective-permute-done | bytes 1048608 | tf_op jit(solution)/shard_map/ppermute | solution.py:594
  493.0 12.8 %convolution_convert_fusion = bf16[2048,2048]{1,0:T(8,128)(2,1)} fusion(bf16[1024,2048]{1,0:T(8,128)(2,1)S(1)} %copy-done.70, bf16[256,2048]{1,0:T(8,128)(2,1)S(1)} %collective-permute-done.25.refs_3_, bf16[256,2048]{1,0:T(8,128)(2,1)S(1)} %collective-permute-done.24.refs_2_, bf16[256,2048]{1,0:T(8,128)(2,1)S(1)} %collective-permute-done.23.refs_1_, ...), kind=kOutput, calls=%fused_computation | convolution fusion | flops 8610906112 | bytes 16777216 | tf_op jit(solution)/shard_map/dot_general | solution.py:29
  505.9 54.0 %feed_back.1 = (bf16[1024,2048]{1,0:T(8,128)(2,1)}, f32[1,2048]{1,0:T(1,128)}, bf16[256,2048]{1,0:T(8,128)(2,1)}, bf16[256,2048]{1,0:T(8,128)(2,1)}, bf16[256,20...) custom-call(bf16[256,2048]{1,0:T(8,128)(2,1)} %get-tuple-element.95.refs_0_, bf16[256,2048]{1,0:T(8,128)(2,1)} %copy-done.66, ...), custom_call_target="tpu_custom_call" | custom-call | flops 17179869184 | bytes 33562624 | tf_op jit(solution)/shard_map/feed_back/pallas_call | solution.py:509
  560.0 13.4 %convolution_convert_fusion.1 = bf16[2048,2048]{1,0:T(8,128)(2,1)} fusion(bf16[1024,2048]{1,0:T(8,128)(2,1)} %get-tuple-element.131, bf16[256,2048]{1,0:T(8,128)(2,1)S(1)} %copy-done.62, bf16[256,2048]{1,0:T(8,128)(2,1)S(1)} %copy-done.58, bf16[256,2048]{1,0:T(8,128)(2,1)S(1)} %copy-done.60, bf16[256,2048]{1,0:T(8,128)(2,1)S(1)} %copy-done.56), kind=kOutput, calls=%fused_computation.1 | convolution fusion | flops 8610906112 | bytes 16777216 | tf_op jit(solution)/shard_map/dot_general | solution.py:29
  578.9 24.0 %collective-permute-done.28.refs_2_ = bf16[256,2048]{1,0:T(8,128)(2,1)S(1)} collective-permute-done((bf16[256,2048]{1,0:T(8,128)(2,1)S(1)}, bf16[256,2048]{1,0:T(8,128)(2,1)S(1)}, u32[]{:S(2)}, u32[]{:S(2)}) %collective-permute-start.28) | collective-permute-done | bytes 1048608 | tf_op jit(solution)/shard_map/ppermute | solution.py:594
  603.9 6.7 middle_back.1
  611.8 23.5 %collective-permute-done.30.refs_2_ = bf16[256,2048]{1,0:T(8,128)(2,1)S(1)} collective-permute-done((bf16[256,2048]{1,0:T(8,128)(2,1)}, bf16[256,2048]{1,0:T(8,128)(2,1)S(1)}, u32[]{:S(2)}, u32[]{:S(2)}) %collective-permute-start.30) | collective-permute-done | bytes 1048608 | tf_op jit(solution)/shard_map/ppermute | solution.py:594
  648.1 10.3 %attend_back.3 = (bf16[1024,256]{1,0:T(8,128)(2,1)}, bf16[1024,256]{1,0:T(8,128)(2,1)}, bf16[1024,256]{1,0:T(8,128)(2,1)}, f32[2,8,128]{2,1,0:T(8,128)}) custom-call(s32[5]{0:T(128)} %pad_add_fusion.scalars, bf16[1024,256]{1,0:T(8,128)(2,1)} %proj.11.q_ref, bf16[1024,256]{1,0:T(8,128)(2,1)} %proj.12.k_ref, bf16[1024,256]{1,0:T(8,128)(2,1)} %proj.13.v_ref, ...), custom_call_target="tpu_custom_call" | custom-call | flops 4294967296 | bytes 3678208 | tf_op jit(solution)/shard_map/attend_back/pallas_call | solution.py:352
  658.4 10.6 %attend_back.2 = (bf16[1024,256]{1,0:T(8,128)(2,1)}, bf16[1024,256]{1,0:T(8,128)(2,1)}, bf16[1024,256]{1,0:T(8,128)(2,1)}, f32[2,8,128]{2,1,0:T(8,128)}) custom-call(s32[5]{0:T(128)} %pad_add_fusion.scalars, bf16[1024,256]{1,0:T(8,128)(2,1)} %proj.8.q_ref, bf16[1024,256]{1,0:T(8,128)(2,1)} %proj.9.k_ref, bf16[1024,256]{1,0:T(8,128)(2,1)} %proj.10.v_ref, ...), custom_call_target="tpu_custom_call" | custom-call | flops 4294967296 | bytes 3678208 | tf_op jit(solution)/shard_map/attend_back/pallas_call | solution.py:352
  717.5 10.9 %collective-permute-done.62 = f32[36,36]{1,0:T(8,128)S(1)} collective-permute-done((f32[36,36]{1,0:T(8,128)S(1)}, f32[36,36]{1,0:T(8,128)S(1)}, u32[]{:S(2)}, u32[]{:S(2)}) %collective-permute-start.62) | collective-permute-done | bytes 5216 | tf_op jit(solution)/shard_map/ppermute | solution.py:594
  730.5 6.0 unproj.7
  752.4 21.3 %collective-permute-done.34.refs_2_ = bf16[256,2048]{1,0:T(8,128)(2,1)S(1)} collective-permute-done((bf16[256,2048]{1,0:T(8,128)(2,1)S(1)}, bf16[256,2048]{1,0:T(8,128)(2,1)S(1)}, u32[]{:S(2)}, u32[]{:S(2)}) %collective-permute-start.34) | collective-permute-done | bytes 1048608 | tf_op jit(solution)/shard_map/ppermute | solution.py:594
  773.7 22.5 %collective-permute-done.37.refs_5_ = bf16[256,2048]{1,0:T(8,128)(2,1)S(1)} collective-permute-done((bf16[256,2048]{1,0:T(8,128)(2,1)S(1)}, bf16[256,2048]{1,0:T(8,128)(2,1)S(1)}, u32[]{:S(2)}, u32[]{:S(2)}) %collective-permute-start.37) | collective-permute-done | bytes 1048608 | tf_op jit(solution)/shard_map/ppermute | solution.py:594
  796.2 21.7 %collective-permute-done.40.refs_8_ = bf16[256,2048]{1,0:T(8,128)(2,1)S(1)} collective-permute-done((bf16[256,2048]{1,0:T(8,128)(2,1)S(1)}, bf16[256,2048]{1,0:T(8,128)(2,1)S(1)}, u32[]{:S(2)}, u32[]{:S(2)}) %collective-permute-start.40) | collective-permute-done | bytes 1048608 | tf_op jit(solution)/shard_map/ppermute | solution.py:594
  818.9 28.2 %front_back.1 = (f32[8,256,2048]{2,1,0:T(8,128)}, f32[256,32]{1,0:T(8,128)}, f32[24,2048]{1,0:T(8,128)}, f32[24,2048]{1,0:T(8,128)}) custom-call(bf16[256,2048]{1,0:T(8,128)(2,1)} %get-tuple-element.107.refs_0_, bf16[256,2048]{1,0:T(8,128)(2,1)} %copy-done.18, bf16[256,2048]{1,0:T(8,128)(2,1)} %copy-done.23, bf16[256,2048]{1,0:T(8,128)(2,1)} %get-tuple-element.113.refs_3_, ...), custom_call_target="tpu_custom_call" | custom-call | flops 131072000 | bytes 37126144 | tf_op jit(solution)/shard_map/front_back/pallas_call | solution.py:162
  875.4 64.0 %collective-permute-done.45 = f32[9,2048]{1,0:T(8,128)S(1)} collective-permute-done((f32[9,2048]{1,0:T(8,128)S(1)}, f32[9,2048]{1,0:T(8,128)S(1)}, u32[]{:S(2)}, u32[]{:S(2)}) %collective-permute-start.45) | collective-permute-done | bytes 73760 | tf_op jit(solution)/shard_map/ppermute | solution.py:594
  946.7 37.8 %collective-permute-done.50 = bf16[512,1024]{1,0:T(8,128)(2,1)} collective-permute-done((bf16[512,1024]{1,0:T(8,128)(2,1)S(1)}, bf16[512,1024]{1,0:T(8,128)(2,1)}, u32[]{:S(2)}, u32[]{:S(2)}) %collective-permute-start.50) | collective-permute-done | bytes 1048608 | tf_op jit(solution)/shard_map/ppermute | solution.py:594
  987.7 18.4 %collective-permute-done.46 = bf16[512,1024]{0,1:T(8,128)(2,1)} collective-permute-done((bf16[512,1024]{0,1:T(8,128)(2,1)}, bf16[512,1024]{0,1:T(8,128)(2,1)}, u32[]{:S(2)}, u32[]{:S(2)}) %collective-permute-start.46) | collective-permute-done | bytes 1048608 | tf_op jit(solution)/shard_map/ppermute | solution.py:594
  (375 shorter events, 219.0 us)
Async XLA Ops:
  7.2 241.6 %all-gather.5.cloned.1.call-start = ((), (), s32[]{:S(2)}) async-start(), calls=%async_computation.3 | async-start | bytes 5242880 | tf_op jit(solution)/shard_map/all_gather | solution.py:637
  10.7 262.0 %all-gather.7.cloned.1.call-start = ((), (), s32[]{:S(2)}) async-start(), calls=%async_computation.4 | async-start | bytes 5242880 | tf_op jit(solution)/shard_map/all_gather | solution.py:637
  10.8 49.9 %collective-permute-start.9 = (bf16[512,1024]{1,0:T(8,128)(2,1)}, bf16[512,1024]{1,0:T(8,128)(2,1)S(1)}, u32[]{:S(2)}, u32[]{:S(2)}) collective-permute-start(bf16[512,1024]{1,0:T(8,128)(2,1)} %pad_maximum_fusion.2), channel_id=1, source_target_pairs={{0,4},{4,0},{1,5},{5,1},{2,6},{6,2},{3,7},{7,3},{8,12},{12,8},{9,1... | collective-permute-start | bytes 3145736 | tf_op jit(solution)/shard_map/ppermute | solution.py:594
  61.7 305.6 %all-gather.11.cloned.1.call-start = ((), (), s32[]{:S(2)}) async-start(), calls=%async_computation.6 | async-start | bytes 10485760 | tf_op jit(solution)/shard_map/all_gather | solution.py:637
  62.3 47.8 %collective-permute-start.18 = (bf16[512,1024]{1,0:T(8,128)(2,1)S(1)}, bf16[512,1024]{1,0:T(8,128)(2,1)S(1)}, u32[]{:S(2)}, u32[]{:S(2)}) collective-permute-start(bf16[512,1024]{1,0:T(8,128)(2,1)S(1)} %bitcast.45), channel_id=1, source_target_pairs={{0,4},{4,0},{1,5},{5,1},{2,6},{6,2},{3,7},{7,3},{8,12},{12,8},{9,1... | collective-permute-start | bytes 3145736 | tf_op jit(solution)/shard_map/ppermute | solution.py:594
  111.6 255.7 %all-gather.9.cloned.1.call-start = ((), (), s32[]{:S(2)}) async-start(), calls=%async_computation.5 | async-start | bytes 10485760 | tf_op jit(solution)/shard_map/all_gather | solution.py:637
  111.7 46.9 %collective-permute-start.17 = (bf16[512,1024]{1,0:T(8,128)(2,1)S(1)}, bf16[512,1024]{1,0:T(8,128)(2,1)S(1)}, u32[]{:S(2)}, u32[]{:S(2)}) collective-permute-start(bf16[512,1024]{1,0:T(8,128)(2,1)S(1)} %copy-done.34), channel_id=1, source_target_pairs={{0,4},{4,0},{1,5},{5,1},{2,6},{6,2},{3,7},{7,3},{8,12},{12,8},{9,1... | collective-permute-start | bytes 3145736 | tf_op jit(solution)/shard_map/ppermute | solution.py:594
  160.1 702.7 %reduce-scatter.8.cloned.1.call-start = ((), (), s32[]{:S(2)}) async-start(), calls=%async_computation.9 | async-start | bytes 10485760 | tf_op jit(solution)/shard_map/reduce_scatter | solution.py:641
  173.7 26.3 %collective-permute-start.1 = (bf16[256,2048]{1,0:T(8,128)(2,1)}, bf16[256,2048]{1,0:T(8,128)(2,1)S(1)}, u32[]{:S(2)}, u32[]{:S(2)}) collective-permute-start(bf16[256,2048]{1,0:T(8,128)(2,1)} %get-tuple-element.77.refs_0_), channel_id=1, source_target_pairs={{0,2},{2,0},{1,3},{3,1},{4,6},{6,4},{5,7},{7,5},{8,10},{10,8},{9,1... | collective-permute-start | bytes 3145736 | tf_op jit(solution)/shard_map/ppermute | solution.py:594
  173.7 68.0 %collective-permute-start.4 = (bf16[256,2048]{1,0:T(8,128)(2,1)}, bf16[256,2048]{1,0:T(8,128)(2,1)S(1)}, u32[]{:S(2)}, u32[]{:S(2)}) collective-permute-start(bf16[256,2048]{1,0:T(8,128)(2,1)} %get-tuple-element.78.refs_0_), channel_id=1, source_target_pairs={{0,2},{2,0},{1,3},{3,1},{4,6},{6,4},{5,7},{7,5},{8,10},{10,8},{9,1... | collective-permute-start | bytes 3145736 | tf_op jit(solution)/shard_map/ppermute | solution.py:594
  175.7 66.5 %collective-permute-start = (bf16[256,2048]{1,0:T(8,128)(2,1)}, bf16[256,2048]{1,0:T(8,128)(2,1)}, u32[]{:S(2)}, u32[]{:S(2)}) collective-permute-start(bf16[256,2048]{1,0:T(8,128)(2,1)} %get-tuple-element.77.refs_0_), channel_id=1, source_target_pairs={{0,1},{1,0},{2,3},{3,2},{4,5},{5,4},{6,7},{7,6},{8,9},{9,8},{10,11... | collective-permute-start | bytes 3145736 | tf_op jit(solution)/shard_map/ppermute | solution.py:594
  175.7 68.1 %collective-permute-start.7 = (bf16[256,2048]{1,0:T(8,128)(2,1)}, bf16[256,2048]{1,0:T(8,128)(2,1)S(1)}, u32[]{:S(2)}, u32[]{:S(2)}) collective-permute-start(bf16[256,2048]{1,0:T(8,128)(2,1)} %get-tuple-element.79.refs_0_), channel_id=1, source_target_pairs={{0,2},{2,0},{1,3},{3,1},{4,6},{6,4},{5,7},{7,5},{8,10},{10,8},{9,1... | collective-permute-start | bytes 3145736 | tf_op jit(solution)/shard_map/ppermute | solution.py:594
  175.8 65.9 %collective-permute-start.10 = (f32[3,256]{1,0:T(4,128)S(1)}, f32[3,256]{1,0:T(4,128)S(1)}, u32[]{:S(2)}, u32[]{:S(2)}) collective-permute-start(f32[3,256]{1,0:T(4,128)S(1)} %copy-done.52), channel_id=1, source_target_pairs={{0,4},{4,0},{1,5},{5,1},{2,6},{6,2},{3,7},{7,3},{8,12},{12,8},{9,1... | collective-permute-start | bytes 9224 | tf_op jit(solution)/shard_map/ppermute | solution.py:594
  200.0 48.8 %collective-permute-start.2 = (bf16[256,2048]{1,0:T(8,128)(2,1)S(1)}, bf16[256,2048]{1,0:T(8,128)(2,1)}, u32[]{:S(2)}, u32[]{:S(2)}) collective-permute-start(bf16[256,2048]{1,0:T(8,128)(2,1)S(1)} %collective-permute-done.1.refs_2_), channel_id=1, source_target_pairs={{0,1},{1,0},{2,3},{3,2},{4,5},{5,4},{6,7},{7,6},{8,9},{9,8},{10,11... | collective-permute-start | bytes 3145736 | tf_op jit(solution)/shard_map/ppermute | solution.py:594
  305.7 25.5 %collective-permute-start.13 = (bf16[256,2048]{1,0:T(8,128)(2,1)S(1)}, bf16[256,2048]{1,0:T(8,128)(2,1)S(1)}, u32[]{:S(2)}, u32[]{:S(2)}) collective-permute-start(bf16[256,2048]{1,0:T(8,128)(2,1)S(1)} %add_convert_fusion.5), channel_id=1, source_target_pairs={{0,2},{2,0},{1,3},{3,1},{4,6},{6,4},{5,7},{7,5},{8,10},{10,8},{9,1... | collective-permute-start | bytes 3145736 | tf_op jit(solution)/shard_map/ppermute | solution.py:594
  337.2 24.8 %collective-permute-start.15 = (bf16[256,2048]{1,0:T(8,128)(2,1)}, bf16[256,2048]{1,0:T(8,128)(2,1)S(1)}, u32[]{:S(2)}, u32[]{:S(2)}) collective-permute-start(bf16[256,2048]{1,0:T(8,128)(2,1)} %get-tuple-element.87.refs_0_), channel_id=1, source_target_pairs={{0,2},{2,0},{1,3},{3,1},{4,6},{6,4},{5,7},{7,5},{8,10},{10,8},{9,1... | collective-permute-start | bytes 3145736 | tf_op jit(solution)/shard_map/ppermute | solution.py:594
  338.6 28.7 %collective-permute-start.14 = (bf16[256,2048]{1,0:T(8,128)(2,1)}, bf16[256,2048]{1,0:T(8,128)(2,1)S(1)}, u32[]{:S(2)}, u32[]{:S(2)}) collective-permute-start(bf16[256,2048]{1,0:T(8,128)(2,1)} %get-tuple-element.87.refs_0_), channel_id=1, source_target_pairs={{0,1},{1,0},{2,3},{3,2},{4,5},{5,4},{6,7},{7,6},{8,9},{9,8},{10,11... | collective-permute-start | bytes 3145736 | tf_op jit(solution)/shard_map/ppermute | solution.py:594
  428.4 25.3 %collective-permute-start.22 = (bf16[256,2048]{1,0:T(8,128)(2,1)S(1)}, bf16[256,2048]{1,0:T(8,128)(2,1)S(1)}, u32[]{:S(2)}, u32[]{:S(2)}) collective-permute-start(bf16[256,2048]{1,0:T(8,128)(2,1)S(1)} %add_convert_fusion.4), channel_id=1, source_target_pairs={{0,2},{2,0},{1,3},{3,1},{4,6},{6,4},{5,7},{7,5},{8,10},{10,8},{9,1... | collective-permute-start | bytes 3145736 | tf_op jit(solution)/shard_map/ppermute | solution.py:594
  505.8 364.1 %reduce-scatter.6.cloned.1.call-start = ((), (), s32[]{:S(2)}) async-start(), calls=%async_computation.8 | async-start | bytes 10485760 | tf_op jit(solution)/shard_map/reduce_scatter | solution.py:641
  573.4 366.7 %reduce-scatter.4.cloned.1.call-start = ((), (), s32[]{:S(2)}) async-start(), calls=%async_computation.7 | async-start | bytes 10485760 | tf_op jit(solution)/shard_map/reduce_scatter | solution.py:641
  577.6 25.3 %collective-permute-start.28 = (bf16[256,2048]{1,0:T(8,128)(2,1)S(1)}, bf16[256,2048]{1,0:T(8,128)(2,1)S(1)}, u32[]{:S(2)}, u32[]{:S(2)}) collective-permute-start(bf16[256,2048]{1,0:T(8,128)(2,1)S(1)} %add_convert_fusion.3), channel_id=1, source_target_pairs={{0,2},{2,0},{1,3},{3,1},{4,6},{6,4},{5,7},{7,5},{8,10},{10,8},{9,1... | collective-permute-start | bytes 3145736 | tf_op jit(solution)/shard_map/ppermute | solution.py:594
  700.1 36.4 %collective-permute-start.33 = (bf16[256,2048]{1,0:T(8,128)(2,1)}, bf16[256,2048]{1,0:T(8,128)(2,1)S(1)}, u32[]{:S(2)}, u32[]{:S(2)}) collective-permute-start(bf16[256,2048]{1,0:T(8,128)(2,1)} %get-tuple-element.110), channel_id=1, source_target_pairs={{0,1},{1,0},{2,3},{3,2},{4,5},{5,4},{6,7},{7,6},{8,9},{9,8},{10,11... | collective-permute-start | bytes 3145736 | tf_op jit(solution)/shard_map/ppermute | solution.py:594
  707.1 30.2 %collective-permute-start.36 = (bf16[256,2048]{1,0:T(8,128)(2,1)}, bf16[256,2048]{1,0:T(8,128)(2,1)S(1)}, u32[]{:S(2)}, u32[]{:S(2)}) collective-permute-start(bf16[256,2048]{1,0:T(8,128)(2,1)} %get-tuple-element.116), channel_id=1, source_target_pairs={{0,1},{1,0},{2,3},{3,2},{4,5},{5,4},{6,7},{7,6},{8,9},{9,8},{10,11... | collective-permute-start | bytes 3145736 | tf_op jit(solution)/shard_map/ppermute | solution.py:594
  740.2 33.5 %collective-permute-start.34 = (bf16[256,2048]{1,0:T(8,128)(2,1)S(1)}, bf16[256,2048]{1,0:T(8,128)(2,1)S(1)}, u32[]{:S(2)}, u32[]{:S(2)}) collective-permute-start(bf16[256,2048]{1,0:T(8,128)(2,1)S(1)} %add_convert_fusion.2), channel_id=1, source_target_pairs={{0,2},{2,0},{1,3},{3,1},{4,6},{6,4},{5,7},{7,5},{8,10},{10,8},{9,1... | collective-permute-start | bytes 3145736 | tf_op jit(solution)/shard_map/ppermute | solution.py:594
  745.6 50.6 %collective-permute-start.37 = (bf16[256,2048]{1,0:T(8,128)(2,1)S(1)}, bf16[256,2048]{1,0:T(8,128)(2,1)S(1)}, u32[]{:S(2)}, u32[]{:S(2)}) collective-permute-start(bf16[256,2048]{1,0:T(8,128)(2,1)S(1)} %add_convert_fusion.1), channel_id=1, source_target_pairs={{0,2},{2,0},{1,3},{3,1},{4,6},{6,4},{5,7},{7,5},{8,10},{10,8},{9,1... | collective-permute-start | bytes 3145736 | tf_op jit(solution)/shard_map/ppermute | solution.py:594
  746.5 71.5 %collective-permute-start.40 = (bf16[256,2048]{1,0:T(8,128)(2,1)S(1)}, bf16[256,2048]{1,0:T(8,128)(2,1)S(1)}, u32[]{:S(2)}, u32[]{:S(2)}) collective-permute-start(bf16[256,2048]{1,0:T(8,128)(2,1)S(1)} %add_convert_fusion), channel_id=1, source_target_pairs={{0,2},{2,0},{1,3},{3,1},{4,6},{6,4},{5,7},{7,5},{8,10},{10,8},{9,1... | collective-permute-start | bytes 3145736 | tf_op jit(solution)/shard_map/ppermute | solution.py:594
  749.4 104.9 %collective-permute-start.64 = (f32[36,36]{1,0:T(8,128)S(1)}, f32[36,36]{1,0:T(8,128)S(1)}, u32[]{:S(2)}, u32[]{:S(2)}) collective-permute-start(f32[36,36]{1,0:T(8,128)S(1)} %add.158), channel_id=1, source_target_pairs={{0,4},{4,0},{1,5},{5,1},{2,6},{6,2},{3,7},{7,3},{8,12},{12,8},{9,1... | collective-permute-start | bytes 15560 | tf_op jit(solution)/shard_map/ppermute | solution.py:594
  751.0 103.9 %collective-permute-start.59 = (f32[38,2048]{1,0:T(8,128)S(1)}, f32[38,2048]{1,0:T(8,128)S(1)}, u32[]{:S(2)}, u32[]{:S(2)}) collective-permute-start(f32[38,2048]{1,0:T(8,128)S(1)} %add.153), channel_id=1, source_target_pairs={{0,4},{4,0},{1,5},{5,1},{2,6},{6,2},{3,7},{7,3},{8,12},{12,8},{9,1... | collective-permute-start | bytes 933896 | tf_op jit(solution)/shard_map/ppermute | solution.py:594
  864.0 78.9 %collective-permute-start.54 = (bf16[512,1024]{1,0:T(8,128)(2,1)S(1)}, bf16[512,1024]{1,0:T(8,128)(2,1)}, u32[]{:S(2)}, u32[]{:S(2)}) collective-permute-start(bf16[512,1024]{1,0:T(8,128)(2,1)S(1)} %slice.181), channel_id=1, source_target_pairs={{0,4},{4,0},{1,5},{5,1},{2,6},{6,2},{3,7},{7,3},{8,12},{12,8},{9,1... | collective-permute-start | bytes 3145736 | tf_op jit(solution)/shard_map/ppermute | solution.py:594
  868.6 70.8 %collective-permute-start.45 = (f32[9,2048]{1,0:T(8,128)S(1)}, f32[9,2048]{1,0:T(8,128)S(1)}, u32[]{:S(2)}, u32[]{:S(2)}) collective-permute-start(f32[9,2048]{1,0:T(8,128)S(1)} %add.139), channel_id=1, source_target_pairs={{0,4},{4,0},{1,5},{5,1},{2,6},{6,2},{3,7},{7,3},{8,12},{12,8},{9,1... | collective-permute-start | bytes 221192 | tf_op jit(solution)/shard_map/ppermute | solution.py:594
  871.2 113.2 %collective-permute-start.50 = (bf16[512,1024]{1,0:T(8,128)(2,1)S(1)}, bf16[512,1024]{1,0:T(8,128)(2,1)}, u32[]{:S(2)}, u32[]{:S(2)}) collective-permute-start(bf16[512,1024]{1,0:T(8,128)(2,1)S(1)} %slice.179), channel_id=1, source_target_pairs={{0,4},{4,0},{1,5},{5,1},{2,6},{6,2},{3,7},{7,3},{8,12},{12,8},{9,1... | collective-permute-start | bytes 3145736 | tf_op jit(solution)/shard_map/ppermute | solution.py:594
  942.3 63.8 %collective-permute-start.46 = (bf16[512,1024]{0,1:T(8,128)(2,1)}, bf16[512,1024]{0,1:T(8,128)(2,1)}, u32[]{:S(2)}, u32[]{:S(2)}) collective-permute-start(bf16[512,1024]{0,1:T(8,128)(2,1)} %slice.174), channel_id=1, source_target_pairs={{0,4},{4,0},{1,5},{5,1},{2,6},{6,2},{3,7},{7,3},{8,12},{12,8},{9,1... | collective-permute-start | bytes 3145736 | tf_op jit(solution)/shard_map/ppermute | solution.py:594
  (111 other events, 1929.8 us)
Sparse Core Ops, SparseCore 0:
  10.8 55.3 all-gather.4
  68.1 52.6 all-gather.6
  123.3 87.5 all-gather.10
  213.2 87.5 all-gather.8
  505.9 85.6 reduce-scatter.7
  594.8 86.4 reduce-scatter.5
  693.6 93.3 reduce-scatter.3

commit v2 on v1

v2 whole, which is shorter than its diff:
```python
import functools

import jax
import jax.numpy as jnp
from jax import lax
from jax.experimental import pallas as pl
from jax.experimental.pallas import tpu as pltpu
from jax.sharding import Mesh, PartitionSpec as P

HD = 128
ROT = 32
LEN = 1024
EPS_LAYER = 1e-05
EPS_RMS = 1e-06
BF = jnp.bfloat16
F32 = jnp.float32
FINEST = lax.Precision.HIGHEST
LOG2E = 1.4426950408889634
SCALE = HD**-0.5
VMEM_CAP = 56 * 1024 * 1024
ALL = ("row", "zh", "zl", "core")

NN = (((1,), (0,)), ((), ()))
NT = (((1,), (1,)), ((), ()))
TN = (((0,), (0,)), ((), ()))


def dot(a, b, dims, precision=None):
    return lax.dot_general(a, b, dims, precision=precision, preferred_element_type=F32)


def params():
    return pltpu.CompilerParams(vmem_limit_bytes=VMEM_CAP)


def cost(flops, arrays, extra=0):
    moved = sum(int(a.size) * a.dtype.itemsize for a in arrays)
    return pl.CostEstimate(flops=int(flops), bytes_accessed=int(moved), transcendentals=int(extra))


def sds(shape, dtype):
    return jax.ShapeDtypeStruct(shape, dtype)


def mix_stream(stack_ref, coeffs, s, rows):
    total = None
    for j in range(8):
        term = coeffs[:, 8 * s + j : 8 * s + j + 1] * stack_ref[j, rows, :].astype(F32)
        total = term if total is None else total + term
    return total


def centre(values):
    centred = values - jnp.mean(values, axis=-1, keepdims=True)
    spread = jnp.mean(centred * centred, axis=-1, keepdims=True)
    return centred, lax.rsqrt(spread + EPS_LAYER)


def front_kernel(stack_ref, mix_ref, gain_ref, bias_ref, first_ref, rest_ref, res_ref):
    chunk = 16

    def step(i, carry):
        rows = pl.ds(pl.multiple_of(i * chunk, chunk), chunk)
        coeffs = mix_ref[rows, :]
        for s in range(3):
            centred, rstd = centre(mix_stream(stack_ref, coeffs, s, rows))
            normed = centred * rstd * gain_ref[s : s + 1, :] + bias_ref[s : s + 1, :]
            if s == 0:
                first_ref[0, rows, :] = normed.astype(BF)
            else:
                rest_ref[s - 1, rows, :] = normed.astype(BF)
        res_ref[rows, :] = mix_stream(stack_ref, coeffs, 3, rows)
        return carry

    lax.fori_loop(0, stack_ref.shape[1] // chunk, step, 0)


def front(stack, mix, gain, bias):
    n_in, tokens, width = stack.shape
    tile = 32
    row_block = lambda i: (i, 0)
    outs = [sds((n, tokens, width), BF) for n in (1, 2)] + [sds((tokens, width), F32)]
    return pl.pallas_call(
        front_kernel,
        grid=(tokens // tile,),
        in_specs=[
            pl.BlockSpec((n_in, tile, width), lambda i: (0, i, 0)),
            pl.BlockSpec((tile, mix.shape[1]), row_block),
            pl.BlockSpec(gain.shape, lambda i: (0, 0)),
            pl.BlockSpec(bias.shape, lambda i: (0, 0)),
        ],
        out_specs=[
            pl.BlockSpec((1, tile, width), lambda i: (0, i, 0)),
            pl.BlockSpec((2, tile, width), lambda i: (0, i, 0)),
            pl.BlockSpec((tile, width), row_block),
        ],
        out_shape=outs,
        compiler_params=params(),
        cost_estimate=cost(70 * tokens * width, [stack, *outs]),
        name="front",
    )(stack, mix, gain, bias)


def norm_back_kernel(streams, pieces, *refs):
    parts = refs[:pieces]
    stack_ref, mix_ref, gain_ref, grad_ref, sums_ref = refs[pieces:]
    chunk = 16
    width = grad_ref.shape[2]

    @pl.when(pl.program_id(0) == 0)
    def _():
        sums_ref[...] = jnp.zeros_like(sums_ref)

    def step(i, carry):
        rows = pl.ds(pl.multiple_of(i * chunk, chunk), chunk)
        coeffs = mix_ref[rows, :]
        for n, s in enumerate(streams):
            centred, rstd = centre(mix_stream(stack_ref, coeffs, s, rows))
            hat = centred * rstd
            grad = None
            for part in parts:
                term = (part[n, 0, rows, :] if len(part.shape) == 4 else part[n, rows, :]).astype(
                    F32
                )
                grad = term if grad is None else grad + term
            grad = grad.astype(BF).astype(F32)
            sums_ref[n, 0:8, :] += jnp.sum((grad * hat).reshape(chunk // 8, 8, width), axis=0)
            sums_ref[n, 8:16, :] += jnp.sum(grad.reshape(chunk // 8, 8, width), axis=0)
            scaled = grad * gain_ref[s : s + 1, :]
            grad_ref[n, rows, :] = rstd * (
                scaled
                - jnp.mean(scaled, axis=-1, keepdims=True)
                - hat * jnp.mean(scaled * hat, axis=-1, keepdims=True)
            )
        return carry

    lax.fori_loop(0, grad_ref.shape[1] // chunk, step, 0)


def norm_back(streams, parts, stack, mix, gain):
    n_in, tokens, width = stack.shape
    count = len(streams)
    tile = 32
    row_block = lambda i: (i, 0)
    outs = [sds((count, tokens, width), F32), sds((count, 16, width), F32)]
    specs = [
        pl.BlockSpec((count, 1, tile, width), lambda i: (0, 0, i, 0))
        if len(p.shape) == 4
        else pl.BlockSpec((count, tile, width), lambda i: (0, i, 0))
        for p in parts
    ]
    return pl.pallas_call(
        functools.partial(norm_back_kernel, streams, len(parts)),
        grid=(tokens // tile,),
        in_specs=specs
        + [
            pl.BlockSpec((n_in, tile, width), lambda i: (0, i, 0)),
            pl.BlockSpec((tile, mix.shape[1]), row_block),
            pl.BlockSpec(gain.shape, lambda i: (0, 0)),
        ],
        out_specs=[
            pl.BlockSpec((count, tile, width), lambda i: (0, i, 0)),
            pl.BlockSpec((count, 16, width), lambda i: (0, 0, 0)),
        ],
        out_shape=outs,
        compiler_params=params(),
        cost_estimate=cost(40 * count * tokens * width, [stack, *parts, *outs]),
        name="norm_back",
    )(*parts, stack, mix, gain)


def stack_back_kernel(*refs):
    first_ref, rest_ref, last_ref = refs[:3]
    grads = [first_ref.at[0], rest_ref.at[0], rest_ref.at[1], last_ref]
    stack_ref, mix_ref, stack_out, coeff_out = refs[3:]
    chunk = 8

    def step(i, carry):
        rows = pl.ds(pl.multiple_of(i * 2 * chunk, 2 * chunk), 2 * chunk)
        for part in range(2):
            own = pl.ds(pl.multiple_of(i * 2 * chunk + part * chunk, chunk), chunk)
            coeffs = mix_ref[own, :]
            lanes = lax.broadcasted_iota(jnp.int32, coeffs.shape, 1)
            gathered = jnp.zeros(coeffs.shape, F32)
            for j in range(8):
                given = stack_ref[j, rows, :].astype(F32)[part * chunk : (part + 1) * chunk]
                total = None
                for s in range(4):
                    grad = grads[s][own, :]
                    term = coeffs[:, 8 * s + j : 8 * s + j + 1] * grad
                    total = term if total is None else total + term
                    inner = jnp.sum(grad * given, axis=-1, keepdims=True)
                    gathered = jnp.where(lanes == 8 * s + j, inner, gathered)
                stack_out[j, own, :] = total
            coeff_out[own, :] = gathered
        return carry

    lax.fori_loop(0, coeff_out.shape[0] // (2 * chunk), step, 0)


def stack_back(grads, stack, mix):
    n_in, tokens, width = stack.shape
    tile = 32
    row_block = lambda i: (i, 0)
    outs = [sds(stack.shape, F32), sds(mix.shape, F32)]
    return pl.pallas_call(
        stack_back_kernel,
        grid=(tokens // tile,),
        in_specs=[
            pl.BlockSpec((1, tile, width), lambda i: (0, i, 0)),
            pl.BlockSpec((2, tile, width), lambda i: (0, i, 0)),
            pl.BlockSpec((tile, width), row_block),
        ]
        + [
            pl.BlockSpec((n_in, tile, width), lambda i: (0, i, 0)),
            pl.BlockSpec((tile, mix.shape[1]), row_block),
        ],
        out_specs=[
            pl.BlockSpec((n_in, tile, width), lambda i: (0, i, 0)),
            pl.BlockSpec((tile, mix.shape[1]), row_block),
        ],
        out_shape=outs,
        compiler_params=params(),
        cost_estimate=cost(130 * tokens * width, [stack, *grads, *outs]),
        name="stack_back",
    )(*grads, stack, mix)


def turn(values, cos_table, sine_table):
    lanes = lax.broadcasted_iota(jnp.int32, values.shape, 1)
    half = ROT // 2
    swapped = jnp.where(
        lanes < half, pltpu.roll(values, HD - half, 1), pltpu.roll(values, half, 1)
    )
    return values * cos_table + swapped * sine_table


def qkv_kernel(blocks, halves, first, count, *refs):
    x_refs, weights, biases = refs[:blocks], refs[blocks : blocks + halves], refs[blocks + halves : blocks + 2 * halves]
    cos_ref, sine_ref, out_ref = refs[blocks + 2 * halves :]
    rows = x_refs[0].shape[1]
    cols = weights[0].shape[1]
    step = pl.program_id(0)

    def work(rotary):
        for b, x_ref in enumerate(x_refs):
            here = slice(b * rows, (b + 1) * rows)
            for h in range(halves):
                total = dot(x_ref[0], weights[h][...], NN) + biases[h][0]
                for n in range(cols // HD):
                    values = total[:, n * HD : (n + 1) * HD]
                    if rotary:
                        values = turn(values, cos_ref[here, :], sine_ref[here, :])
                    start = h * cols + n * HD
                    out_ref[0, here, start : start + HD] = values.astype(BF)

    for n in range(count):
        pl.when(step == n)(lambda n=n: work(first + n < 2))


def qkv_proj(x_blocks, weights, first, biases, tables):
    blocks, halves = len(x_blocks), len(weights)
    count, rows, width = x_blocks[0].shape
    cols = biases[0].shape[2]
    tokens = blocks * rows
    out = sds((count, tokens, halves * cols), BF)
    table = pl.BlockSpec((tokens, HD), lambda s: (0, 0))
    return pl.pallas_call(
        functools.partial(qkv_kernel, blocks, halves, first, count),
        grid=(count,),
        in_specs=[pl.BlockSpec((1, rows, width), lambda s: (s, 0, 0))] * blocks
        + [pl.BlockSpec((width, cols), lambda s: (0, first + s))] * halves
        + [pl.BlockSpec((1, 1, cols), lambda s: (first + s, 0, 0))] * halves
        + [table, table],
        out_specs=pl.BlockSpec((1, tokens, halves * cols), lambda s: (s, 0, 0)),
        out_shape=out,
        compiler_params=params(),
        cost_estimate=cost(2 * count * halves * tokens * width * cols, [*x_blocks, out]),
        name="qkv_proj",
    )(*x_blocks, *weights, *biases, *tables)


def proj_kernel(blocks, *refs):
    x_refs, weights, out_ref = refs[:blocks], refs[blocks:-1], refs[-1]
    rows = x_refs[0].shape[0]
    for h, weight_ref in enumerate(weights):
        cols = weight_ref.shape[1]
        for b, x_ref in enumerate(x_refs):
            out_ref[b * rows : (b + 1) * rows, h * cols : (h + 1) * cols] = dot(
                x_ref[...], weight_ref[...], NN
            ).astype(BF)


def proj(x_blocks, weights, part, cols):
    blocks, halves = len(x_blocks), len(weights)
    rows, width = x_blocks[0].shape
    out = sds((blocks * rows, halves * cols), BF)
    whole = lambda a: pl.BlockSpec(a.shape, lambda i: (0, 0))
    return pl.pallas_call(
        functools.partial(proj_kernel, blocks),
        grid=(1,),
        in_specs=[whole(x) for x in x_blocks]
        + [pl.BlockSpec((width, cols), lambda i: (0, part))] * halves,
        out_specs=whole(out),
        out_shape=out,
        compiler_params=params(),
        cost_estimate=cost(2 * halves * blocks * rows * width * cols, [*x_blocks, out]),
        name="proj",
    )(*x_blocks, *weights)


def put_blocks(outs, block, values):
    outs[block % 2][0, block // 2] = values


def unproj_kernel(a_ref, *refs):
    weights, outs = refs[:-2], refs[-2:]
    _, pairs, rows, _ = outs[0].shape
    for b in range(2 * pairs):
        here = slice(b * rows, (b + 1) * rows)
        total = None
        for h, weight_ref in enumerate(weights):
            cols = weight_ref.shape[1]
            term = dot(a_ref[0, here, h * cols : (h + 1) * cols], weight_ref[...], NT)
            total = term if total is None else total + term
        put_blocks(outs, b, total.astype(BF))


def unproj(part, first, count, weights, place, blocks):
    halves = len(weights)
    _, tokens, cols = part.shape
    width = weights[0].shape[0]
    tile = 512
    rows = tokens // blocks
    outs = [sds((count, blocks // 2, rows, width), BF)] * 2
    return pl.pallas_call(
        unproj_kernel,
        grid=(count, width // tile),
        in_specs=[pl.BlockSpec((1, tokens, cols), lambda s, i: (first + s, 0, 0))]
        + [pl.BlockSpec((tile, cols // halves), lambda s, i: (i, place + s))] * halves,
        out_specs=[pl.BlockSpec((1, blocks // 2, rows, tile), lambda s, i: (s, 0, 0, i))] * 2,
        out_shape=outs,
        compiler_params=params(),
        cost_estimate=cost(2 * count * tokens * cols * width, outs),
        name="unproj",
    )(part, *weights)


def masked_scores(scalars, keys, query, block, blocks):
    rows = query.shape[0]
    raw = dot(keys, query, NT)
    lanes = lax.broadcasted_iota(jnp.int32, (1, rows), 1)
    limit = jnp.maximum(lanes + scalars[block], scalars[blocks] - 1)
    places = lax.broadcasted_iota(jnp.int32, (rows, rows), 0)
    kept = []
    for b in range(blocks):
        allowed = places <= limit - scalars[b]
        kept.append(jnp.where(allowed, raw[b * rows : (b + 1) * rows, :], -1e30))
    return jnp.concatenate(kept, axis=0)


def attend_kernel(blocks, scalars, query_ref, kv_ref, out_ref, log_ref):
    q_ref, k_ref, v_ref = query_ref.at[0], kv_ref.at[0], kv_ref.at[1]
    rows = q_ref.shape[0] // blocks
    factor = SCALE * LOG2E
    for b in range(blocks):
        here = slice(b * rows, (b + 1) * rows)
        scores = masked_scores(scalars, k_ref[...], q_ref[here, :], b, blocks)
        top = jnp.max(scores, axis=0, keepdims=True)
        probs = jnp.exp2((scores - top) * factor)
        total = jnp.sum(probs, axis=0, keepdims=True)
        mixed = dot(v_ref[...], probs.astype(BF), TN) / total
        out_ref[0, here, :] = mixed.T.astype(BF)
        log_ref[0, :, here] = top * factor + jnp.log2(total)


def attend(scalars, query, kv, blocks):
    _, tokens, cols = kv.shape
    heads = cols // HD
    outs = [sds((1, tokens, cols), BF), sds((heads, 1, tokens), F32)]
    return pl.pallas_call(
        functools.partial(attend_kernel, blocks),
        grid=(heads,),
        in_specs=[
            pl.BlockSpec(memory_space=pltpu.SMEM),
            pl.BlockSpec((1, tokens, HD), lambda h: (0, 0, h)),
            pl.BlockSpec((2, tokens, HD), lambda h: (0, 0, h)),
        ],
        out_specs=[
            pl.BlockSpec((1, tokens, HD), lambda h: (0, 0, h)),
            pl.BlockSpec((1, 1, tokens), lambda h: (h, 0, 0)),
        ],
        out_shape=outs,
        compiler_params=params(),
        cost_estimate=cost(8 * heads * tokens * tokens * HD, [query, kv, *outs]),
        name="attend",
    )(scalars, query, kv)


def attend_back_kernel(
    blocks, scalars, query_ref, kv_ref, g_ref, log_ref, cos_ref, sine_ref, grad_ref, sums_ref,
    key_acc, value_acc,
):
    q_ref, k_ref, v_ref = query_ref.at[0], kv_ref.at[0], kv_ref.at[1]
    rows = q_ref.shape[0] // blocks
    factor = SCALE * LOG2E
    sums = []
    query_sum = jnp.zeros((1, HD), F32)
    for b in range(blocks):
        here = slice(b * rows, (b + 1) * rows)
        query, grad = q_ref[here, :], g_ref[here, :]
        scores = masked_scores(scalars, k_ref[...], query, b, blocks)
        probs = jnp.exp2(scores * factor - log_ref[0, :, here])
        grad_probs = dot(v_ref[...], grad, NT)
        inner = jnp.sum(probs * grad_probs, axis=0, keepdims=True)
        grad_scores = (probs * (grad_probs - inner)).astype(BF)
        key_term = dot(grad_scores, query, NN)
        value_term = dot(probs.astype(BF), grad, NN)
        if b == 0:
            key_acc[...] = key_term
            value_acc[...] = value_term
        else:
            key_acc[...] += key_term
            value_acc[...] += value_term
        grad_query = dot(k_ref[...], grad_scores, TN).T * SCALE
        low = turn(grad_query, cos_ref[here, :], -sine_ref[here, :]).astype(BF)
        grad_ref[0, here, :] = low
        query_sum = query_sum + jnp.sum(low.astype(F32), axis=0, keepdims=True)
    low_key = turn(key_acc[...] * SCALE, cos_ref[...], -sine_ref[...]).astype(BF)
    grad_ref[1] = low_key
    low_value = value_acc[...].astype(BF)
    grad_ref[2] = low_value
    sums_ref[0, 0:1, :] = query_sum
    sums_ref[0, 1:2, :] = jnp.sum(low_key.astype(F32), axis=0, keepdims=True)
    sums_ref[0, 2:3, :] = jnp.sum(low_value.astype(F32), axis=0, keepdims=True)


def attend_back(scalars, query, kv, grad, log_total, tables, blocks):
    _, tokens, cols = kv.shape
    heads = cols // HD
    stacked = pl.BlockSpec((3, tokens, HD), lambda h: (0, 0, h))
    fixed = pl.BlockSpec((tokens, HD), lambda h: (0, 0))
    outs = [sds((3, tokens, cols), BF), sds((heads, 8, HD), F32)]
    return pl.pallas_call(
        functools.partial(attend_back_kernel, blocks),
        grid=(heads,),
        in_specs=[
            pl.BlockSpec(memory_space=pltpu.SMEM),
            pl.BlockSpec((1, tokens, HD), lambda h: (0, 0, h)),
            pl.BlockSpec((2, tokens, HD), lambda h: (0, 0, h)),
            pl.BlockSpec((tokens, HD), lambda h: (0, h)),
            pl.BlockSpec((1, 1, tokens), lambda h: (h, 0, 0)),
            fixed,
            fixed,
        ],
        out_specs=[stacked, pl.BlockSpec((1, 8, HD), lambda h: (h, 0, 0))],
        out_shape=outs,
        scratch_shapes=[pltpu.VMEM((tokens, HD), F32)] * 2,
        compiler_params=params(),
        cost_estimate=cost(16 * heads * tokens * tokens * HD, [query, kv, grad, *outs]),
        name="attend_back",
    )(scalars, query, kv, grad, log_total, *tables)


def total_of(refs, rows=slice(None)):
    total = None
    for ref in refs:
        term = (ref[0, 0, rows, :] if len(ref.shape) == 4 else ref[0, rows, :]).astype(F32)
        total = term if total is None else total + term
    return total


def term_spec(term, tile):
    width = term.shape[-1]
    if len(term.shape) == 4:
        return pl.BlockSpec((1, 1, tile, width), lambda i: (0, 0, i, 0))
    return pl.BlockSpec((1, tile, width), lambda i: (0, i, 0))


def middle_kernel(pieces, *refs):
    parts = refs[:pieces]
    res_ref, out_bias_ref, gain_ref, bias_ref, hid_ref, norm_ref = refs[pieces:]
    attn = (total_of(parts) + out_bias_ref[...]).astype(BF)
    hidden = res_ref[...] + attn.astype(F32)
    hid_ref[...] = hidden
    centred, rstd = centre(hidden)
    norm_ref[...] = (centred * rstd * gain_ref[3:4, :] + bias_ref[3:4, :]).astype(BF)


def middle(parts, residual, out_bias, gain, bias):
    tokens, width = residual.shape
    tile = 64
    block = pl.BlockSpec((tile, width), lambda i: (i, 0))
    whole = lambda a: pl.BlockSpec(a.shape, lambda i: (0, 0))
    outs = [sds((tokens, width), F32), sds((tokens, width), BF)]
    return pl.pallas_call(
        functools.partial(middle_kernel, len(parts)),
        grid=(tokens // tile,),
        in_specs=[term_spec(p, tile) for p in parts] + [block, whole(out_bias), whole(gain), whole(bias)],
        out_specs=[block] * 2,
        out_shape=outs,
        compiler_params=params(),
        cost_estimate=cost(20 * tokens * width, [*parts, residual, *outs]),
        name="middle",
    )(*parts, residual, out_bias, gain, bias)


def middle_back_kernel(pieces, *refs):
    parts = refs[:pieces]
    hid_ref, layer_ref, gain_ref = refs[pieces : pieces + 3]
    grad_ref, low_ref, sums_ref = refs[pieces + 3 :]
    grad = total_of(parts).astype(BF).astype(F32)
    centred, rstd = centre(hid_ref[...])
    hat = centred * rstd
    scaled = grad * gain_ref[3:4, :]
    grad_hidden = layer_ref[...] + rstd * (
        scaled
        - jnp.mean(scaled, axis=-1, keepdims=True)
        - hat * jnp.mean(scaled * hat, axis=-1, keepdims=True)
    )
    grad_ref[...] = grad_hidden
    low = grad_hidden.astype(BF)
    low_ref[...] = low

    @pl.when(pl.program_id(0) == 0)
    def _():
        sums_ref[...] = jnp.zeros_like(sums_ref)

    sums_ref[0:1, :] += jnp.sum(grad * hat, axis=0, keepdims=True)
    sums_ref[1:2, :] += jnp.sum(grad, axis=0, keepdims=True)
    sums_ref[2:3, :] += jnp.sum(low.astype(F32), axis=0, keepdims=True)


def middle_back(parts, hidden, grad_layer, gain):
    tokens, width = hidden.shape
    tile = 64
    block = pl.BlockSpec((tile, width), lambda i: (i, 0))
    outs = [sds((tokens, width), F32), sds((tokens, width), BF), sds((8, width), F32)]
    return pl.pallas_call(
        functools.partial(middle_back_kernel, len(parts)),
        grid=(tokens // tile,),
        in_specs=[term_spec(p, tile) for p in parts] + [block] * 2 + [pl.BlockSpec(gain.shape, lambda i: (0, 0))],
        out_specs=[block] * 2 + [pl.BlockSpec((8, width), lambda i: (0, 0))],
        out_shape=outs,
        compiler_params=params(),
        cost_estimate=cost(30 * tokens * width, [*parts, hidden, grad_layer, *outs]),
        name="middle_back",
    )(*parts, hidden, grad_layer, gain)


def gelu_pair(values):
    tail = 0.5 * (1.0 + lax.erf(values * (0.5**0.5)))
    slope = tail + values * jnp.exp2(values * values * (-0.5 * LOG2E)) * 0.3989422804014327
    return values * tail, slope


def expand_block(x_refs, weight_ref, extra_ref, back, act_ref, second_ref, columns, act_columns):
    rows = x_refs[0].shape[0]
    total = None
    for b, x_ref in enumerate(x_refs):
        here = slice(b * rows, (b + 1) * rows)
        up = dot(x_ref[...], weight_ref[...], NN)
        if back:
            low = (up * extra_ref[here, columns].astype(F32)).astype(BF)
            part = jnp.sum(low.astype(F32), axis=0, keepdims=True)
            total = part if total is None else total + part
        else:
            act, slope = gelu_pair(up + extra_ref[...])
            low = act.astype(BF)
            second_ref[here, columns] = slope.astype(BF)
        act_ref[here, act_columns] = low
    if back:
        second_ref[...] = total


def expand_kernel(blocks, *refs):
    x_refs = refs[:blocks]
    weight_ref, bias_ref, act_ref, slope_ref = refs[blocks:]
    every = slice(None)
    expand_block(x_refs, weight_ref, bias_ref, False, act_ref, slope_ref, every, every)


def expand(x_blocks, weight, bias):
    blocks = len(x_blocks)
    rows, width = x_blocks[0].shape
    tokens = blocks * rows
    hidden = bias.shape[1]
    tile = 256
    whole = pl.BlockSpec((rows, width), lambda i: (0, 0))
    column = pl.BlockSpec((tokens, tile), lambda i: (0, i))
    outs = [sds((tokens, hidden), BF)] * 2
    return pl.pallas_call(
        functools.partial(expand_kernel, blocks),
        grid=(hidden // tile,),
        in_specs=[whole] * blocks
        + [
            pl.BlockSpec((width, tile), lambda i: (0, i)),
            pl.BlockSpec((1, tile), lambda i: (0, i)),
        ],
        out_specs=[column] * 2,
        out_shape=outs,
        compiler_params=params(),
        cost_estimate=cost(2 * tokens * width * hidden, [*x_blocks, *outs]),
        name="expand",
    )(*x_blocks, weight, bias)


def feed_kernel(blocks, ready, steps, tile, back, *refs):
    halves = len(steps)
    x_refs = refs[:blocks]
    refs = refs[blocks:]
    done_refs, refs = refs[:ready], refs[ready:]
    n_new = halves - ready
    first_refs, refs = refs[:n_new], refs[n_new:]
    extra_refs, refs = refs[:n_new], refs[n_new:]
    second_refs, refs = refs[:halves], refs[halves:]
    act_refs, refs = refs[:n_new], refs[n_new:]
    other_refs, refs = refs[:n_new], refs[n_new:]
    outs, held = refs[:2], refs[2]
    step = pl.program_id(0)
    hidden = held.shape[1] // max(n_new, 1)
    per = hidden // tile
    every = slice(None)
    for n in range(n_new):
        for i in range(per):

            @pl.when(step == n * per + i)
            def _():
                columns = slice(i * tile, (i + 1) * tile)
                expand_block(
                    x_refs, first_refs[n], extra_refs[n], back, act_refs[n], other_refs[n],
                    every, every,
                )
                held[:, n * hidden + i * tile : n * hidden + (i + 1) * tile] = act_refs[n][...]

    @pl.when(step >= n_new * per)
    def _():
        _, pairs, rows, _ = outs[0].shape
        for b in range(2 * pairs):
            here = slice(b * rows, (b + 1) * rows)
            total = None
            for h in range(halves):
                if h < ready:
                    a = done_refs[h][here, :]
                else:
                    a = held[here, (h - ready) * hidden : (h - ready + 1) * hidden]
                term = dot(a, second_refs[h][...], NT)
                total = term if total is None else total + term
            put_blocks(outs, b, total.astype(BF))


def feed(x_blocks, done, weights, first_part, extras, back):
    blocks, halves, ready = len(x_blocks), len(weights), len(done)
    rows, width = x_blocks[0].shape
    tokens = blocks * rows
    n_new = halves - ready
    hidden = weights[0].shape[1] // 2
    tile, out_tile = 256, 512
    per = hidden // tile
    grid = n_new * per + width // out_tile
    second_part = 1 - first_part
    whole = lambda a: pl.BlockSpec(a.shape, lambda i: (0, 0))
    within = lambda i, n: jnp.clip(i - n * per, 0, per - 1)
    late = lambda i: jnp.maximum(i - n_new * per, 0)
    first_specs, extra_specs, act_specs, other_specs = [], [], [], []
    for n in range(n_new):
        column = pl.BlockSpec((tokens, tile), lambda i, n=n: (0, within(i, n)))
        line = pl.BlockSpec((1, tile), lambda i, n=n: (0, within(i, n)))
        first_specs.append(
            pl.BlockSpec((width, tile), lambda i, n=n: (0, first_part * per + within(i, n)))
        )
        extra_specs.append(column if back else line)
        act_specs.append(column)
        other_specs.append(line if back else column)
    outs = (
        [sds((tokens, hidden), BF)] * n_new
        + [sds((1, hidden), F32) if back else sds((tokens, hidden), BF)] * n_new
        + [sds((1, blocks // 2, rows, width), BF)] * 2
    )
    found = pl.pallas_call(
        functools.partial(feed_kernel, blocks, ready, [per] * halves, tile, back),
        grid=(grid,),
        in_specs=[whole(x) for x in x_blocks]
        + [whole(d) for d in done]
        + first_specs
        + extra_specs
        + [pl.BlockSpec((out_tile, hidden), lambda i: (late(i), second_part))] * halves,
        out_specs=act_specs
        + other_specs
        + [pl.BlockSpec((1, blocks // 2, rows, out_tile), lambda i: (0, 0, 0, late(i)))] * 2,
        out_shape=outs,
        scratch_shapes=[pltpu.VMEM((tokens, n_new * hidden), BF)],
        compiler_params=params(),
        cost_estimate=cost(2 * tokens * width * hidden * (n_new + halves), [*x_blocks, *outs]),
        name="feed_back" if back else "feed",
    )(*x_blocks, *done, *weights[ready:], *extras, *weights)
    return found[:n_new], found[n_new : 2 * n_new], found[2 * n_new :]


def weight_grad_kernel(blocks, *refs):
    left = jnp.concatenate([r[...] for r in refs[:blocks]], axis=0)
    out_ref = refs[-1]
    start = 0
    for right in refs[blocks:-1]:
        cols = right.shape[1]
        out_ref[:, start : start + cols] = dot(left, right[...], TN).astype(BF)
        start += cols


def weight_grad(lefts, rights):
    rows, width = lefts[0].shape
    tile = 512
    out = sds((width, sum(r.shape[1] for r in rights)), BF)
    return pl.pallas_call(
        functools.partial(weight_grad_kernel, len(lefts)),
        grid=(width // tile,),
        in_specs=[pl.BlockSpec((rows, tile), lambda i: (0, i))] * len(lefts)
        + [pl.BlockSpec(r.shape, lambda i: (0, 0)) for r in rights],
        out_specs=pl.BlockSpec((tile, out.shape[1]), lambda i: (i, 0)),
        out_shape=out,
        compiler_params=params(),
        cost_estimate=cost(
            2 * rows * len(lefts) * width * out.shape[1], [*rights, *lefts, out]
        ),
        name="weight_grad",
    )(*lefts, *rights)


def piece_places(order, pieces):
    places = []
    for k in range(pieces):
        place = 0
        for bit in order:
            place = 2 * place + ((k >> bit) & 1)
        places.append(place)
    return places


def piece_grad_kernel(blocks, halves, table, *refs):
    firsts, rests, attn = (refs[n * blocks : (n + 1) * blocks] for n in range(3))
    grad_ref, head_ref = refs[3 * blocks : 3 * blocks + 2]
    outs = refs[3 * blocks + 2 :]
    cols = head_ref.shape[2] // halves
    for group in range(4):
        if group == 0:
            left = [r[0] for r in firsts]
        elif group < 3:
            left = [r[group - 1] for r in rests]
        else:
            left = [r[...] for r in attn]
        right = grad_ref[group] if group < 3 else head_ref[0]
        grad = dot(jnp.concatenate(left, axis=0), right, TN).astype(BF)
        first = (group % 2) * cols
        for h in range(halves):
            outs[(group // 2) * halves + h][:, first : first + cols] = grad[
                :, h * cols : (h + 1) * cols
            ]


def piece_grad(rank, pieces, orders, firsts, rests, grads, attn, head, halves):
    blocks = len(firsts)
    _, rows, width = firsts[0].shape
    cols = head.shape[2] // halves
    feats = width // pieces
    table = jnp.concatenate(
        [
            jnp.arange(pieces, dtype=jnp.int32)[None] ^ rank,
            jnp.array([piece_places(order, pieces) for order in orders], jnp.int32),
        ],
        axis=0,
    )
    outs = [sds((width, 2 * cols), BF)] * (2 * halves)
    found = pl.pallas_call(
        functools.partial(piece_grad_kernel, blocks, halves),
        grid_spec=pltpu.PrefetchScalarGridSpec(
            num_scalar_prefetch=1,
            grid=(pieces,),
            in_specs=[pl.BlockSpec((1, rows, feats), lambda i, t: (0, 0, t[0, i]))] * blocks
            + [pl.BlockSpec((2, rows, feats), lambda i, t: (0, 0, t[0, i]))] * blocks
            + [pl.BlockSpec((rows, feats), lambda i, t: (0, t[0, i]))] * blocks
            + [pl.BlockSpec(grads.shape, lambda i, t: (0, 0, 0))]
            + [pl.BlockSpec(head.shape, lambda i, t: (0, 0, 0))],
            out_specs=[
                pl.BlockSpec((feats, 2 * cols), lambda i, t, p=p: (t[p + 1, i], 0))
                for p in range(2)
                for _ in range(halves)
            ],
        ),
        out_shape=outs,
        compiler_params=params(),
        cost_estimate=cost(
            8 * rows * blocks * width * cols * halves, [*firsts, *rests, grads, *attn, head, *outs]
        ),
        name="piece_grad",
    )(table, *firsts, *rests, *attn, grads, head)
    return [found[p * halves : (p + 1) * halves] for p in range(2)]


def mixing_kernel(pieces, *refs):
    parts = refs[:pieces]
    hid_ref, down_bias_ref, gain_ref, in_ref, out_w_ref, og_ref, cg_ref = refs[
        pieces : pieces + 7
    ]
    layer_ref, coeff_ref, grad_ref, low_ref, sums_ref, in_grad_ref, out_grad_ref = refs[
        pieces + 7 :
    ]
    down = (total_of(parts) + down_bias_ref[...]).astype(BF)
    layer = hid_ref[...] + down.astype(F32)
    layer_ref[...] = layer
    rms = lax.rsqrt(jnp.mean(layer * layer, axis=-1, keepdims=True) + EPS_RMS)
    unit = layer * rms
    gain = gain_ref[...]
    scaled = unit * gain
    act, slope = gelu_pair(dot(scaled, in_ref[...], NN, FINEST))
    coeff_ref[...] = dot(act, out_w_ref[...], NN, FINEST)
    coeff_grad = cg_ref[...]
    grad_pre = dot(coeff_grad, out_w_ref[...], NT, FINEST) * slope
    grad_scaled = dot(grad_pre, in_ref[...], NT, FINEST)
    grad_unit = grad_scaled * gain
    grad_layer = (
        rms * (grad_unit - unit * jnp.mean(grad_unit * unit, axis=-1, keepdims=True))
        + og_ref[...].astype(F32)
    )
    grad_ref[...] = grad_layer
    low = grad_layer.astype(BF)
    low_ref[...] = low

    @pl.when(pl.program_id(0) == 0)
    def _():
        sums_ref[...] = jnp.zeros_like(sums_ref)
        in_grad_ref[...] = jnp.zeros_like(in_grad_ref)
        out_grad_ref[...] = jnp.zeros_like(out_grad_ref)

    sums_ref[0:1, :] += jnp.sum(low.astype(F32), axis=0, keepdims=True)
    sums_ref[1:2, :] += jnp.sum(grad_scaled * unit, axis=0, keepdims=True)
    in_grad_ref[...] += dot(grad_pre, scaled, TN, FINEST)
    out_grad_ref[...] += dot(act, coeff_grad, TN, FINEST)


def mixing(parts, hidden, down_bias, gain, mix_in, mix_out, out_grad, coeff_grad):
    tokens, width = hidden.shape
    tile = 128
    block = pl.BlockSpec((tile, width), lambda i: (i, 0))
    whole = lambda a: pl.BlockSpec(a.shape, lambda i: (0, 0))
    narrow = pl.BlockSpec((tile, coeff_grad.shape[1]), lambda i: (i, 0))
    outs = [
        sds((tokens, width), F32),
        sds(coeff_grad.shape, F32),
        sds((tokens, width), F32),
        sds((tokens, width), BF),
        sds((8, width), F32),
        sds((mix_in.shape[1], width), F32),
        sds(mix_out.shape, F32),
    ]
    return pl.pallas_call(
        functools.partial(mixing_kernel, len(parts)),
        grid=(tokens // tile,),
        in_specs=[term_spec(p, tile) for p in parts]
        + [block]
        + [whole(a) for a in (down_bias, gain, mix_in, mix_out)]
        + [block, narrow],
        out_specs=[block, narrow, block, block] + [whole(a) for a in outs[4:]],
        out_shape=outs,
        compiler_params=params(),
        cost_estimate=cost(3000 * tokens * width, [*parts, hidden, out_grad, *outs]),
        name="mixing",
    )(*parts, hidden, down_bias, gain, mix_in, mix_out, out_grad, coeff_grad)


def swap(values, axis, bits):
    size = lax.axis_size(axis)
    return lax.ppermute(values, axis, [(i, i ^ bits) for i in range(size)])


def send_tokens(values):
    return swap(values, "core", 1), [
        swap(values, "zl", k) for k in range(1, lax.axis_size("zl"))
    ]


def token_blocks(values, beside, arrived):
    blocks = [values, beside]
    for part in arrived:
        blocks += [part, swap(part, "core", 1)]
    return blocks


def chip_sums(own, theirs):
    got = swap(theirs, "core", 1)
    sums = [
        (own[:, k].astype(F32) + got[:, k].astype(F32)).astype(BF)
        for k in range(1, own.shape[1])
    ]
    return [own, got], sums


def send_sums(sums):
    return [swap(part, "zl", k + 1) for k, part in enumerate(sums)]


def together(first, second):
    both = lax.optimization_barrier((*first, *second))
    return list(both[: len(first)]), list(both[len(first) :])


def halves_of(values):
    return [values] + [swap(values, "zh", h) for h in range(1, lax.axis_size("zh"))]


def tree(terms):
    while len(terms) > 1:
        terms = [a + b for a, b in zip(terms[::2], terms[1::2])]
    return terms[0]


def sum_parts(values, axes):
    size = lax.axis_size(axes)
    return [values] + [
        lax.ppermute(values, axes, [(i, i ^ k) for i in range(size)]) for k in range(1, size)
    ]


def exchange_orders():
    bits = list(range(lax.axis_size("row").bit_length() - 1))
    return [bits, bits[1:] + bits[:1]]


def gather_pieces(values, order):
    held = {0: values}
    for bit in order:
        for k in list(held):
            held[k ^ (1 << bit)] = swap(held[k], "row", 1 << bit)
    return [held[k] for k in range(len(held))]


def send_half(values, bit):
    return swap(values[values.shape[0] // 2 :], "row", 1 << bit)


def add_half(values, got):
    return values[: got.shape[0]].astype(F32) + got.astype(F32)


def gather_weight(values):
    return lax.all_gather(values, "row", axis=0, tiled=True)


def scatter_rows(grad):
    return lax.psum_scatter(grad, "row", scatter_dimension=0, tiled=True)


def other_halves(mine, halves):
    cols = mine.shape[1] // halves
    return [swap(mine[:, h * cols : (h + 1) * cols], "zh", h) for h in range(1, halves)]


def total_grad(mine, others):
    total = mine.astype(F32)
    for other in others:
        total = total + other.astype(F32)
    return total


def after(values, *earlier):
    return lax.optimization_barrier((values, *earlier))


def on_device(
    layer_stack, mix_coeffs, prefix, ln_gain, ln_bias, qkv_weight, qkv_bias, out_weight,
    out_bias, up_weight, up_bias, down_weight, down_bias, mix_gain, mix_in, mix_out, out_grad,
    coeff_grad,
):
    tokens, width = layer_stack.shape[1:]
    halves = lax.axis_size("zh")
    group = lax.axis_size("zl") * 2
    cols = qkv_bias.shape[1]
    feats = qkv_weight.shape[1]
    place = lax.axis_index("zl") * 2 + lax.axis_index("core")

    attn_local = jnp.concatenate(
        [qkv_weight[s] for s in range(3)] + [out_weight.T], axis=1
    )
    biases = halves_of(jnp.concatenate([qkv_bias.reshape(1, -1), up_bias.reshape(1, -1)], axis=1))
    attn_local, biases[-1] = after(attn_local, biases[-1])
    qkv_biases = [x[:, : 3 * cols].reshape(3, 1, cols) for x in biases]
    up_biases = [x[:, 3 * cols :] for x in biases]
    attn_halves = halves_of(attn_local)
    orders = exchange_orders()
    rank = lax.axis_index("row")
    row_count = lax.axis_size("row")
    offsets = (rank ^ jnp.arange(row_count, dtype=jnp.int32)) * feats
    attn_full = [gather_weight(attn_halves[0])]
    feed_local = jnp.concatenate([up_weight, down_weight.T], axis=1)
    bases = (place ^ jnp.arange(group, dtype=jnp.int32)) * tokens
    prefix_here = lax.dynamic_slice_in_dim(prefix, lax.axis_index("zh"), 1, 0)
    scalars = jnp.concatenate([bases, prefix_here])
    positions = (bases[:, None] + jnp.arange(tokens, dtype=jnp.int32)[None, :]).reshape(-1)
    inv_freq = 10000.0 ** (-(jnp.arange(ROT // 2, dtype=F32) * 2.0) / ROT)
    angles = positions.astype(F32)[:, None] * inv_freq[None, :]
    cos_half, sine_half = jnp.cos(angles), jnp.sin(angles)
    rest = jnp.zeros((positions.shape[0], HD - ROT), F32)
    tables = (
        jnp.concatenate([cos_half, cos_half, rest + 1.0], axis=1),
        jnp.concatenate([-sine_half, sine_half, rest], axis=1),
    )

    mix_flat = mix_coeffs.reshape(tokens, -1)
    query_in, kv_in, residual = front(layer_stack, mix_flat, ln_gain, ln_bias)
    query_beside, query_arrived = send_tokens(query_in)
    kv_beside, kv_arrived = send_tokens(kv_in)
    for h in range(1, halves):
        (attn_halves[h],), query_arrived = together([attn_halves[h]], query_arrived)
        attn_full.append(gather_weight(attn_halves[h]))
    feed_full = [gather_weight(after(feed_local, attn_halves[-1])[0])]
    feed_halves, kv_arrived = together(halves_of(feed_local)[1:], kv_arrived)
    query_all = token_blocks(query_in, query_beside, query_arrived)
    kv_all = token_blocks(kv_in, kv_beside, kv_arrived)
    query = qkv_proj(query_all, attn_full, 0, qkv_biases, tables)
    kv = qkv_proj(kv_all, attn_full, 1, qkv_biases, tables)
    head, log_total = attend(scalars, query, kv, group)
    feed_halves, (head,) = together(feed_halves, [head])
    feed_full += [gather_weight(held) for held in feed_halves]
    terms, sums = chip_sums(*unproj(head, 0, 1, attn_full, 3, group))
    arrived = send_sums(sums)
    hidden, normed2 = middle(
        terms + arrived, residual, out_bias.reshape(1, -1), ln_gain, ln_bias
    )
    normed2_all = token_blocks(normed2, *send_tokens(normed2))
    act, slope = zip(expand(normed2_all, feed_full[0], up_biases[0]))
    new_act, new_slope, (own, theirs) = feed(
        normed2_all, act, feed_full, 0, up_biases[1:], False
    )
    act, slope = [*act, *new_act], [*slope, *new_slope]
    terms, sums = chip_sums(own, theirs)
    layer_out, coeff_out, grad_layer, grad_down, mix_sums, mix_in_part, mix_out_part = mixing(
        terms + send_sums(sums), hidden, down_bias.reshape(1, -1), mix_gain.reshape(1, -1),
        mix_in, mix_out, out_grad, coeff_grad,
    )

    mixed = mix_in_part.shape[0]
    early = jnp.concatenate(
        [
            mix_in_part,
            mix_sums[:2],
            jnp.pad(mix_out_part.reshape(1, -1), ((0, 0), (0, width - mix_out.size))),
        ],
        axis=0,
    )
    rounds = [("core", 1)]
    for axis in ("row", "zl", "zh"):
        rounds += [(axis, 1 << bit) for bit in range(lax.axis_size(axis).bit_length() - 1)]
    beside, arrived = send_tokens(grad_down)
    (got,), (beside,) = together([swap(early, *rounds[0])], [beside])
    early = early + got
    (got,), arrived = together([swap(early, *rounds[1])], arrived)
    early = early + got
    grad_down_all = token_blocks(grad_down, beside, arrived)
    got = swap(early, *rounds[2])
    down_wide = weight_grad(grad_down_all, act)
    got, down_wide, grad_down_all[0] = after(got, down_wide, grad_down_all[0])
    early = early + got
    down_mine = scatter_rows(down_wide)
    got = swap(early, *rounds[3])
    grad_up, up_bias_part, (own, theirs) = feed(grad_down_all, (), feed_full, 1, slope, True)
    got, theirs, late_grad = after(got, theirs, grad_up[0])
    early = early + got
    terms, sums = chip_sums(own, theirs)
    arrived = send_sums(sums)
    got = swap(early, *rounds[4])
    up_wide = weight_grad(normed2_all, (late_grad, *grad_up[1:]))
    (got, up_wide), arrived = together([got, up_wide], arrived)
    early = early + got
    for more in rounds[5:]:
        early = early + swap(early, *more)
    up_mine = scatter_rows(up_wide)
    grad_hidden, grad_attn, mid_sums = middle_back(terms + arrived, hidden, grad_layer, ln_gain)
    grad_attn_all = token_blocks(grad_attn, *send_tokens(grad_attn))
    grad_heads = proj(grad_attn_all, attn_full, 3, cols)
    half_cols = down_mine.shape[1] // halves
    down_parts = [
        [down_mine[:, h * half_cols + n * half_cols // 2 : h * half_cols + (n + 1) * half_cols // 2] for n in range(2)]
        for h in range(halves)
    ]
    crossing = [swap(down_parts[h][0], "zh", h) for h in range(1, halves)]
    grads, bias_sums = attend_back(scalars, query, kv, grad_heads, log_total, tables, group)
    early_parts, (grads,) = together(crossing, [grads])
    crossing = [swap(down_parts[h][1], "zh", h) for h in range(1, halves)]
    kv_terms, kv_sums = chip_sums(*unproj(grads, 1, 2, attn_full, 1, group))
    own, theirs = unproj(grads, 0, 1, attn_full, 0, group)
    late_parts, (own, theirs) = together(crossing, [own, theirs])
    down_others = [
        jnp.concatenate([a, b], axis=1) for a, b in zip(early_parts, late_parts)
    ]
    query_terms, query_sums = chip_sums(own, theirs)
    (late_head, *kv_sums), query_sums = together([head, *kv_sums], query_sums)
    attn_parts = piece_grad(
        rank, row_count, orders, query_all, kv_all, grads, grad_attn_all, late_head, halves
    )
    kv_crossing, query_crossing = send_sums(kv_sums), send_sums(query_sums)
    norm = lambda streams, terms: norm_back(streams, terms, layer_stack, mix_flat, ln_gain)
    near = [attn_parts[p][0] for p in range(2)]
    far = [attn_parts[p][h] for h in range(1, halves) for p in range(2)]
    which = [p for h in range(1, halves) for p in range(2)]
    steps = len(orders[0])
    got = [send_half(v, orders[p][0]) for v, p in zip(far, which)]
    got, (*kv_crossing, near[0], near[1]) = together(got, [*kv_crossing, *near])
    far = [add_half(v, g).astype(BF) for v, g in zip(far, got)]
    got = [send_half(v, orders[p][1]) for v, p in zip(far, which)]
    near_got = [send_half(v, orders[p][0]) for p, v in enumerate(near)]
    kv_grads, kv_sums = norm((1, 2), kv_terms + kv_crossing)
    got, (kv_grads,) = together(got, [kv_grads])
    far = [add_half(v, g).astype(BF) for v, g in zip(far, got)]
    for n in range(2, steps):
        got = [send_half(v, orders[p][n]) for v, p in zip(far, which)]
        far = [add_half(v, g).astype(BF) for v, g in zip(far, got)]
    up_others = other_halves(up_mine, halves)
    query_crossing, near_got = together(query_crossing, near_got)
    near = [add_half(v, g) for v, g in zip(near, near_got)]
    for n in range(1, steps):
        near = [v.astype(BF) for v in near]
        near_got = [send_half(v, orders[p][n]) for p, v in enumerate(near)]
        if n == 1:
            query_grads, query_sums = norm((0,), query_terms + query_crossing)
            near_got, (query_grads, *up_others) = together(near_got, [query_grads, *up_others])
        near = [add_half(v, g) for v, g in zip(near, near_got)]
    stream_grads = (query_grads, kv_grads, grad_hidden)
    sums = [query_sums[0], kv_sums[0], kv_sums[1]]
    attn_others = [swap(v, "zh", n // 2 + 1) for n, v in enumerate(far)]
    mix_in_grad = early[:mixed].T
    down_bias_grad, mix_gain_grad = early[mixed], early[mixed + 1]
    mix_out_grad = early[mixed + 2, : mix_out.size].reshape(mix_out.shape)
    heads = cols // HD
    bias_line = lax.broadcasted_iota(jnp.int32, (halves * group, 1), 0)
    zh = lax.axis_index("zh")
    bias_rows = 0.0
    for h in range(halves):
        here = bias_sums[h * heads : (h + 1) * heads, :3].transpose(1, 0, 2).reshape(1, -1)
        line = jnp.concatenate([here, up_bias_part[h]], axis=1)
        bias_rows = bias_rows + jnp.where(bias_line == (zh ^ h) * group + place, line, 0.0)
    late = jnp.concatenate(
            [
                *[part[0:8].sum(axis=0, keepdims=True) for part in sums],
                mid_sums[0:1],
                *[part[8:16].sum(axis=0, keepdims=True) for part in sums],
                mid_sums[1:3],
                jnp.pad(bias_rows, ((0, 0), (0, width - bias_rows.shape[1]))),
            ],
            axis=0,
    )
    late = tree(sum_parts(late, ("row",)))
    late = tree(sum_parts(late, ("zl", "core")))
    late = sum_parts(late, ("zh",))
    stack_grad, coeffs_grad = stack_back(stream_grads, layer_stack, mix_flat)
    late, (stack_grad, *attn_others) = together(late, [stack_grad, *attn_others])
    late = tree(late)
    half_cols = up_mine.shape[1] // halves
    down_grad = total_grad(down_mine[:, :half_cols], down_others).T
    up_grad = total_grad(up_mine[:, :half_cols], up_others)
    attn_grad = [total_grad(near[p], attn_others[p::2]) for p in range(2)]
    qkv_grad = jnp.stack(
        [attn_grad[0][:, :cols], attn_grad[0][:, cols:], attn_grad[1][:, :cols]], axis=0
    )
    out_w_grad = attn_grad[1][:, cols:].T

    bias_grad = lax.dynamic_slice_in_dim(late, 9 + zh * group + place, 1, 0)
    qkv_bias_grad = bias_grad[0, : 3 * cols].reshape(3, cols)
    up_bias_grad = bias_grad[0, 3 * cols : 3 * cols + up_bias.shape[0]]
    return (
        layer_out,
        coeff_out,
        stack_grad,
        coeffs_grad.reshape(mix_coeffs.shape),
        late[0:4],
        late[4:8],
        qkv_grad,
        qkv_bias_grad,
        out_w_grad,
        late[8],
        up_grad,
        up_bias_grad,
        down_grad,
        down_bias_grad,
        mix_gain_grad,
        mix_in_grad,
        mix_out_grad,
    )


def solution(mesh):
    rows, cols = mesh.shape["row"], mesh.shape["col"]
    col = ("zh", "zl", "core")

    def run(*args):
        seqs = args[2].shape[0] // rows
        fine = Mesh(mesh.devices.reshape(rows, seqs, cols // (2 * seqs), 2), ALL)
        in_specs = (
            P(None, ALL, None),
            P(ALL, None, None),
            P("row"),
            P(),
            P(),
            P(None, "row", col),
            P(None, col),
            P(col, "row"),
            P(),
            P("row", col),
            P(col),
            P(col, "row"),
            P(),
            P(),
            P(),
            P(),
            P(ALL, None),
            P(ALL, None),
        )
        out_specs = (
            P(ALL, None),
            P(ALL, None),
            P(None, ALL, None),
            P(ALL, None, None),
            P(),
            P(),
            P(None, "row", col),
            P(None, col),
            P(col, "row"),
            P(),
            P("row", col),
            P(col),
            P(col, "row"),
            P(),
            P(),
            P(),
            P(),
        )
        return jax.shard_map(
            on_device, mesh=fine, in_specs=in_specs, out_specs=out_specs, check_vma=False
        )(*args)

    return run
```

time: 1030 us -> 839 us (0.81)
  waiting for transfers between devices: 573 us -> 403 us
  matrix products: 41.8 us -> 0 us
  other arithmetic: 25 us -> 47.3 us
  local copies, waits for them, and re-layouts: 40.8 us -> 55.7 us
  Pallas kernels: 272 us -> 259 us
    ppermute x65 -> x46, waiting for transfers between devices: 573 us -> 377 us  [swap(): return lax.ppermute(values, axis, [(i, i ^ bits) for i in range(size)])]
    dot_general x6 -> x0, matrix products: 41.8 us -> none  [dot(): lax.dot_general(a, b, dims, precision=precision, preferred_element_type=F32)]
    convert_element_type x6 -> x11, other arithmetic: 4.78 us -> 22.6 us  [the longest x5 17 us: chip_sums(): (own[:, k].astype(F32) + got[:, k].astype(F32)).astype(BF)]
    ppermute x0 -> x7, waiting for transfers between devices: none -> 16.1 us  [sum_parts(): lax.ppermute(values, axes, [(i, i ^ k) for i in range(size)])]
    ppermute x65 -> x46, starting transfers between devices: 48.5 us -> 40.5 us  [swap(): return lax.ppermute(values, axis, [(i, i ^ bits) for i in range(size)])]
    pallas_call x2 -> x1, Pallas kernels: 20.9 us -> 18.1 us  [attend_back(): pl.pallas_call(functools.partial(attend_back_kernel, blocks), grid=(heads...]
    unnamed x156 -> x103, local copies, waits for them, and re-layouts: 22 us -> 19.3 us
  transfers between devices with their start and end apart: 72 -> 59, of which waited for: 33 -> 33; matrix products, arithmetic and copies ran while one was open for 8% -> 9% of each run, Pallas kernels for 20% -> 27%
where the time goes in v2:
time: 839 us; the launch traced here: 827 us
  waiting for transfers between devices  403 us (48%)
  Pallas kernels  259 us (31%)
  local copies, waits for them, and re-layouts  55.7 us (7%)
  other arithmetic  47.3 us (6%)
  starting transfers between devices  47 us (6%)
  between operations  14.9 us (2%)
    ppermute x46, waiting for transfers between devices, swap(): return lax.ppermute(values, axis, [(i, i ^ bits) for i in range(size)])  377 us
    pallas_call x2, Pallas kernels, feed(): pl.pallas_call(functools.partial(feed_kernel, blocks, ready, [per] * halv...  48.8 us
    ppermute x46, starting transfers between devices, swap(): return lax.ppermute(values, axis, [(i, i ^ bits) for i in range(size)])  40.5 us
    pallas_call x2, Pallas kernels, weight_grad(): pl.pallas_call(functools.partial(weight_grad_kernel, len(lefts)), grid=(w...  27.8 us
    pallas_call x2, Pallas kernels, norm_back(): pl.pallas_call(functools.partial(norm_back_kernel, streams, len(parts)),...  25.6 us
    pallas_call x3, Pallas kernels, unproj(): pl.pallas_call(unproj_kernel, grid=(count, width // tile), in_specs=[pl.B...  22.2 us
    unnamed x103, local copies, waits for them, and re-layouts  19.3 us
    pallas_call x1, Pallas kernels, attend_back(): pl.pallas_call(functools.partial(attend_back_kernel, blocks), grid=(heads...  18.1 us
  transfers between devices with their start and end apart: 59, of which 33 were waited for; matrix products, arithmetic and copies ran while one was open for 9% of the time, Pallas kernels for 27%

profile of v2, /device:TPU:0, one launch (start us, length us, event | category | flops | bytes accessed | tf_op | source)
XLA Modules:
  0.0 826.9 jit_solution(17143032545075650379)
XLA Ops:
  16.9 13.2 %front.1 = (bf16[1,256,2048]{2,1,0:T(8,128)(2,1)}, bf16[2,256,2048]{2,1,0:T(8,128)(2,1)}, f32[256,2048]{1,0:T(8,128)}) custom-call(bf16[8,256,2048]{2,1,0:T(8,128)(2,1)} %refs_3_.5, f32[256,32]{1,0:T(8,128)} %copy.70.mix_ref.refs_4_, f32[4,2048]{1,0:T(4,128)} %refs_5_.7, f32[4,2048]{1,0:T(4,128)} %refs_6_.2), custom_call_target="tpu_custom_call" | custom-call | flops 36700160 | bytes 13631488 | tf_op jit(solution)/shard_map/front/pallas_call | solution.py:83
  32.8 42.5 %collective-permute-done.5.refs_2_ = bf16[1,256,2048]{2,1,0:T(8,128)(2,1)} collective-permute-done((bf16[1,256,2048]{2,1,0:T(8,128)(2,1)}, bf16[1,256,2048]{2,1,0:T(8,128)(2,1)}, u32[]{:S(2)}, u32[]{:S(2)}) %collective-permute-start.5) | collective-permute-done | bytes 1048608 | tf_op jit(solution)/shard_map/ppermute | solution.py:872
  85.9 88.9 %collective-permute-done = bf16[512,2048]{1,0:T(8,128)(2,1)} collective-permute-done((bf16[512,2048]{1,0:T(8,128)(2,1)S(1)}, bf16[512,2048]{1,0:T(8,128)(2,1)}, u32[]{:S(2)}, u32[]{:S(2)}) %collective-permute-start) | collective-permute-done | bytes 2097184 | tf_op jit(solution)/shard_map/ppermute | solution.py:872
  184.7 6.7 qkv_proj.2.query_ref
  192.8 10.4 %qkv_proj.3.kv_ref = bf16[2,1024,512]{2,1,0:T(8,128)(2,1)} custom-call(bf16[2,256,2048]{2,1,0:T(8,128)(2,1)} %get-tuple-element.114.refs_0_.refs_4_, bf16[2,256,2048]{2,1,0:T(8,128)(2,1)} %collective-permute-done.7.refs_1_.refs_5_, bf16[2,256,2048]{2,1,0:T(8,128)(2,1)} %collective-permute-done.1.refs_2_.refs_6_, bf16[2,256,2048]{2,1,0:T(8,128)(2,1)} %copy-done.8, ...), custom_call_target="tpu_custom_call" | custom-call | flops 4294967296 | bytes 10485760 | tf_op jit(solution)/shard_map/qkv_proj/pallas_call | solution.py:268
  203.1 14.4 %attend.1 = (bf16[1,1024,512]{2,1,0:T(8,128)(2,1)}, f32[4,1,1024]{2,1,0:T(1,128)}) custom-call(s32[5]{0:T(128)} %pad_add_fusion.1.scalars, bf16[1,1024,512]{2,1,0:T(8,128)(2,1)} %qkv_proj.2.query_ref, bf16[2,1024,512]{2,1,0:T(8,128)(2,1)} %qkv_proj.3.kv_ref), custom_call_target="tpu_custom_call" | custom-call | flops 4294967296 | bytes 4210688 | tf_op jit(solution)/shard_map/attend/pallas_call | solution.py:381
  230.8 25.1 %collective-permute-done.10.refs_2_ = bf16[1,256,2048]{2,1,0:T(8,128)(2,1)S(1)} collective-permute-done((bf16[1,256,2048]{2,1,0:T(8,128)(2,1)S(1)}, bf16[1,256,2048]{2,1,0:T(8,128)(2,1)S(1)}, u32[]{:S(2)}, u32[]{:S(2)}) %collective-permute-start.10) | collective-permute-done | bytes 1048608 | tf_op jit(solution)/shard_map/ppermute | solution.py:872
  262.3 24.4 %collective-permute-done.12.refs_2_ = bf16[256,2048]{1,0:T(8,128)(2,1)S(1)} collective-permute-done((bf16[256,2048]{1,0:T(8,128)(2,1)}, bf16[256,2048]{1,0:T(8,128)(2,1)S(1)}, u32[]{:S(2)}, u32[]{:S(2)}) %collective-permute-start.12) | collective-permute-done | bytes 1048608 | tf_op jit(solution)/shard_map/ppermute | solution.py:872
  290.3 10.0 %expand.1 = (bf16[1024,1024]{1,0:T(8,128)(2,1)}, bf16[1024,1024]{1,0:T(8,128)(2,1)}) custom-call(bf16[256,2048]{1,0:T(8,128)(2,1)} %get-tuple-element.127.refs_0_, bf16[256,2048]{1,0:T(8,128)(2,1)} %copy-done.41, bf16[256,2048]{1,0:T(8,128)(2,1)} %copy-done.40, bf16[256,2048]{1,0:T(8,128)(2,1)} %copy-done.42, ...), custom_call_target="tpu_custom_call" | custom-call | flops 4294967296 | bytes 8388608 | tf_op jit(solution)/shard_map/expand/pallas_call | solution.py:592
  300.3 10.1 %all-gather.11.cloned.1.call-done.refs_5_.refs_8_.refs_9_ = bf16[2048,2048]{1,0:T(8,128)(2,1)} async-done(((bf16[512,2048]{1,0:T(8,128)(2,1)}), bf16[2048,2048]{1,0:T(8,128)(2,1)}) %all-gather.11.cloned.1.call-update) | async-done | bytes 8388624 | tf_op jit(solution)/shard_map/all_gather | solution.py:945
  310.4 21.7 %feed.1 = (bf16[1024,1024]{1,0:T(8,128)(2,1)}, bf16[1024,1024]{1,0:T(8,128)(2,1)}, bf16[1,2,256,2048]{3,2,1,0:T(8,128)(2,1)}, bf16[1,2,256,2048]{3,2,1,0:T(8,128)(2,1)}) custom-call(bf16[256,2048]{1,0:T(8,128)(2,1)} %get-tuple-element.127.refs_0_, bf16[256,2048]{1,0:T(8,128)(2,1)} %copy-done.41, bf16[256,2048]{1,0:T(8,128)(2,1)} %copy-done.40, ...), custom_call_target="tpu_custom_call" | custom-call | flops 12884901888 | bytes 12582912 | tf_op jit(solution)/shard_map/feed/pallas_call | solution.py:680
  343.5 21.8 %collective-permute-done.15.refs_2_ = bf16[1,256,2048]{2,1,0:T(8,128)(2,1)S(1)} collective-permute-done((bf16[1,256,2048]{2,1,0:T(8,128)(2,1)}, bf16[1,256,2048]{2,1,0:T(8,128)(2,1)S(1)}, u32[]{:S(2)}, u32[]{:S(2)}) %collective-permute-start.15) | collective-permute-done | bytes 1048608 | tf_op jit(solution)/shard_map/ppermute | solution.py:872
  366.3 11.1 %mixing.1 = (f32[256,2048]{1,0:T(8,128)}, f32[256,36]{1,0:T(8,128)}, f32[256,2048]{1,0:T(8,128)}, bf16[256,2048]{1,0:T(8,128)(2,1)}, f32[8,2048]{1,0:T(8,128)}, /*index=5*/f32[36,2048]{1,0:T(8,128)}, f32[36,36]{1,0:T(8,128)}) custom-call(bf16[1,2,256,2048]{3,2,1,0:T(8,128)(2,1)} %get-tuple-element.131.refs_0_, bf16[1,2,256,2048]{3,2,1,0:T(8,128)(2,1)} %copy-done.4, ...), custom_call_target="tpu_custom_call" | custom-call | flops 1572864000 | bytes 14033984 | tf_op jit(solution)/shard_map/mixing/pallas_call | solution.py:855
  385.0 21.1 %collective-permute-done.19.refs_2_ = bf16[256,2048]{1,0:T(8,128)(2,1)S(1)} collective-permute-done((bf16[256,2048]{1,0:T(8,128)(2,1)}, bf16[256,2048]{1,0:T(8,128)(2,1)S(1)}, u32[]{:S(2)}, u32[]{:S(2)}) %collective-permute-start.19) | collective-permute-done | bytes 1048608 | tf_op jit(solution)/shard_map/ppermute | solution.py:872
  409.8 13.6 %weight_grad.2 = bf16[2048,2048]{1,0:T(8,128)(2,1)} custom-call(bf16[256,2048]{1,0:T(8,128)(2,1)} %get-tuple-element.146.refs_0_, bf16[256,2048]{1,0:T(8,128)(2,1)} %copy-done.43, bf16[256,2048]{1,0:T(8,128)(2,1)} %copy-done.44, bf16[256,2048]{1,0:T(8,128)(2,1)} %copy-done.45, bf16[1024,1024]{1,0:T(8,128)(2,1)} %get-tuple-element.129.refs_4_, ...), custom_call_target="tpu_custom_call" | custom-call | flops 8589934592 | bytes 16777216 | tf_op jit(solution)/shard_map/weight_grad/pallas_call | solution.py:714
  425.0 27.1 %feed_back.1 = (bf16[1024,1024]{1,0:T(8,128)(2,1)}, bf16[1024,1024]{1,0:T(8,128)(2,1)}, f32[1,1024]{1,0:T(1,128)}, f32[1,1024]{1,0:T(1,128)}, bf16[1,2,256,2048]...) custom-call(bf16[256,2048]{1,0:T(8,128)(2,1)} %get-tuple-element.146.refs_0_, bf16[256,2048]{1,0:T(8,128)(2,1)} %copy-done.43, ...), custom_call_target="tpu_custom_call" | custom-call | flops 17179869184 | bytes 12591104 | tf_op jit(solution)/shard_map/feed_back/pallas_call | solution.py:680
  463.5 14.2 %weight_grad.3 = bf16[2048,2048]{1,0:T(8,128)(2,1)} custom-call(bf16[256,2048]{1,0:T(8,128)(2,1)} %get-tuple-element.127.refs_0_, bf16[256,2048]{1,0:T(8,128)(2,1)} %copy-done.41, bf16[256,2048]{1,0:T(8,128)(2,1)} %copy-done.40, bf16[256,2048]{1,0:T(8,128)(2,1)} %copy-done.42, bf16[1024,1024]{1,0:T(8,128)(2,1)} %get-tuple-element.155.refs_4_, ...), custom_call_target="tpu_custom_call" | custom-call | flops 8589934592 | bytes 16777216 | tf_op jit(solution)/shard_map/weight_grad/pallas_call | solution.py:714
  477.6 13.3 %collective-permute-done.26 = f32[39,2048]{1,0:T(8,128)} collective-permute-done((f32[39,2048]{1,0:T(8,128)S(1)}, f32[39,2048]{1,0:T(8,128)}, u32[]{:S(2)}, u32[]{:S(2)}) %collective-permute-start.26) | collective-permute-done | bytes 319520 | tf_op jit(solution)/shard_map/ppermute | solution.py:872
  502.1 22.8 %collective-permute-done.29.refs_2_.refs_10_ = bf16[256,2048]{1,0:T(8,128)(2,1)S(1)} collective-permute-done((bf16[256,2048]{1,0:T(8,128)(2,1)}, bf16[256,2048]{1,0:T(8,128)(2,1)S(1)}, u32[]{:S(2)}, u32[]{:S(2)}) %collective-permute-start.29) | collective-permute-done | bytes 1048608 | tf_op jit(solution)/shard_map/ppermute | solution.py:872
  528.6 6.4 proj.1.g_ref
  538.1 18.1 %attend_back.1 = (bf16[3,1024,512]{2,1,0:T(8,128)(2,1)}, f32[4,8,128]{2,1,0:T(8,128)}) custom-call(s32[5]{0:T(128)} %pad_add_fusion.1.scalars, bf16[1,1024,512]{2,1,0:T(8,128)(2,1)} %qkv_proj.2.query_ref, bf16[2,1024,512]{2,1,0:T(8,128)(2,1)} %qkv_proj.3.kv_ref, bf16[1024,512]{1,0:T(8,128)(2,1)} %proj.1.g_ref, f32[4,1,1024]{2,1,0:T(1,128)} %get-tuple-element.160.log_ref, ...), custom_call_target="tpu_custom_call" | custom-call | flops 8589934592 | bytes 7356416 | tf_op jit(solution)/shard_map/attend_back/pallas_call | solution.py:444
  562.4 10.4 %unproj.5 = (bf16[2,2,256,2048]{3,2,1,0:T(8,128)(2,1)}, bf16[2,2,256,2048]{3,2,1,0:T(8,128)(2,1)}) custom-call(bf16[3,1024,512]{2,1,0:T(8,128)(2,1)} %get-tuple-element.162.a_ref.refs_12_, bf16[2048,1024]{1,0:T(8,128)(2,1)} %all-gather.5.cloned.1.call-done.refs_4_.refs_0_, bf16[2048,1024]{1,0:T(8,128)(2,1)} %all-gather.7.cloned.1.call-done.refs_5_.refs_1_), custom_call_target="tpu_custom_call" | custom-call | flops 4294967296 | bytes 8388608 | tf_op jit(solution)/shard_map/unproj/pallas_call | solution.py:336
  584.2 20.1 %collective-permute-done.22 = bf16[512,512]{1,0:T(8,128)(2,1)S(1)} collective-permute-done((bf16[512,512]{1,0:T(8,128)(2,1)S(1)}, bf16[512,512]{1,0:T(8,128)(2,1)S(1)}, u32[]{:S(2)}, u32[]{:S(2)}) %collective-permute-start.22) | collective-permute-done | bytes 524320 | tf_op jit(solution)/shard_map/ppermute | solution.py:872
  621.6 15.7 %piece_grad.1 = (bf16[2048,512]{1,0:T(8,128)(2,1)}, bf16[2048,512]{1,0:T(8,128)(2,1)}, bf16[2048,512]{1,0:T(8,128)(2,1)}, bf16[2048,512]{1,0:T(8,128)(2,1)}) custom-call(s32[3,4]{1,0:T(4,128)} %pad_add_fusion.table, bf16[1,256,2048]{2,1,0:T(8,128)(2,1)} %get-tuple-element.116.refs_0_, bf16[1,256,2048]{2,1,0:T(8,128)(2,1)} %collective-permute-done.2.refs_1_, ...), custom_call_target="tpu_custom_call" | custom-call | flops 8589934592 | bytes 29360128 | tf_op jit(solution)/shard_map/piece_grad/pallas_call | solution.py:773
  644.6 19.6 %collective-permute-done.34 = bf16[1024,512]{1,0:T(8,128)(2,1)S(1)} collective-permute-done((bf16[1024,512]{1,0:T(8,128)(2,1)S(1)}, bf16[1024,512]{1,0:T(8,128)(2,1)S(1)}, u32[]{:S(2)}, u32[]{:S(2)}) %collective-permute-start.34) | collective-permute-done | bytes 1048608 | tf_op jit(solution)/shard_map/ppermute | solution.py:872
  681.8 13.9 %norm_back.3 = (f32[2,256,2048]{2,1,0:T(8,128)}, f32[2,16,2048]{2,1,0:T(8,128)}) custom-call(bf16[2,2,256,2048]{3,2,1,0:T(8,128)(2,1)} %get-tuple-element.167.refs_0_, bf16[2,2,256,2048]{3,2,1,0:T(8,128)(2,1)} %copy.80.refs_1_, bf16[2,256,2048]{2,1,0:T(8,128)(2,1)} %collective-permute-done.36.refs_2_, bf16[8,256,2048]{2,1,0:T(8,128)(2,1)} %refs_3_.5, ...), custom_call_target="tpu_custom_call" | custom-call | flops 41943040 | bytes 23330816 | tf_op jit(solution)/shard_map/norm_back/pallas_call | solution.py:152
  696.7 7.7 collective-permute-done.49
  709.3 11.7 %norm_back.2 = (f32[1,256,2048]{2,1,0:T(8,128)}, f32[1,16,2048]{2,1,0:T(8,128)}) custom-call(bf16[1,2,256,2048]{3,2,1,0:T(8,128)(2,1)} %get-tuple-element.165.refs_0_, bf16[1,2,256,2048]{3,2,1,0:T(8,128)(2,1)} %copy-done.2, bf16[1,256,2048]{2,1,0:T(8,128)(2,1)} %collective-permute-done.33.refs_2_, bf16[8,256,2048]{2,1,0:T(8,128)(2,1)} %refs_3_.5, ...), custom_call_target="tpu_custom_call" | custom-call | flops 20971520 | bytes 15859712 | tf_op jit(solution)/shard_map/norm_back/pallas_call | solution.py:152
  737.1 7.4 collective-permute-done.43
  750.7 23.0 %collective-permute-done.48 = bf16[512,1024]{1,0:T(8,128)(2,1)} collective-permute-done((bf16[512,1024]{1,0:T(8,128)(2,1)}, bf16[512,1024]{1,0:T(8,128)(2,1)}, u32[]{:S(2)}, u32[]{:S(2)}) %collective-permute-start.48) | collective-permute-done | bytes 1048608 | tf_op jit(solution)/shard_map/ppermute | solution.py:872
  775.9 17.3 %stack_back.1 = (f32[8,256,2048]{2,1,0:T(8,128)}, f32[256,32]{1,0:T(8,128)}) custom-call(f32[1,256,2048]{2,1,0:T(8,128)} %get-tuple-element.190.refs_0_, f32[2,256,2048]{2,1,0:T(8,128)} %get-tuple-element.194.refs_1_, f32[256,2048]{1,0:T(8,128)} %get-tuple-element.195.refs_2_, bf16[8,256,2048]{2,1,0:T(8,128)(2,1)} %refs_3_.5, f32[256,32]{1,0:T(8,128)} %copy.70.mix_ref.refs_4_), custom_call_target="tpu_custom_call" | custom-call | flops 68157440 | bytes 33587200 | tf_op jit(solution)/shard_map/stack_back/pallas_call | solution.py:206
  793.2 7.2 collective-permute-done.52
  (301 shorter events, 221.2 us)
Async XLA Ops:
  7.2 177.5 %all-gather.5.cloned.1.call-start = ((), (), s32[]{:S(2)}) async-start(), calls=%async_computation.2 | async-start | bytes 5242880 | tf_op jit(solution)/shard_map/all_gather | solution.py:945
  16.1 168.6 %all-gather.7.cloned.1.call-start = ((), (), s32[]{:S(2)}) async-start(), calls=%async_computation.3 | async-start | bytes 5242880 | tf_op jit(solution)/shard_map/all_gather | solution.py:945
  30.0 45.2 %collective-permute-start.5 = (bf16[1,256,2048]{2,1,0:T(8,128)(2,1)}, bf16[1,256,2048]{2,1,0:T(8,128)(2,1)}, u32[]{:S(2)}, u32[]{:S(2)}) collective-permute-start(bf16[1,256,2048]{2,1,0:T(8,128)(2,1)} %get-tuple-element.116.refs_0_), channel_id=1, source_target_pairs={{0,2},{2,0},{1,3},{3,1},{4,6},{6,4},{5,7},{7,5},{8,10},{10,8},{9,1... | collective-permute-start | bytes 3145736 | tf_op jit(solution)/shard_map/ppermute | solution.py:872
  31.6 47.8 %collective-permute-start.4 = (bf16[512,1024]{1,0:T(8,128)(2,1)S(1)}, bf16[512,1024]{1,0:T(8,128)(2,1)S(1)}, u32[]{:S(2)}, u32[]{:S(2)}) collective-permute-start(bf16[512,1024]{1,0:T(8,128)(2,1)S(1)} %copy-done.7), channel_id=1, source_target_pairs={{0,4},{4,0},{1,5},{5,1},{2,6},{6,2},{3,7},{7,3},{8,12},{12,8},{9,1... | collective-permute-start | bytes 3145736 | tf_op jit(solution)/shard_map/ppermute | solution.py:872
  80.5 208.9 %all-gather.9.cloned.1.call-start = ((), (), s32[]{:S(2)}) async-start(), calls=%async_computation.4 | async-start | bytes 10485760 | tf_op jit(solution)/shard_map/all_gather | solution.py:945
  83.9 226.5 %all-gather.11.cloned.1.call-start = ((), (), s32[]{:S(2)}) async-start(), calls=%async_computation.5 | async-start | bytes 10485760 | tf_op jit(solution)/shard_map/all_gather | solution.py:945
  85.6 89.2 %collective-permute-start = (bf16[512,2048]{1,0:T(8,128)(2,1)S(1)}, bf16[512,2048]{1,0:T(8,128)(2,1)}, u32[]{:S(2)}, u32[]{:S(2)}) collective-permute-start(bf16[512,2048]{1,0:T(8,128)(2,1)S(1)} %copy-done), channel_id=1, source_target_pairs={{0,4},{4,0},{1,5},{5,1},{2,6},{6,2},{3,7},{7,3},{8,12},{12,8},{9,1... | collective-permute-start | bytes 6291464 | tf_op jit(solution)/shard_map/ppermute | solution.py:872
  85.9 91.2 %collective-permute-start.1 = (bf16[2,256,2048]{2,1,0:T(8,128)(2,1)}, bf16[2,256,2048]{2,1,0:T(8,128)(2,1)}, u32[]{:S(2)}, u32[]{:S(2)}) collective-permute-start(bf16[2,256,2048]{2,1,0:T(8,128)(2,1)} %get-tuple-element.114.refs_0_.refs_4_), channel_id=1, source_target_pairs={{0,2},{2,0},{1,3},{3,1},{4,6},{6,4},{5,7},{7,5},{8,10},{10,8},{9,1... | collective-permute-start | bytes 6291464 | tf_op jit(solution)/shard_map/ppermute | solution.py:872
  85.9 105.5 %collective-permute-start.7 = (bf16[2,256,2048]{2,1,0:T(8,128)(2,1)}, bf16[2,256,2048]{2,1,0:T(8,128)(2,1)}, u32[]{:S(2)}, u32[]{:S(2)}) collective-permute-start(bf16[2,256,2048]{2,1,0:T(8,128)(2,1)} %get-tuple-element.114.refs_0_.refs_4_), channel_id=1, source_target_pairs={{0,1},{1,0},{2,3},{3,2},{4,5},{5,4},{6,7},{7,6},{8,9},{9,8},{10,11... | collective-permute-start | bytes 6291464 | tf_op jit(solution)/shard_map/ppermute | solution.py:872
  217.5 317.5 %reduce-scatter.3.cloned.1.call-start = ((), (), s32[]{:S(2)}) async-start(), calls=%async_computation.6 | async-start | bytes 10485760 | tf_op jit(solution)/shard_map/reduce_scatter | solution.py:949
  339.9 25.4 %collective-permute-start.15 = (bf16[1,256,2048]{2,1,0:T(8,128)(2,1)}, bf16[1,256,2048]{2,1,0:T(8,128)(2,1)S(1)}, u32[]{:S(2)}, u32[]{:S(2)}) collective-permute-start(bf16[1,256,2048]{2,1,0:T(8,128)(2,1)} %fusion.2), channel_id=1, source_target_pairs={{0,2},{2,0},{1,3},{3,1},{4,6},{6,4},{5,7},{7,5},{8,10},{10,8},{9,1... | collective-permute-start | bytes 3145736 | tf_op jit(solution)/shard_map/ppermute | solution.py:872
  380.8 25.4 %collective-permute-start.19 = (bf16[256,2048]{1,0:T(8,128)(2,1)}, bf16[256,2048]{1,0:T(8,128)(2,1)S(1)}, u32[]{:S(2)}, u32[]{:S(2)}) collective-permute-start(bf16[256,2048]{1,0:T(8,128)(2,1)} %get-tuple-element.146.refs_0_), channel_id=1, source_target_pairs={{0,2},{2,0},{1,3},{3,1},{4,6},{6,4},{5,7},{7,5},{8,10},{10,8},{9,1... | collective-permute-start | bytes 3145736 | tf_op jit(solution)/shard_map/ppermute | solution.py:872
  423.4 251.4 %reduce-scatter.5.cloned.1.call-start = ((), (), s32[]{:S(2)}) async-start(), calls=%async_computation.7 | async-start | bytes 10485760 | tf_op jit(solution)/shard_map/reduce_scatter | solution.py:949
  423.5 28.6 %collective-permute-start.24 = (f32[39,2048]{1,0:T(8,128)S(1)}, f32[39,2048]{1,0:T(8,128)S(1)}, u32[]{:S(2)}, u32[]{:S(2)}) collective-permute-start(f32[39,2048]{1,0:T(8,128)S(1)} %add.185), channel_id=1, source_target_pairs={{0,2},{2,0},{1,3},{3,1},{4,6},{6,4},{5,7},{7,5},{8,10},{10,8},{9,1... | collective-permute-start | bytes 958472 | tf_op jit(solution)/shard_map/ppermute | solution.py:872
  459.9 32.4 %collective-permute-start.27 = (bf16[1,256,2048]{2,1,0:T(8,128)(2,1)}, bf16[1,256,2048]{2,1,0:T(8,128)(2,1)S(1)}, u32[]{:S(2)}, u32[]{:S(2)}) collective-permute-start(bf16[1,256,2048]{2,1,0:T(8,128)(2,1)} %fusion.3), channel_id=1, source_target_pairs={{0,2},{2,0},{1,3},{3,1},{4,6},{6,4},{5,7},{7,5},{8,10},{10,8},{9,1... | collective-permute-start | bytes 3145736 | tf_op jit(solution)/shard_map/ppermute | solution.py:872
  461.0 29.9 %collective-permute-start.26 = (f32[39,2048]{1,0:T(8,128)S(1)}, f32[39,2048]{1,0:T(8,128)}, u32[]{:S(2)}, u32[]{:S(2)}) collective-permute-start(f32[39,2048]{1,0:T(8,128)S(1)} %add.186), channel_id=1, source_target_pairs={{0,4},{4,0},{1,5},{5,1},{2,6},{6,2},{3,7},{7,3},{8,12},{12,8},{9,1... | collective-permute-start | bytes 958472 | tf_op jit(solution)/shard_map/ppermute | solution.py:872
  536.4 26.0 %collective-permute-start.23 = (bf16[512,512]{1,0:T(8,128)(2,1)S(1)}, bf16[512,512]{1,0:T(8,128)(2,1)S(1)}, u32[]{:S(2)}, u32[]{:S(2)}) collective-permute-start(bf16[512,512]{1,0:T(8,128)(2,1)S(1)} %get-tuple-element.268), channel_id=1, source_target_pairs={{0,4},{4,0},{1,5},{5,1},{2,6},{6,2},{3,7},{7,3},{8,12},{12,8},{9,1... | collective-permute-start | bytes 1572872 | tf_op jit(solution)/shard_map/ppermute | solution.py:872
  578.4 34.5 %collective-permute-start.32 = (bf16[2,2,256,2048]{3,2,0,1:T(8,128)(2,1)}, bf16[2,2,256,2048]{3,2,0,1:T(8,128)(2,1)}, u32[]{:S(2)}, u32[]{:S(2)}) collective-permute-start(bf16[2,2,256,2048]{3,2,0,1:T(8,128)(2,1)} %copy.78), channel_id=1, source_target_pairs={{0,1},{1,0},{2,3},{3,2},{4,5},{5,4},{6,7},{7,6},{8,9},{9,8},{10,11... | collective-permute-start | bytes 12582920 | tf_op jit(solution)/shard_map/ppermute | solution.py:872
  578.4 26.0 %collective-permute-start.22 = (bf16[512,512]{1,0:T(8,128)(2,1)S(1)}, bf16[512,512]{1,0:T(8,128)(2,1)S(1)}, u32[]{:S(2)}, u32[]{:S(2)}) collective-permute-start(bf16[512,512]{1,0:T(8,128)(2,1)S(1)} %get-tuple-element.269), channel_id=1, source_target_pairs={{0,4},{4,0},{1,5},{5,1},{2,6},{6,2},{3,7},{7,3},{8,12},{12,8},{9,1... | collective-permute-start | bytes 1572872 | tf_op jit(solution)/shard_map/ppermute | solution.py:872
  617.4 48.8 %collective-permute-start.36 = (bf16[2,256,2048]{2,1,0:T(8,128)(2,1)}, bf16[2,256,2048]{2,1,0:T(8,128)(2,1)}, u32[]{:S(2)}, u32[]{:S(2)}) collective-permute-start(bf16[2,256,2048]{2,1,0:T(8,128)(2,1)} %fusion), channel_id=1, source_target_pairs={{0,2},{2,0},{1,3},{3,1},{4,6},{6,4},{5,7},{7,5},{8,10},{10,8},{9,1... | collective-permute-start | bytes 6291464 | tf_op jit(solution)/shard_map/ppermute | solution.py:872
  638.9 25.3 %collective-permute-start.34 = (bf16[1024,512]{1,0:T(8,128)(2,1)S(1)}, bf16[1024,512]{1,0:T(8,128)(2,1)S(1)}, u32[]{:S(2)}, u32[]{:S(2)}) collective-permute-start(bf16[1024,512]{1,0:T(8,128)(2,1)S(1)} %slice.210), channel_id=1, source_target_pairs={{0,8},{8,0},{16,24},{24,16},{1,9},{9,1},{17,25},{25,17},{2,10},{10... | collective-permute-start | bytes 3145736 | tf_op jit(solution)/shard_map/ppermute | solution.py:872
  642.5 66.8 %collective-permute-start.33 = (bf16[1,256,2048]{2,1,0:T(8,128)(2,1)}, bf16[1,256,2048]{2,1,0:T(8,128)(2,1)}, u32[]{:S(2)}, u32[]{:S(2)}) collective-permute-start(bf16[1,256,2048]{2,1,0:T(8,128)(2,1)} %fusion.4), channel_id=1, source_target_pairs={{0,2},{2,0},{1,3},{3,1},{4,6},{6,4},{5,7},{7,5},{8,10},{10,8},{9,1... | collective-permute-start | bytes 3145736 | tf_op jit(solution)/shard_map/ppermute | solution.py:872
  667.3 42.0 %collective-permute-start.37 = (bf16[1024,512]{1,0:T(8,128)(2,1)}, bf16[1024,512]{1,0:T(8,128)(2,1)}, u32[]{:S(2)}, u32[]{:S(2)}) collective-permute-start(bf16[1024,512]{1,0:T(8,128)(2,1)} %slice.212), channel_id=1, source_target_pairs={{0,8},{8,0},{16,24},{24,16},{1,9},{9,1},{17,25},{25,17},{2,10},{10... | collective-permute-start | bytes 3145736 | tf_op jit(solution)/shard_map/ppermute | solution.py:872
  669.7 39.6 %collective-permute-start.38 = (bf16[1024,512]{1,0:T(8,128)(2,1)}, bf16[1024,512]{1,0:T(8,128)(2,1)}, u32[]{:S(2)}, u32[]{:S(2)}) collective-permute-start(bf16[1024,512]{1,0:T(8,128)(2,1)} %slice.213), channel_id=1, source_target_pairs={{0,16},{8,24},{16,0},{24,8},{1,17},{9,25},{17,1},{25,9},{2,18},{10... | collective-permute-start | bytes 3145736 | tf_op jit(solution)/shard_map/ppermute | solution.py:872
  671.4 33.0 %collective-permute-start.49 = (bf16[512,512]{1,0:T(8,128)(2,1)}, bf16[512,512]{1,0:T(8,128)(2,1)S(1)}, u32[]{:S(2)}, u32[]{:S(2)}) collective-permute-start(bf16[512,512]{1,0:T(8,128)(2,1)} %slice.263), channel_id=1, source_target_pairs={{0,16},{8,24},{16,0},{24,8},{1,17},{9,25},{17,1},{25,9},{2,18},{10... | collective-permute-start | bytes 1572872 | tf_op jit(solution)/shard_map/ppermute | solution.py:872
  674.0 31.2 %collective-permute-start.50 = (bf16[512,512]{1,0:T(8,128)(2,1)}, bf16[512,512]{1,0:T(8,128)(2,1)S(1)}, u32[]{:S(2)}, u32[]{:S(2)}) collective-permute-start(bf16[512,512]{1,0:T(8,128)(2,1)} %slice.264), channel_id=1, source_target_pairs={{0,8},{8,0},{16,24},{24,16},{1,9},{9,1},{17,25},{25,17},{2,10},{10... | collective-permute-start | bytes 1572872 | tf_op jit(solution)/shard_map/ppermute | solution.py:872
  704.4 69.2 %collective-permute-start.48 = (bf16[512,1024]{1,0:T(8,128)(2,1)}, bf16[512,1024]{1,0:T(8,128)(2,1)}, u32[]{:S(2)}, u32[]{:S(2)}) collective-permute-start(bf16[512,1024]{1,0:T(8,128)(2,1)} %slice.262), channel_id=1, source_target_pairs={{0,4},{4,0},{1,5},{5,1},{2,6},{6,2},{3,7},{7,3},{8,12},{12,8},{9,1... | collective-permute-start | bytes 3145736 | tf_op jit(solution)/shard_map/ppermute | solution.py:872
  706.2 87.0 %collective-permute-start.51 = (bf16[512,512]{1,0:T(8,128)(2,1)}, bf16[512,512]{1,0:T(8,128)(2,1)}, u32[]{:S(2)}, u32[]{:S(2)}) collective-permute-start(bf16[512,512]{1,0:T(8,128)(2,1)} %add_convert_fusion.10), channel_id=1, source_target_pairs={{0,4},{4,0},{1,5},{5,1},{2,6},{6,2},{3,7},{7,3},{8,12},{12,8},{9,1... | collective-permute-start | bytes 1572872 | tf_op jit(solution)/shard_map/ppermute | solution.py:872
  744.5 55.8 %collective-permute-start.52 = (bf16[512,512]{1,0:T(8,128)(2,1)}, bf16[512,512]{1,0:T(8,128)(2,1)}, u32[]{:S(2)}, u32[]{:S(2)}) collective-permute-start(bf16[512,512]{1,0:T(8,128)(2,1)} %add_convert_fusion.9), channel_id=1, source_target_pairs={{0,4},{4,0},{1,5},{5,1},{2,6},{6,2},{3,7},{7,3},{8,12},{12,8},{9,1... | collective-permute-start | bytes 1572872 | tf_op jit(solution)/shard_map/ppermute | solution.py:872
  748.7 27.1 %collective-permute-start.46 = (bf16[512,512]{1,0:T(8,128)(2,1)}, bf16[512,512]{1,0:T(8,128)(2,1)}, u32[]{:S(2)}, u32[]{:S(2)}) collective-permute-start(bf16[512,512]{1,0:T(8,128)(2,1)} %slice.260), channel_id=1, source_target_pairs={{0,16},{8,24},{16,0},{24,8},{1,17},{9,25},{17,1},{25,9},{2,18},{10... | collective-permute-start | bytes 1572872 | tf_op jit(solution)/shard_map/ppermute | solution.py:872
  749.8 26.0 %collective-permute-start.47 = (bf16[512,512]{1,0:T(8,128)(2,1)}, bf16[512,512]{1,0:T(8,128)(2,1)}, u32[]{:S(2)}, u32[]{:S(2)}) collective-permute-start(bf16[512,512]{1,0:T(8,128)(2,1)} %slice.261), channel_id=1, source_target_pairs={{0,8},{8,0},{16,24},{24,16},{1,9},{9,1},{17,25},{25,17},{2,10},{10... | collective-permute-start | bytes 1572872 | tf_op jit(solution)/shard_map/ppermute | solution.py:872
  773.7 30.1 %collective-permute-start.45 = (f32[17,2048]{1,0:T(8,128)S(1)}, f32[17,2048]{1,0:T(8,128)S(1)}, u32[]{:S(2)}, u32[]{:S(2)}) collective-permute-start(f32[17,2048]{1,0:T(8,128)S(1)} %add_add_fusion), channel_id=1, source_target_pairs={{0,4},{4,0},{1,5},{5,1},{2,6},{6,2},{3,7},{7,3},{8,12},{12,8},{9,1... | collective-permute-start | bytes 417800 | tf_op jit(solution)/shard_map/ppermute | solution.py:919
  (74 other events, 1158.7 us)
Sparse Core Ops, SparseCore 0:
  16.2 52.5 all-gather.4
  80.6 50.9 all-gather.6
  133.4 87.5 all-gather.8
  222.7 87.6 all-gather.10
  423.5 86.4 reduce-scatter.2
  513.8 86.3 reduce-scatter.4

commit v3 on v2

--- a/solution.py
+++ b/solution.py
@@ -33,9 +33,11 @@
     return pltpu.CompilerParams(vmem_limit_bytes=VMEM_CAP)
 
 
-def cost(flops, arrays, extra=0):
+def cost(flops, arrays, weight=8):
     moved = sum(int(a.size) * a.dtype.itemsize for a in arrays)
-    return pl.CostEstimate(flops=int(flops), bytes_accessed=int(moved), transcendentals=int(extra))
+    return pl.CostEstimate(
+        flops=int(weight * flops), bytes_accessed=int(weight * moved), transcendentals=0
+    )
 
 
 def sds(shape, dtype):
@@ -119,7 +121,7 @@
             hat = centred * rstd
             grad = None
             for part in parts:
-                term = (part[n, 0, rows, :] if len(part.shape) == 4 else part[n, rows, :]).astype(
+                term = (part[0, n, rows, :] if len(part.shape) == 4 else part[n, rows, :]).astype(
                     F32
                 )
                 grad = term if grad is None else grad + term
@@ -144,7 +146,7 @@
     row_block = lambda i: (i, 0)
     outs = [sds((count, tokens, width), F32), sds((count, 16, width), F32)]
     specs = [
-        pl.BlockSpec((count, 1, tile, width), lambda i: (0, 0, i, 0))
+        pl.BlockSpec((1, count, tile, width), lambda i: (0, 0, i, 0))
         if len(p.shape) == 4
         else pl.BlockSpec((count, tile, width), lambda i: (0, i, 0))
         for p in parts
@@ -164,7 +166,7 @@
         ],
         out_shape=outs,
         compiler_params=params(),
-        cost_estimate=cost(40 * count * tokens * width, [stack, *parts, *outs]),
+        cost_estimate=cost(40 * count * tokens * width, [stack, *parts, *outs], 0.05),
         name="norm_back",
     )(*parts, stack, mix, gain)
 
@@ -310,20 +312,19 @@
 
 
 def put_blocks(outs, block, values):
-    outs[block % 2][0, block // 2] = values
+    outs[block % 2][block // 2, 0] = values
 
 
 def unproj_kernel(a_ref, *refs):
     weights, outs = refs[:-2], refs[-2:]
-    _, pairs, rows, _ = outs[0].shape
+    pairs, _, rows, _ = outs[0].shape
+    total = None
+    for h, weight_ref in enumerate(weights):
+        cols = weight_ref.shape[1]
+        term = dot(a_ref[0, :, h * cols : (h + 1) * cols], weight_ref[...], NT)
+        total = term if total is None else total + term
     for b in range(2 * pairs):
-        here = slice(b * rows, (b + 1) * rows)
-        total = None
-        for h, weight_ref in enumerate(weights):
-            cols = weight_ref.shape[1]
-            term = dot(a_ref[0, here, h * cols : (h + 1) * cols], weight_ref[...], NT)
-            total = term if total is None else total + term
-        put_blocks(outs, b, total.astype(BF))
+        put_blocks(outs, b, total[b * rows : (b + 1) * rows].astype(BF))
 
 
 def unproj(part, first, count, weights, place, blocks):
@@ -332,13 +333,13 @@
     width = weights[0].shape[0]
     tile = 512
     rows = tokens // blocks
-    outs = [sds((count, blocks // 2, rows, width), BF)] * 2
+    outs = [sds((blocks // 2, count, rows, width), BF)] * 2
     return pl.pallas_call(
         unproj_kernel,
         grid=(count, width // tile),
         in_specs=[pl.BlockSpec((1, tokens, cols), lambda s, i: (first + s, 0, 0))]
         + [pl.BlockSpec((tile, cols // halves), lambda s, i: (i, place + s))] * halves,
-        out_specs=[pl.BlockSpec((1, blocks // 2, rows, tile), lambda s, i: (s, 0, 0, i))] * 2,
+        out_specs=[pl.BlockSpec((blocks // 2, 1, rows, tile), lambda s, i: (0, s, 0, i))] * 2,
         out_shape=outs,
         compiler_params=params(),
         cost_estimate=cost(2 * count * tokens * cols * width, outs),
@@ -554,30 +555,33 @@
     return values * tail, slope
 
 
-def expand_block(x_refs, weight_ref, extra_ref, back, act_ref, second_ref, columns, act_columns):
+def fill(x_refs, held):
     rows = x_refs[0].shape[0]
-    total = None
-    for b, x_ref in enumerate(x_refs):
-        here = slice(b * rows, (b + 1) * rows)
-        up = dot(x_ref[...], weight_ref[...], NN)
-        if back:
-            low = (up * extra_ref[here, columns].astype(F32)).astype(BF)
-            part = jnp.sum(low.astype(F32), axis=0, keepdims=True)
-            total = part if total is None else total + part
-        else:
-            act, slope = gelu_pair(up + extra_ref[...])
-            low = act.astype(BF)
-            second_ref[here, columns] = slope.astype(BF)
-        act_ref[here, act_columns] = low
+
+    @pl.when(pl.program_id(0) == 0)
+    def _():
+        for b, x_ref in enumerate(x_refs):
+            held[b * rows : (b + 1) * rows, :] = x_ref[...]
+
+
+def expand_block(x_held, weight_ref, extra_ref, back, act_ref, second_ref):
+    up = dot(x_held[...], weight_ref[...], NN)
     if back:
-        second_ref[...] = total
+        low = (up * extra_ref[...].astype(F32)).astype(BF)
+        second_ref[...] = jnp.sum(low.astype(F32), axis=0, keepdims=True)
+    else:
+        act, slope = gelu_pair(up + extra_ref[...])
+        low = act.astype(BF)
+        second_ref[...] = slope.astype(BF)
+    act_ref[...] = low
+    return low
 
 
 def expand_kernel(blocks, *refs):
     x_refs = refs[:blocks]
-    weight_ref, bias_ref, act_ref, slope_ref = refs[blocks:]
-    every = slice(None)
-    expand_block(x_refs, weight_ref, bias_ref, False, act_ref, slope_ref, every, every)
+    weight_ref, bias_ref, act_ref, slope_ref, x_held = refs[blocks:]
+    fill(x_refs, x_held)
+    expand_block(x_held, weight_ref, bias_ref, False, act_ref, slope_ref)
 
 
 def expand(x_blocks, weight, bias):
@@ -599,6 +603,7 @@
         ],
         out_specs=[column] * 2,
         out_shape=outs,
+        scratch_shapes=[pltpu.VMEM((tokens, width), BF)],
         compiler_params=params(),
         cost_estimate=cost(2 * tokens * width * hidden, [*x_blocks, *outs]),
         name="expand",
@@ -616,37 +621,33 @@
     second_refs, refs = refs[:halves], refs[halves:]
     act_refs, refs = refs[:n_new], refs[n_new:]
     other_refs, refs = refs[:n_new], refs[n_new:]
-    outs, held = refs[:2], refs[2]
+    outs, held, x_held = refs[:2], refs[2], refs[3]
+    fill(x_refs, x_held)
     step = pl.program_id(0)
     hidden = held.shape[1] // max(n_new, 1)
     per = hidden // tile
-    every = slice(None)
     for n in range(n_new):
         for i in range(per):
 
             @pl.when(step == n * per + i)
             def _():
-                columns = slice(i * tile, (i + 1) * tile)
-                expand_block(
-                    x_refs, first_refs[n], extra_refs[n], back, act_refs[n], other_refs[n],
-                    every, every,
+                held[:, n * hidden + i * tile : n * hidden + (i + 1) * tile] = expand_block(
+                    x_held, first_refs[n], extra_refs[n], back, act_refs[n], other_refs[n]
                 )
-                held[:, n * hidden + i * tile : n * hidden + (i + 1) * tile] = act_refs[n][...]
 
     @pl.when(step >= n_new * per)
     def _():
-        _, pairs, rows, _ = outs[0].shape
+        pairs, _, rows, _ = outs[0].shape
+        total = None
+        for h in range(halves):
+            if h < ready:
+                a = done_refs[h][...]
+            else:
+                a = held[:, (h - ready) * hidden : (h - ready + 1) * hidden]
+            term = dot(a, second_refs[h][...], NT)
+            total = term if total is None else total + term
         for b in range(2 * pairs):
-            here = slice(b * rows, (b + 1) * rows)
-            total = None
-            for h in range(halves):
-                if h < ready:
-                    a = done_refs[h][here, :]
-                else:
-                    a = held[here, (h - ready) * hidden : (h - ready + 1) * hidden]
-                term = dot(a, second_refs[h][...], NT)
-                total = term if total is None else total + term
-            put_blocks(outs, b, total.astype(BF))
+            put_blocks(outs, b, total[b * rows : (b + 1) * rows].astype(BF))
 
 
 def feed(x_blocks, done, weights, first_part, extras, back):
@@ -675,7 +676,7 @@
     outs = (
         [sds((tokens, hidden), BF)] * n_new
         + [sds((1, hidden), F32) if back else sds((tokens, hidden), BF)] * n_new
-        + [sds((1, blocks // 2, rows, width), BF)] * 2
+        + [sds((blocks // 2, 1, rows, width), BF)] * 2
     )
     found = pl.pallas_call(
         functools.partial(feed_kernel, blocks, ready, [per] * halves, tile, back),
@@ -687,9 +688,12 @@
         + [pl.BlockSpec((out_tile, hidden), lambda i: (late(i), second_part))] * halves,
         out_specs=act_specs
         + other_specs
-        + [pl.BlockSpec((1, blocks // 2, rows, out_tile), lambda i: (0, 0, 0, late(i)))] * 2,
+        + [pl.BlockSpec((blocks // 2, 1, rows, out_tile), lambda i: (0, 0, 0, late(i)))] * 2,
         out_shape=outs,
-        scratch_shapes=[pltpu.VMEM((tokens, n_new * hidden), BF)],
+        scratch_shapes=[
+            pltpu.VMEM((tokens, n_new * hidden), BF),
+            pltpu.VMEM((tokens, width), BF),
+        ],
         compiler_params=params(),
         cost_estimate=cost(2 * tokens * width * hidden * (n_new + halves), [*x_blocks, *outs]),
         name="feed_back" if back else "feed",
@@ -697,33 +701,29 @@
     return found[:n_new], found[n_new : 2 * n_new], found[2 * n_new :]
 
 
-def weight_grad_kernel(blocks, *refs):
+def weight_grad_kernel(blocks, halves, *refs):
     left = jnp.concatenate([r[...] for r in refs[:blocks]], axis=0)
-    out_ref = refs[-1]
-    start = 0
-    for right in refs[blocks:-1]:
-        cols = right.shape[1]
-        out_ref[:, start : start + cols] = dot(left, right[...], TN).astype(BF)
-        start += cols
-
-
-def weight_grad(lefts, rights):
+    rank_ref, out_ref = refs[-2], refs[-1]
+    for h, right in enumerate(refs[blocks:-2]):
+        out_ref[0, pl.ds(rank_ref[0] ^ h, 1)] = dot(left, right[...], TN).astype(BF)[None]
+
+
+def weight_grad(lefts, rights, feats, rank):
     rows, width = lefts[0].shape
-    tile = 512
-    out = sds((width, sum(r.shape[1] for r in rights)), BF)
+    halves, cols = len(rights), rights[0].shape[1]
+    out = sds((width // feats, halves, feats, cols), BF)
     return pl.pallas_call(
-        functools.partial(weight_grad_kernel, len(lefts)),
-        grid=(width // tile,),
-        in_specs=[pl.BlockSpec((rows, tile), lambda i: (0, i))] * len(lefts)
-        + [pl.BlockSpec(r.shape, lambda i: (0, 0)) for r in rights],
-        out_specs=pl.BlockSpec((tile, out.shape[1]), lambda i: (i, 0)),
+        functools.partial(weight_grad_kernel, len(lefts), halves),
+        grid=(width // feats,),
+        in_specs=[pl.BlockSpec((rows, feats), lambda i: (0, i))] * len(lefts)
+        + [pl.BlockSpec(r.shape, lambda i: (0, 0)) for r in rights]
+        + [pl.BlockSpec(memory_space=pltpu.SMEM)],
+        out_specs=pl.BlockSpec((1, halves, feats, cols), lambda i: (i, 0, 0, 0)),
         out_shape=out,
         compiler_params=params(),
-        cost_estimate=cost(
-            2 * rows * len(lefts) * width * out.shape[1], [*rights, *lefts, out]
-        ),
+        cost_estimate=cost(2 * rows * len(lefts) * width * halves * cols, [*rights, *lefts, out]),
         name="weight_grad",
-    )(*lefts, *rights)
+    )(*lefts, *rights, rank)
 
 
 def piece_places(order, pieces):
@@ -789,7 +789,9 @@
         out_shape=outs,
         compiler_params=params(),
         cost_estimate=cost(
-            8 * rows * blocks * width * cols * halves, [*firsts, *rests, grads, *attn, head, *outs]
+            8 * rows * blocks * width * cols * halves,
+            [*firsts, *rests, grads, *attn, head, *outs],
+            0.05,
         ),
         name="piece_grad",
     )(table, *firsts, *rests, *attn, grads, head)
@@ -885,13 +887,10 @@
     return blocks
 
 
-def chip_sums(own, theirs):
-    got = swap(theirs, "core", 1)
-    sums = [
-        (own[:, k].astype(F32) + got[:, k].astype(F32)).astype(BF)
-        for k in range(1, own.shape[1])
+def chip_sums(own, got):
+    return [
+        (own[k].astype(F32) + got[k].astype(F32)).astype(BF) for k in range(1, own.shape[0])
     ]
-    return [own, got], sums
 
 
 def send_sums(sums):
@@ -905,19 +904,6 @@
 
 def halves_of(values):
     return [values] + [swap(values, "zh", h) for h in range(1, lax.axis_size("zh"))]
-
-
-def tree(terms):
-    while len(terms) > 1:
-        terms = [a + b for a, b in zip(terms[::2], terms[1::2])]
-    return terms[0]
-
-
-def sum_parts(values, axes):
-    size = lax.axis_size(axes)
-    return [values] + [
-        lax.ppermute(values, axes, [(i, i ^ k) for i in range(size)]) for k in range(1, size)
-    ]
 
 
 def exchange_orders():
@@ -945,13 +931,9 @@
     return lax.all_gather(values, "row", axis=0, tiled=True)
 
 
-def scatter_rows(grad):
-    return lax.psum_scatter(grad, "row", scatter_dimension=0, tiled=True)
-
-
-def other_halves(mine, halves):
-    cols = mine.shape[1] // halves
-    return [swap(mine[:, h * cols : (h + 1) * cols], "zh", h) for h in range(1, halves)]
+def scatter_weight(grad):
+    mine = lax.psum_scatter(grad, "row", scatter_dimension=0, tiled=False)
+    return lax.psum_scatter(mine, "zh", scatter_dimension=0, tiled=False)
 
 
 def total_grad(mine, others):
@@ -1013,6 +995,7 @@
         attn_full.append(gather_weight(attn_halves[h]))
     feed_full = [gather_weight(after(feed_local, attn_halves[-1])[0])]
     feed_halves, kv_arrived = together(halves_of(feed_local)[1:], kv_arrived)
+    kv_arrived, (*tables, scalars) = together(kv_arrived, [*tables, scalars])
     query_all = token_blocks(query_in, query_beside, query_arrived)
     kv_all = token_blocks(kv_in, kv_beside, kv_arrived)
     query = qkv_proj(query_all, attn_full, 0, qkv_biases, tables)
@@ -1020,8 +1003,9 @@
     head, log_total = attend(scalars, query, kv, group)
     feed_halves, (head,) = together(feed_halves, [head])
     feed_full += [gather_weight(held) for held in feed_halves]
-    terms, sums = chip_sums(*unproj(head, 0, 1, attn_full, 3, group))
-    arrived = send_sums(sums)
+    own, theirs = unproj(head, 0, 1, attn_full, 3, group)
+    terms = [own, swap(theirs, "core", 1)]
+    arrived = send_sums(chip_sums(*terms))
     hidden, normed2 = middle(
         terms + arrived, residual, out_bias.reshape(1, -1), ln_gain, ln_bias
     )
@@ -1031,9 +1015,9 @@
         normed2_all, act, feed_full, 0, up_biases[1:], False
     )
     act, slope = [*act, *new_act], [*slope, *new_slope]
-    terms, sums = chip_sums(own, theirs)
+    terms = [own, swap(theirs, "core", 1)]
     layer_out, coeff_out, grad_layer, grad_down, mix_sums, mix_in_part, mix_out_part = mixing(
-        terms + send_sums(sums), hidden, down_bias.reshape(1, -1), mix_gain.reshape(1, -1),
+        terms + send_sums(chip_sums(*terms)), hidden, down_bias.reshape(1, -1), mix_gain.reshape(1, -1),
         mix_in, mix_out, out_grad, coeff_grad,
     )
 
@@ -1047,7 +1031,7 @@
         axis=0,
     )
     rounds = [("core", 1)]
-    for axis in ("row", "zl", "zh"):
+    for axis in ("row", "zh", "zl"):
         rounds += [(axis, 1 << bit) for bit in range(lax.axis_size(axis).bit_length() - 1)]
     beside, arrived = send_tokens(grad_down)
     (got,), (beside,) = together([swap(early, *rounds[0])], [beside])
@@ -1056,76 +1040,64 @@
     early = early + got
     grad_down_all = token_blocks(grad_down, beside, arrived)
     got = swap(early, *rounds[2])
-    down_wide = weight_grad(grad_down_all, act)
+    half_rank = lax.axis_index("zh").reshape(1)
+    down_wide = weight_grad(grad_down_all, act, feats, half_rank)
     got, down_wide, grad_down_all[0] = after(got, down_wide, grad_down_all[0])
     early = early + got
-    down_mine = scatter_rows(down_wide)
+    down_mine = scatter_weight(down_wide)
     got = swap(early, *rounds[3])
     grad_up, up_bias_part, (own, theirs) = feed(grad_down_all, (), feed_full, 1, slope, True)
     got, theirs, late_grad = after(got, theirs, grad_up[0])
     early = early + got
-    terms, sums = chip_sums(own, theirs)
-    arrived = send_sums(sums)
+    terms = [own, swap(theirs, "core", 1)]
+    arrived = send_sums(chip_sums(*terms))
+    up_wide = weight_grad(normed2_all, (late_grad, *grad_up[1:]), feats, half_rank)
+    (up_wide,), arrived = together([up_wide], arrived)
+    up_mine = scatter_weight(up_wide)
+    grad_hidden, grad_attn, mid_sums = middle_back(terms + arrived, hidden, grad_layer, ln_gain)
+    grad_attn_all = token_blocks(grad_attn, *send_tokens(grad_attn))
+    grad_heads = proj(grad_attn_all, attn_full, 3, cols)
     got = swap(early, *rounds[4])
-    up_wide = weight_grad(normed2_all, (late_grad, *grad_up[1:]))
-    (got, up_wide), arrived = together([got, up_wide], arrived)
+    grads, bias_sums = attend_back(scalars, query, kv, grad_heads, log_total, tables, group)
+    got, grads = after(got, grads)
     early = early + got
     for more in rounds[5:]:
         early = early + swap(early, *more)
-    up_mine = scatter_rows(up_wide)
-    grad_hidden, grad_attn, mid_sums = middle_back(terms + arrived, hidden, grad_layer, ln_gain)
-    grad_attn_all = token_blocks(grad_attn, *send_tokens(grad_attn))
-    grad_heads = proj(grad_attn_all, attn_full, 3, cols)
-    half_cols = down_mine.shape[1] // halves
-    down_parts = [
-        [down_mine[:, h * half_cols + n * half_cols // 2 : h * half_cols + (n + 1) * half_cols // 2] for n in range(2)]
-        for h in range(halves)
-    ]
-    crossing = [swap(down_parts[h][0], "zh", h) for h in range(1, halves)]
-    grads, bias_sums = attend_back(scalars, query, kv, grad_heads, log_total, tables, group)
-    early_parts, (grads,) = together(crossing, [grads])
-    crossing = [swap(down_parts[h][1], "zh", h) for h in range(1, halves)]
-    kv_terms, kv_sums = chip_sums(*unproj(grads, 1, 2, attn_full, 1, group))
-    own, theirs = unproj(grads, 0, 1, attn_full, 0, group)
-    late_parts, (own, theirs) = together(crossing, [own, theirs])
-    down_others = [
-        jnp.concatenate([a, b], axis=1) for a, b in zip(early_parts, late_parts)
-    ]
-    query_terms, query_sums = chip_sums(own, theirs)
-    (late_head, *kv_sums), query_sums = together([head, *kv_sums], query_sums)
+    query_own, theirs = unproj(grads, 0, 1, attn_full, 0, group)
+    grads, query_own = after(grads, query_own)
+    query_got = swap(theirs, "core", 1)
+    kv_own, theirs = unproj(grads, 1, 2, attn_full, 1, group)
+    query_got, kv_own = after(query_got, kv_own)
+    query_crossing = send_sums(chip_sums(query_own, query_got))
+    kv_got = swap(theirs, "core", 1)
+    kv_sums = chip_sums(kv_own, kv_got)
+    late_head, *kv_sums = after(head, *kv_sums)
+    kv_crossing = send_sums(kv_sums)
     attn_parts = piece_grad(
         rank, row_count, orders, query_all, kv_all, grads, grad_attn_all, late_head, halves
     )
-    kv_crossing, query_crossing = send_sums(kv_sums), send_sums(query_sums)
     norm = lambda streams, terms: norm_back(streams, terms, layer_stack, mix_flat, ln_gain)
     near = [attn_parts[p][0] for p in range(2)]
     far = [attn_parts[p][h] for h in range(1, halves) for p in range(2)]
     which = [p for h in range(1, halves) for p in range(2)]
     steps = len(orders[0])
     got = [send_half(v, orders[p][0]) for v, p in zip(far, which)]
-    got, (*kv_crossing, near[0], near[1]) = together(got, [*kv_crossing, *near])
+    query_grads, query_sums = norm((0,), [query_own, query_got, *query_crossing])
+    got, (query_grads, *near) = together(got, [query_grads, *near])
     far = [add_half(v, g).astype(BF) for v, g in zip(far, got)]
     got = [send_half(v, orders[p][1]) for v, p in zip(far, which)]
     near_got = [send_half(v, orders[p][0]) for p, v in enumerate(near)]
-    kv_grads, kv_sums = norm((1, 2), kv_terms + kv_crossing)
-    got, (kv_grads,) = together(got, [kv_grads])
+    got, kv_crossing = together(got, kv_crossing)
     far = [add_half(v, g).astype(BF) for v, g in zip(far, got)]
     for n in range(2, steps):
         got = [send_half(v, orders[p][n]) for v, p in zip(far, which)]
         far = [add_half(v, g).astype(BF) for v, g in zip(far, got)]
-    up_others = other_halves(up_mine, halves)
-    query_crossing, near_got = together(query_crossing, near_got)
+    attn_others = [swap(v, "zh", n // 2 + 1) for n, v in enumerate(far)]
+    kv_grads, kv_sums = norm((1, 2), [kv_own, kv_got, *kv_crossing])
+    near_got, (kv_grads,) = together(near_got, [kv_grads])
     near = [add_half(v, g) for v, g in zip(near, near_got)]
-    for n in range(1, steps):
-        near = [v.astype(BF) for v in near]
-        near_got = [send_half(v, orders[p][n]) for p, v in enumerate(near)]
-        if n == 1:
-            query_grads, query_sums = norm((0,), query_terms + query_crossing)
-            near_got, (query_grads, *up_others) = together(near_got, [query_grads, *up_others])
-        near = [add_half(v, g) for v, g in zip(near, near_got)]
     stream_grads = (query_grads, kv_grads, grad_hidden)
     sums = [query_sums[0], kv_sums[0], kv_sums[1]]
-    attn_others = [swap(v, "zh", n // 2 + 1) for n, v in enumerate(far)]
     mix_in_grad = early[:mixed].T
     down_bias_grad, mix_gain_grad = early[mixed], early[mixed + 1]
     mix_out_grad = early[mixed + 2, : mix_out.size].reshape(mix_out.shape)
@@ -1147,15 +1119,26 @@
             ],
             axis=0,
     )
-    late = tree(sum_parts(late, ("row",)))
-    late = tree(sum_parts(late, ("zl", "core")))
-    late = sum_parts(late, ("zh",))
+    near = [v.astype(BF) for v in near]
+    near_got = [send_half(v, orders[p][1]) for p, v in enumerate(near)]
+    got = swap(late, *rounds[1])
     stack_grad, coeffs_grad = stack_back(stream_grads, layer_stack, mix_flat)
-    late, (stack_grad, *attn_others) = together(late, [stack_grad, *attn_others])
-    late = tree(late)
-    half_cols = up_mine.shape[1] // halves
-    down_grad = total_grad(down_mine[:, :half_cols], down_others).T
-    up_grad = total_grad(up_mine[:, :half_cols], up_others)
+    (got, attn_others[0], *near_got), (stack_grad,) = together(
+        [got, attn_others[0], *near_got], [stack_grad]
+    )
+    late = late + got
+    got, attn_others[1] = after(swap(late, *rounds[2]), attn_others[1])
+    late = late + got
+    near = [add_half(v, g) for v, g in zip(near, near_got)]
+    for n in range(2, steps):
+        near = [v.astype(BF) for v in near]
+        near_got = [send_half(v, orders[p][n]) for p, v in enumerate(near)]
+        near = [add_half(v, g) for v, g in zip(near, near_got)]
+    rest = rounds[3:] + rounds[:1]
+    for more in [r for r in rest if r[0] != "zh"] + [r for r in rest if r[0] == "zh"]:
+        late = late + swap(late, *more)
+    down_grad = down_mine.astype(F32).T
+    up_grad = up_mine.astype(F32)
     attn_grad = [total_grad(near[p], attn_others[p::2]) for p in range(2)]
     qkv_grad = jnp.stack(
         [attn_grad[0][:, :cols], attn_grad[0][:, cols:], attn_grad[1][:, :cols]], axis=0

time: 839 us -> 805 us (0.959)
  local copies, waits for them, and re-layouts: 55.7 us -> 39.5 us
    ppermute x7 -> x0, waiting for transfers between devices: 16.1 us -> none  [sum_parts(): lax.ppermute(values, axes, [(i, i ^ k) for i in range(size)])]
    ppermute x46 -> x48, waiting for transfers between devices: 377 us -> 380 us  [swap(): return lax.ppermute(values, axis, [(i, i ^ bits) for i in range(size)])]
    unnamed x103 -> x105, local copies, waits for them, and re-layouts: 19.3 us -> 16.9 us
    ppermute x46 -> x48, starting transfers between devices: 40.5 us -> 38.6 us  [swap(): return lax.ppermute(values, axis, [(i, i ^ bits) for i in range(size)])]
    convert_element_type x5 -> x6, other arithmetic: 17 us -> 17 us  [the longest x5 14.2 us: chip_sums(): (own[k].astype(F32) + got[k].astype(F32)).astype(BF)]
  transfers between devices with their start and end apart: 59 -> 56, of which waited for: 33 -> 28; matrix products, arithmetic and copies ran while one was open for 9% -> 8% of each run, Pallas kernels for 27% -> 29%
where the time goes in v3:
time: 805 us; the launch traced here: 793 us
  waiting for transfers between devices  396 us (49%)
  Pallas kernels  260 us (32%)
  other arithmetic  43 us (5%)
  local copies, waits for them, and re-layouts  39.5 us (5%)
  starting transfers between devices  39.3 us (5%)
  between operations  15.3 us (2%)
    ppermute x48, waiting for transfers between devices, swap(): return lax.ppermute(values, axis, [(i, i ^ bits) for i in range(size)])  380 us
    pallas_call x2, Pallas kernels, feed(): pl.pallas_call(functools.partial(feed_kernel, blocks, ready, [per] * halv...  48.2 us
    ppermute x48, starting transfers between devices, swap(): return lax.ppermute(values, axis, [(i, i ^ bits) for i in range(size)])  38.6 us
    pallas_call x2, Pallas kernels, weight_grad(): pl.pallas_call(functools.partial(weight_grad_kernel, len(lefts), halves),...  27.2 us
    pallas_call x2, Pallas kernels, norm_back(): pl.pallas_call(functools.partial(norm_back_kernel, streams, len(parts)),...  25.7 us
    pallas_call x3, Pallas kernels, unproj(): pl.pallas_call(unproj_kernel, grid=(count, width // tile), in_specs=[pl.B...  23.9 us
    pallas_call x1, Pallas kernels, attend_back(): pl.pallas_call(functools.partial(attend_back_kernel, blocks), grid=(heads...  18.1 us
    pallas_call x1, Pallas kernels, stack_back(): pl.pallas_call(stack_back_kernel, grid=(tokens // tile,), in_specs=[pl.Bl...  17.2 us
  transfers between devices with their start and end apart: 56, of which 28 were waited for; matrix products, arithmetic and copies ran while one was open for 8% of the time, Pallas kernels for 29%

profile of v3, /device:TPU:0, one launch (start us, length us, event | category | flops | bytes accessed | tf_op | source)
XLA Modules:
  0.0 792.5 jit_solution(10183594070801681942)
XLA Ops:
  16.9 13.2 %front.1 = (bf16[1,256,2048]{2,1,0:T(8,128)(2,1)}, bf16[2,256,2048]{2,1,0:T(8,128)(2,1)}, f32[256,2048]{1,0:T(8,128)}) custom-call(bf16[8,256,2048]{2,1,0:T(8,128)(2,1)} %refs_3_.5, f32[256,32]{1,0:T(8,128)} %copy.80.mix_ref.refs_4_, f32[4,2048]{1,0:T(4,128)} %refs_5_.7, f32[4,2048]{1,0:T(4,128)} %refs_6_.2), custom_call_target="tpu_custom_call" | custom-call | flops 293601280 | bytes 109051904 | tf_op jit(solution)/shard_map/front/pallas_call | solution.py:85
  32.8 42.4 %collective-permute-done.5.refs_2_ = bf16[1,256,2048]{2,1,0:T(8,128)(2,1)} collective-permute-done((bf16[1,256,2048]{2,1,0:T(8,128)(2,1)}, bf16[1,256,2048]{2,1,0:T(8,128)(2,1)}, u32[]{:S(2)}, u32[]{:S(2)}) %collective-permute-start.5) | collective-permute-done | bytes 1048608 | tf_op jit(solution)/shard_map/ppermute | solution.py:874
  91.8 83.0 %collective-permute-done = bf16[512,2048]{1,0:T(8,128)(2,1)} collective-permute-done((bf16[512,2048]{1,0:T(8,128)(2,1)S(1)}, bf16[512,2048]{1,0:T(8,128)(2,1)}, u32[]{:S(2)}, u32[]{:S(2)}) %collective-permute-start) | collective-permute-done | bytes 2097184 | tf_op jit(solution)/shard_map/ppermute | solution.py:874
  178.3 6.8 qkv_proj.2.query_ref
  186.4 10.4 %qkv_proj.3.kv_ref = bf16[2,1024,512]{2,1,0:T(8,128)(2,1)} custom-call(bf16[2,256,2048]{2,1,0:T(8,128)(2,1)} %get-tuple-element.115.refs_0_.refs_4_, bf16[2,256,2048]{2,1,0:T(8,128)(2,1)} %collective-permute-done.7.refs_1_.refs_5_, bf16[2,256,2048]{2,1,0:T(8,128)(2,1)} %collective-permute-done.1.refs_2_.refs_6_, bf16[2,256,2048]{2,1,0:T(8,128)(2,1)} %copy-done.11, ...), custom_call_target="tpu_custom_call" | custom-call | flops 34359738368 | bytes 83886080 | tf_op jit(solution)/shard_map/qkv_proj/pallas_call | solution.py:270
  196.8 14.4 %attend.1 = (bf16[1,1024,512]{2,1,0:T(8,128)(2,1)}, f32[4,1,1024]{2,1,0:T(1,128)}) custom-call(s32[5]{0:T(128)} %pad_add_fusion.1.scalars, bf16[1,1024,512]{2,1,0:T(8,128)(2,1)} %qkv_proj.2.query_ref, bf16[2,1024,512]{2,1,0:T(8,128)(2,1)} %qkv_proj.3.kv_ref), custom_call_target="tpu_custom_call" | custom-call | flops 34359738368 | bytes 33685504 | tf_op jit(solution)/shard_map/attend/pallas_call | solution.py:382
  224.7 25.3 %collective-permute-done.10.refs_2_ = bf16[1,256,2048]{2,1,0:T(8,128)(2,1)S(1)} collective-permute-done((bf16[1,256,2048]{2,1,0:T(8,128)(2,1)S(1)}, bf16[1,256,2048]{2,1,0:T(8,128)(2,1)S(1)}, u32[]{:S(2)}, u32[]{:S(2)}) %collective-permute-start.10) | collective-permute-done | bytes 1048608 | tf_op jit(solution)/shard_map/ppermute | solution.py:874
  256.4 24.6 %collective-permute-done.12.refs_2_ = bf16[256,2048]{1,0:T(8,128)(2,1)S(1)} collective-permute-done((bf16[256,2048]{1,0:T(8,128)(2,1)}, bf16[256,2048]{1,0:T(8,128)(2,1)S(1)}, u32[]{:S(2)}, u32[]{:S(2)}) %collective-permute-start.12) | collective-permute-done | bytes 1048608 | tf_op jit(solution)/shard_map/ppermute | solution.py:874
  284.7 9.9 %expand.1 = (bf16[1024,1024]{1,0:T(8,128)(2,1)}, bf16[1024,1024]{1,0:T(8,128)(2,1)}) custom-call(bf16[256,2048]{1,0:T(8,128)(2,1)} %get-tuple-element.132.refs_0_, bf16[256,2048]{1,0:T(8,128)(2,1)} %copy-done.42, bf16[256,2048]{1,0:T(8,128)(2,1)} %copy-done.41, bf16[256,2048]{1,0:T(8,128)(2,1)} %copy-done.43, ...), custom_call_target="tpu_custom_call" | custom-call | flops 34359738368 | bytes 67108864 | tf_op jit(solution)/shard_map/expand/pallas_call | solution.py:596
  294.6 15.8 %all-gather.11.cloned.1.call-done.refs_5_.refs_8_.refs_9_ = bf16[2048,2048]{1,0:T(8,128)(2,1)} async-done(((bf16[512,2048]{1,0:T(8,128)(2,1)}), bf16[2048,2048]{1,0:T(8,128)(2,1)}) %all-gather.11.cloned.1.call-update) | async-done | bytes 8388624 | tf_op jit(solution)/shard_map/all_gather | solution.py:931
  310.4 21.4 %feed.1 = (bf16[1024,1024]{1,0:T(8,128)(2,1)}, bf16[1024,1024]{1,0:T(8,128)(2,1)}, bf16[2,1,256,2048]{3,2,1,0:T(8,128)(2,1)}, bf16[2,1,256,2048]{3,2,1,0:T(8,128)(2,1)}) custom-call(bf16[256,2048]{1,0:T(8,128)(2,1)} %get-tuple-element.132.refs_0_, bf16[256,2048]{1,0:T(8,128)(2,1)} %copy-done.42, bf16[256,2048]{1,0:T(8,128)(2,1)} %copy-done.41, ...), custom_call_target="tpu_custom_call" | custom-call | flops 103079215104 | bytes 100663296 | tf_op jit(solution)/shard_map/feed/pallas_call | solution.py:681
  342.2 21.7 %collective-permute-done.15.refs_2_ = bf16[1,256,2048]{2,1,0:T(8,128)(2,1)} collective-permute-done((bf16[1,256,2048]{2,1,0:T(8,128)(2,1)S(1)}, bf16[1,256,2048]{2,1,0:T(8,128)(2,1)}, u32[]{:S(2)}, u32[]{:S(2)}) %collective-permute-start.15) | collective-permute-done | bytes 1048608 | tf_op jit(solution)/shard_map/ppermute | solution.py:874
  363.9 10.9 %mixing.1 = (f32[256,2048]{1,0:T(8,128)}, f32[256,36]{1,0:T(8,128)}, f32[256,2048]{1,0:T(8,128)}, bf16[256,2048]{1,0:T(8,128)(2,1)}, f32[8,2048]{1,0:T(8,128)}, /*index=5*/f32[36,2048]{1,0:T(8,128)}, f32[36,36]{1,0:T(8,128)}) custom-call(bf16[2,1,256,2048]{3,2,1,0:T(8,128)(2,1)} %get-tuple-element.136.refs_0_, bf16[2,1,256,2048]{3,2,1,0:T(8,128)(2,1)} %copy-done.25, ...), custom_call_target="tpu_custom_call" | custom-call | flops 12582912000 | bytes 112271872 | tf_op jit(solution)/shard_map/mixing/pallas_call | solution.py:857
  382.5 21.1 %collective-permute-done.19.refs_2_ = bf16[256,2048]{1,0:T(8,128)(2,1)S(1)} collective-permute-done((bf16[256,2048]{1,0:T(8,128)(2,1)}, bf16[256,2048]{1,0:T(8,128)(2,1)S(1)}, u32[]{:S(2)}, u32[]{:S(2)}) %collective-permute-start.19) | collective-permute-done | bytes 1048608 | tf_op jit(solution)/shard_map/ppermute | solution.py:874
  407.2 13.6 %weight_grad.2 = bf16[4,2,512,1024]{3,2,1,0:T(8,128)(2,1)} custom-call(bf16[256,2048]{1,0:T(8,128)(2,1)} %get-tuple-element.151.refs_0_, bf16[256,2048]{1,0:T(8,128)(2,1)} %copy-done.44, bf16[256,2048]{1,0:T(8,128)(2,1)} %copy-done.45, bf16[256,2048]{1,0:T(8,128)(2,1)} %copy-done.46, bf16[1024,1024]{1,0:T(8,128)(2,1)} %get-tuple-element.134.refs_4_, ...), custom_call_target="tpu_custom_call" | custom-call | flops 68719476736 | bytes 134217728 | tf_op jit(solution)/shard_map/weight_grad/pallas_call | solution.py:715
  423.4 26.9 %feed_back.1 = (bf16[1024,1024]{1,0:T(8,128)(2,1)}, bf16[1024,1024]{1,0:T(8,128)(2,1)}, f32[1,1024]{1,0:T(1,128)}, f32[1,1024]{1,0:T(1,128)}, bf16[2,1,256,2048]...) custom-call(bf16[256,2048]{1,0:T(8,128)(2,1)} %get-tuple-element.151.refs_0_, bf16[256,2048]{1,0:T(8,128)(2,1)} %copy-done.44, ...), custom_call_target="tpu_custom_call" | custom-call | flops 137438953472 | bytes 100728832 | tf_op jit(solution)/shard_map/feed_back/pallas_call | solution.py:681
  459.6 13.6 %weight_grad.3 = bf16[4,2,512,1024]{3,2,1,0:T(8,128)(2,1)} custom-call(bf16[256,2048]{1,0:T(8,128)(2,1)} %get-tuple-element.132.refs_0_, bf16[256,2048]{1,0:T(8,128)(2,1)} %copy-done.42, bf16[256,2048]{1,0:T(8,128)(2,1)} %copy-done.41, bf16[256,2048]{1,0:T(8,128)(2,1)} %copy-done.43, bf16[1024,1024]{1,0:T(8,128)(2,1)} %get-tuple-element.159.refs_4_, ...), custom_call_target="tpu_custom_call" | custom-call | flops 68719476736 | bytes 134217728 | tf_op jit(solution)/shard_map/weight_grad/pallas_call | solution.py:715
  473.2 10.3 %collective-permute-done.25.refs_2_ = bf16[1,256,2048]{2,1,0:T(8,128)(2,1)S(1)} collective-permute-done((bf16[1,256,2048]{2,1,0:T(8,128)(2,1)}, bf16[1,256,2048]{2,1,0:T(8,128)(2,1)S(1)}, u32[]{:S(2)}, u32[]{:S(2)}) %collective-permute-start.25) | collective-permute-done | bytes 1048608 | tf_op jit(solution)/shard_map/ppermute | solution.py:874
  484.5 6.6 middle_back.1
  492.8 22.9 %collective-permute-done.27.refs_2_.refs_10_ = bf16[256,2048]{1,0:T(8,128)(2,1)S(1)} collective-permute-done((bf16[256,2048]{1,0:T(8,128)(2,1)}, bf16[256,2048]{1,0:T(8,128)(2,1)S(1)}, u32[]{:S(2)}, u32[]{:S(2)}) %collective-permute-start.27) | collective-permute-done | bytes 1048608 | tf_op jit(solution)/shard_map/ppermute | solution.py:874
  525.5 18.1 %attend_back.1 = (bf16[3,1024,512]{2,1,0:T(8,128)(2,1)}, f32[4,8,128]{2,1,0:T(8,128)}) custom-call(s32[5]{0:T(128)} %pad_add_fusion.1.scalars, bf16[1,1024,512]{2,1,0:T(8,128)(2,1)} %qkv_proj.2.query_ref, bf16[2,1024,512]{2,1,0:T(8,128)(2,1)} %qkv_proj.3.kv_ref, bf16[1024,512]{1,0:T(8,128)(2,1)} %proj.1.g_ref, f32[4,1,1024]{2,1,0:T(1,128)} %get-tuple-element.164.log_ref, ...), custom_call_target="tpu_custom_call" | custom-call | flops 68719476736 | bytes 58851328 | tf_op jit(solution)/shard_map/attend_back/pallas_call | solution.py:445
  550.1 11.5 %unproj.5 = (bf16[2,2,256,2048]{3,2,1,0:T(8,128)(2,1)}, bf16[2,2,256,2048]{3,2,1,0:T(8,128)(2,1)}) custom-call(bf16[3,1024,512]{2,1,0:T(8,128)(2,1)} %get-tuple-element.170.a_ref.refs_12_, bf16[2048,1024]{1,0:T(8,128)(2,1)} %all-gather.5.cloned.1.call-done.refs_4_.refs_0_, bf16[2048,1024]{1,0:T(8,128)(2,1)} %all-gather.7.cloned.1.call-done.refs_5_.refs_1_), custom_call_target="tpu_custom_call" | custom-call | flops 34359738368 | bytes 67108864 | tf_op jit(solution)/shard_map/unproj/pallas_call | solution.py:337
  580.1 16.1 %piece_grad.1 = (bf16[2048,512]{1,0:T(8,128)(2,1)}, bf16[2048,512]{1,0:T(8,128)(2,1)}, bf16[2048,512]{1,0:T(8,128)(2,1)}, bf16[2048,512]{1,0:T(8,128)(2,1)}) custom-call(s32[3,4]{1,0:T(4,128)} %pad_add_fusion.table, bf16[1,256,2048]{2,1,0:T(8,128)(2,1)} %get-tuple-element.119.refs_0_, bf16[1,256,2048]{2,1,0:T(8,128)(2,1)} %collective-permute-done.2.refs_1_, ...), custom_call_target="tpu_custom_call" | custom-call | flops 429496736 | bytes 1468006 | tf_op jit(solution)/shard_map/piece_grad/pallas_call | solution.py:773
  601.7 11.8 %norm_back.2 = (f32[1,256,2048]{2,1,0:T(8,128)}, f32[1,16,2048]{2,1,0:T(8,128)}) custom-call(bf16[2,1,256,2048]{3,2,1,0:T(8,128)(2,1)} %get-tuple-element.168.refs_0_, bf16[2,1,256,2048]{3,2,1,0:T(8,128)(2,1)} %collective-permute-done.29.refs_1_, bf16[1,256,2048]{2,1,0:T(8,128)(2,1)} %collective-permute-done.30.refs_2_, bf16[8,256,2048]{2,1,0:T(8,128)(2,1)} %refs_3_.5, ...), custom_call_target="tpu_custom_call" | custom-call | flops 1048576 | bytes 792985 | tf_op jit(solution)/shard_map/norm_back/pallas_call | solution.py:154
  613.5 9.1 %collective-permute-done.32 = bf16[1024,512]{1,0:T(8,128)(2,1)S(1)} collective-permute-done((bf16[1024,512]{1,0:T(8,128)(2,1)S(1)}, bf16[1024,512]{1,0:T(8,128)(2,1)S(1)}, u32[]{:S(2)}, u32[]{:S(2)}) %collective-permute-start.32) | collective-permute-done | bytes 1048608 | tf_op jit(solution)/shard_map/ppermute | solution.py:874
  640.2 21.8 %collective-permute-done.35 = bf16[512,512]{1,0:T(8,128)(2,1)S(1)} collective-permute-done((bf16[512,512]{1,0:T(8,128)(2,1)S(1)}, bf16[512,512]{1,0:T(8,128)(2,1)S(1)}, u32[]{:S(2)}, u32[]{:S(2)}) %collective-permute-start.35) | collective-permute-done | bytes 524320 | tf_op jit(solution)/shard_map/ppermute | solution.py:874
  662.1 12.3 %collective-permute-done.36.refs_2_ = bf16[2,256,2048]{2,1,0:T(8,128)(2,1)} collective-permute-done((bf16[2,256,2048]{2,1,0:T(8,128)(2,1)}, bf16[2,256,2048]{2,1,0:T(8,128)(2,1)}, u32[]{:S(2)}, u32[]{:S(2)}) %collective-permute-start.36) | collective-permute-done | bytes 2097184 | tf_op jit(solution)/shard_map/ppermute | solution.py:874
  678.6 13.9 %norm_back.3 = (f32[2,256,2048]{2,1,0:T(8,128)}, f32[2,16,2048]{2,1,0:T(8,128)}) custom-call(bf16[2,2,256,2048]{3,2,1,0:T(8,128)(2,1)} %get-tuple-element.174.refs_0_, bf16[2,2,256,2048]{3,2,1,0:T(8,128)(2,1)} %collective-permute-done.31.refs_1_, bf16[2,256,2048]{2,1,0:T(8,128)(2,1)} %collective-permute-done.36.refs_2_, bf16[8,256,2048]{2,1,0:T(8,128)(2,1)} %refs_3_.5, ...), custom_call_target="tpu_custom_call" | custom-call | flops 2097152 | bytes 1166540 | tf_op jit(solution)/shard_map/norm_back/pallas_call | solution.py:154
  700.1 17.2 %stack_back.1 = (f32[8,256,2048]{2,1,0:T(8,128)}, f32[256,32]{1,0:T(8,128)}) custom-call(f32[1,256,2048]{2,1,0:T(8,128)} %get-tuple-element.197.refs_0_, f32[2,256,2048]{2,1,0:T(8,128)} %get-tuple-element.198.refs_1_, f32[256,2048]{1,0:T(8,128)} %get-tuple-element.199.refs_2_, bf16[8,256,2048]{2,1,0:T(8,128)(2,1)} %refs_3_.5, f32[256,32]{1,0:T(8,128)} %copy.80.mix_ref.refs_4_), custom_call_target="tpu_custom_call" | custom-call | flops 545259520 | bytes 268697600 | tf_op jit(solution)/shard_map/stack_back/pallas_call | solution.py:208
  721.3 16.9 %collective-permute-done.38 = bf16[512,512]{1,0:T(8,128)(2,1)} collective-permute-done((bf16[512,512]{1,0:T(8,128)(2,1)}, bf16[512,512]{1,0:T(8,128)(2,1)}, u32[]{:S(2)}, u32[]{:S(2)}) %collective-permute-start.38) | collective-permute-done | bytes 524320 | tf_op jit(solution)/shard_map/ppermute | solution.py:874
  740.2 16.0 %collective-permute-done.44 = bf16[512,512]{1,0:T(8,128)(2,1)S(1)} collective-permute-done((bf16[512,512]{1,0:T(8,128)(2,1)S(1)}, bf16[512,512]{1,0:T(8,128)(2,1)S(1)}, u32[]{:S(2)}, u32[]{:S(2)}) %collective-permute-start.44) | collective-permute-done | bytes 524320 | tf_op jit(solution)/shard_map/ppermute | solution.py:874
  766.1 10.5 %collective-permute-done.47 = f32[17,2048]{1,0:T(8,128)S(1)} collective-permute-done((f32[17,2048]{1,0:T(8,128)S(1)}, f32[17,2048]{1,0:T(8,128)S(1)}, u32[]{:S(2)}, u32[]{:S(2)}) %collective-permute-start.47) | collective-permute-done | bytes 139296 | tf_op jit(solution)/shard_map/ppermute | solution.py:874
  (297 shorter events, 187.2 us)
Async XLA Ops:
  7.2 171.1 %all-gather.5.cloned.1.call-start = ((), (), s32[]{:S(2)}) async-start(), calls=%async_computation.4 | async-start | bytes 5242880 | tf_op jit(solution)/shard_map/all_gather | solution.py:931
  16.1 162.3 %all-gather.7.cloned.1.call-start = ((), (), s32[]{:S(2)}) async-start(), calls=%async_computation.5 | async-start | bytes 5242880 | tf_op jit(solution)/shard_map/all_gather | solution.py:931
  30.0 45.2 %collective-permute-start.5 = (bf16[1,256,2048]{2,1,0:T(8,128)(2,1)}, bf16[1,256,2048]{2,1,0:T(8,128)(2,1)}, u32[]{:S(2)}, u32[]{:S(2)}) collective-permute-start(bf16[1,256,2048]{2,1,0:T(8,128)(2,1)} %get-tuple-element.119.refs_0_), channel_id=1, source_target_pairs={{0,2},{2,0},{1,3},{3,1},{4,6},{6,4},{5,7},{7,5},{8,10},{10,8},{9,1... | collective-permute-start | bytes 3145736 | tf_op jit(solution)/shard_map/ppermute | solution.py:874
  31.6 47.8 %collective-permute-start.4 = (bf16[512,1024]{1,0:T(8,128)(2,1)S(1)}, bf16[512,1024]{1,0:T(8,128)(2,1)S(1)}, u32[]{:S(2)}, u32[]{:S(2)}) collective-permute-start(bf16[512,1024]{1,0:T(8,128)(2,1)S(1)} %copy-done.4), channel_id=1, source_target_pairs={{0,4},{4,0},{1,5},{5,1},{2,6},{6,2},{3,7},{7,3},{8,12},{12,8},{9,1... | collective-permute-start | bytes 3145736 | tf_op jit(solution)/shard_map/ppermute | solution.py:874
  80.5 203.2 %all-gather.9.cloned.1.call-start = ((), (), s32[]{:S(2)}) async-start(), calls=%async_computation.6 | async-start | bytes 10485760 | tf_op jit(solution)/shard_map/all_gather | solution.py:931
  83.9 226.5 %all-gather.11.cloned.1.call-start = ((), (), s32[]{:S(2)}) async-start(), calls=%async_computation.7 | async-start | bytes 10485760 | tf_op jit(solution)/shard_map/all_gather | solution.py:931
  85.6 89.2 %collective-permute-start = (bf16[512,2048]{1,0:T(8,128)(2,1)S(1)}, bf16[512,2048]{1,0:T(8,128)(2,1)}, u32[]{:S(2)}, u32[]{:S(2)}) collective-permute-start(bf16[512,2048]{1,0:T(8,128)(2,1)S(1)} %copy-done), channel_id=1, source_target_pairs={{0,4},{4,0},{1,5},{5,1},{2,6},{6,2},{3,7},{7,3},{8,12},{12,8},{9,1... | collective-permute-start | bytes 6291464 | tf_op jit(solution)/shard_map/ppermute | solution.py:874
  85.9 91.2 %collective-permute-start.1 = (bf16[2,256,2048]{2,1,0:T(8,128)(2,1)}, bf16[2,256,2048]{2,1,0:T(8,128)(2,1)}, u32[]{:S(2)}, u32[]{:S(2)}) collective-permute-start(bf16[2,256,2048]{2,1,0:T(8,128)(2,1)} %get-tuple-element.115.refs_0_.refs_4_), channel_id=1, source_target_pairs={{0,2},{2,0},{1,3},{3,1},{4,6},{6,4},{5,7},{7,5},{8,10},{10,8},{9,1... | collective-permute-start | bytes 6291464 | tf_op jit(solution)/shard_map/ppermute | solution.py:874
  85.9 92.4 %collective-permute-start.2 = (bf16[1,256,2048]{2,1,0:T(8,128)(2,1)S(1)}, bf16[1,256,2048]{2,1,0:T(8,128)(2,1)}, u32[]{:S(2)}, u32[]{:S(2)}) collective-permute-start(bf16[1,256,2048]{2,1,0:T(8,128)(2,1)S(1)} %copy-done.20), channel_id=1, source_target_pairs={{0,1},{1,0},{2,3},{3,2},{4,5},{5,4},{6,7},{7,6},{8,9},{9,8},{10,11... | collective-permute-start | bytes 3145736 | tf_op jit(solution)/shard_map/ppermute | solution.py:874
  85.9 99.2 %collective-permute-start.7 = (bf16[2,256,2048]{2,1,0:T(8,128)(2,1)}, bf16[2,256,2048]{2,1,0:T(8,128)(2,1)}, u32[]{:S(2)}, u32[]{:S(2)}) collective-permute-start(bf16[2,256,2048]{2,1,0:T(8,128)(2,1)} %get-tuple-element.115.refs_0_.refs_4_), channel_id=1, source_target_pairs={{0,1},{1,0},{2,3},{3,2},{4,5},{5,4},{6,7},{7,6},{8,9},{9,8},{10,11... | collective-permute-start | bytes 6291464 | tf_op jit(solution)/shard_map/ppermute | solution.py:874
  87.1 91.2 %collective-permute-start.6 = (bf16[1,256,2048]{2,1,0:T(8,128)(2,1)}, bf16[1,256,2048]{2,1,0:T(8,128)(2,1)}, u32[]{:S(2)}, u32[]{:S(2)}) collective-permute-start(bf16[1,256,2048]{2,1,0:T(8,128)(2,1)} %collective-permute-done.5.refs_2_), channel_id=1, source_target_pairs={{0,1},{1,0},{2,3},{3,2},{4,5},{5,4},{6,7},{7,6},{8,9},{9,8},{10,11... | collective-permute-start | bytes 3145736 | tf_op jit(solution)/shard_map/ppermute | solution.py:874
  211.2 350.9 %reduce-scatter.15.cloned.1.call-start = ((), (), s32[]{:S(2)}) async-start(), calls=%async_computation.11 | async-start | bytes 10485760
  224.5 25.5 %collective-permute-start.10 = (bf16[1,256,2048]{2,1,0:T(8,128)(2,1)S(1)}, bf16[1,256,2048]{2,1,0:T(8,128)(2,1)S(1)}, u32[]{:S(2)}, u32[]{:S(2)}) collective-permute-start(bf16[1,256,2048]{2,1,0:T(8,128)(2,1)S(1)} %fusion.1), channel_id=1, source_target_pairs={{0,2},{2,0},{1,3},{3,1},{4,6},{6,4},{5,7},{7,5},{8,10},{10,8},{9,1... | collective-permute-start | bytes 3145736 | tf_op jit(solution)/shard_map/ppermute | solution.py:874
  256.4 25.3 %collective-permute-start.11 = (bf16[256,2048]{1,0:T(8,128)(2,1)}, bf16[256,2048]{1,0:T(8,128)(2,1)S(1)}, u32[]{:S(2)}, u32[]{:S(2)}) collective-permute-start(bf16[256,2048]{1,0:T(8,128)(2,1)} %get-tuple-element.132.refs_0_), channel_id=1, source_target_pairs={{0,1},{1,0},{2,3},{3,2},{4,5},{5,4},{6,7},{7,6},{8,9},{9,8},{10,11... | collective-permute-start | bytes 3145736 | tf_op jit(solution)/shard_map/ppermute | solution.py:874
  338.6 25.4 %collective-permute-start.15 = (bf16[1,256,2048]{2,1,0:T(8,128)(2,1)S(1)}, bf16[1,256,2048]{2,1,0:T(8,128)(2,1)}, u32[]{:S(2)}, u32[]{:S(2)}) collective-permute-start(bf16[1,256,2048]{2,1,0:T(8,128)(2,1)S(1)} %fusion.2), channel_id=1, source_target_pairs={{0,2},{2,0},{1,3},{3,1},{4,6},{6,4},{5,7},{7,5},{8,10},{10,8},{9,1... | collective-permute-start | bytes 3145736 | tf_op jit(solution)/shard_map/ppermute | solution.py:874
  378.2 25.4 %collective-permute-start.19 = (bf16[256,2048]{1,0:T(8,128)(2,1)}, bf16[256,2048]{1,0:T(8,128)(2,1)S(1)}, u32[]{:S(2)}, u32[]{:S(2)}) collective-permute-start(bf16[256,2048]{1,0:T(8,128)(2,1)} %get-tuple-element.151.refs_0_), channel_id=1, source_target_pairs={{0,2},{2,0},{1,3},{3,1},{4,6},{6,4},{5,7},{7,5},{8,10},{10,8},{9,1... | collective-permute-start | bytes 3145736 | tf_op jit(solution)/shard_map/ppermute | solution.py:874
  420.8 29.4 %collective-permute-start.22 = (f32[39,2048]{1,0:T(8,128)S(1)}, f32[39,2048]{1,0:T(8,128)S(1)}, u32[]{:S(2)}, u32[]{:S(2)}) collective-permute-start(f32[39,2048]{1,0:T(8,128)S(1)} %add.177), channel_id=1, source_target_pairs={{0,4},{4,0},{1,5},{5,1},{2,6},{6,2},{3,7},{7,3},{8,12},{12,8},{9,1... | collective-permute-start | bytes 958472 | tf_op jit(solution)/shard_map/ppermute | solution.py:874
  423.3 206.5 %reduce-scatter.13.cloned.1.call-start = ((), (), s32[]{:S(2)}) async-start(), calls=%async_computation.10 | async-start | bytes 10485760
  458.1 25.4 %collective-permute-start.25 = (bf16[1,256,2048]{2,1,0:T(8,128)(2,1)}, bf16[1,256,2048]{2,1,0:T(8,128)(2,1)S(1)}, u32[]{:S(2)}, u32[]{:S(2)}) collective-permute-start(bf16[1,256,2048]{2,1,0:T(8,128)(2,1)} %fusion.3), channel_id=1, source_target_pairs={{0,2},{2,0},{1,3},{3,1},{4,6},{6,4},{5,7},{7,5},{8,10},{10,8},{9,1... | collective-permute-start | bytes 3145736 | tf_op jit(solution)/shard_map/ppermute | solution.py:874
  492.7 286.5 %reduce-scatter.11.cloned.1.call-start = ((), (), s32[]{:S(2)}) async-start(), calls=%async_computation.9 | async-start | bytes 3145728 | tf_op jit(solution)/shard_map/reduce_scatter | solution.py:936
  515.8 27.8 %collective-permute-start.23 = (f32[39,2048]{1,0:T(8,128)S(1)}, f32[39,2048]{1,0:T(8,128)S(1)}, u32[]{:S(2)}, u32[]{:S(2)}) collective-permute-start(f32[39,2048]{1,0:T(8,128)S(1)} %add.178), channel_id=1, source_target_pairs={{0,2},{2,0},{1,3},{3,1},{4,6},{6,4},{5,7},{7,5},{8,10},{10,8},{9,1... | collective-permute-start | bytes 958472 | tf_op jit(solution)/shard_map/ppermute | solution.py:874
  562.1 220.3 %reduce-scatter.9.cloned.1.call-start = ((), (), s32[]{:S(2)}) async-start(), calls=%async_computation.8 | async-start | bytes 3145728 | tf_op jit(solution)/shard_map/reduce_scatter | solution.py:936
  573.8 27.9 %collective-permute-start.30 = (bf16[1,256,2048]{2,1,0:T(8,128)(2,1)S(1)}, bf16[1,256,2048]{2,1,0:T(8,128)(2,1)}, u32[]{:S(2)}, u32[]{:S(2)}) collective-permute-start(bf16[1,256,2048]{2,1,0:T(8,128)(2,1)S(1)} %fusion.4), channel_id=1, source_target_pairs={{0,2},{2,0},{1,3},{3,1},{4,6},{6,4},{5,7},{7,5},{8,10},{10,8},{9,1... | collective-permute-start | bytes 3145736 | tf_op jit(solution)/shard_map/ppermute | solution.py:874
  597.6 25.0 %collective-permute-start.32 = (bf16[1024,512]{1,0:T(8,128)(2,1)S(1)}, bf16[1024,512]{1,0:T(8,128)(2,1)S(1)}, u32[]{:S(2)}, u32[]{:S(2)}) collective-permute-start(bf16[1024,512]{1,0:T(8,128)(2,1)S(1)} %slice.195), channel_id=1, source_target_pairs={{0,8},{8,0},{16,24},{24,16},{1,9},{9,1},{17,25},{25,17},{2,10},{10... | collective-permute-start | bytes 3145736 | tf_op jit(solution)/shard_map/ppermute | solution.py:874
  600.3 74.1 %collective-permute-start.36 = (bf16[2,256,2048]{2,1,0:T(8,128)(2,1)}, bf16[2,256,2048]{2,1,0:T(8,128)(2,1)}, u32[]{:S(2)}, u32[]{:S(2)}) collective-permute-start(bf16[2,256,2048]{2,1,0:T(8,128)(2,1)} %fusion), channel_id=1, source_target_pairs={{0,2},{2,0},{1,3},{3,1},{4,6},{6,4},{5,7},{7,5},{8,10},{10,8},{9,1... | collective-permute-start | bytes 6291464 | tf_op jit(solution)/shard_map/ppermute | solution.py:874
  627.1 65.5 %collective-permute-start.39 = (bf16[1024,512]{1,0:T(8,128)(2,1)}, bf16[1024,512]{1,0:T(8,128)(2,1)}, u32[]{:S(2)}, u32[]{:S(2)}) collective-permute-start(bf16[1024,512]{1,0:T(8,128)(2,1)} %slice.211), channel_id=1, source_target_pairs={{0,8},{8,0},{16,24},{24,16},{1,9},{9,1},{17,25},{25,17},{2,10},{10... | collective-permute-start | bytes 3145736 | tf_op jit(solution)/shard_map/ppermute | solution.py:874
  629.2 63.4 %collective-permute-start.40 = (bf16[1024,512]{1,0:T(8,128)(2,1)}, bf16[1024,512]{1,0:T(8,128)(2,1)}, u32[]{:S(2)}, u32[]{:S(2)}) collective-permute-start(bf16[1024,512]{1,0:T(8,128)(2,1)} %slice.212), channel_id=1, source_target_pairs={{0,16},{8,24},{16,0},{24,8},{1,17},{9,25},{17,1},{25,9},{2,18},{10... | collective-permute-start | bytes 3145736 | tf_op jit(solution)/shard_map/ppermute | solution.py:874
  631.4 30.7 %collective-permute-start.35 = (bf16[512,512]{1,0:T(8,128)(2,1)S(1)}, bf16[512,512]{1,0:T(8,128)(2,1)S(1)}, u32[]{:S(2)}, u32[]{:S(2)}) collective-permute-start(bf16[512,512]{1,0:T(8,128)(2,1)S(1)} %slice.237), channel_id=1, source_target_pairs={{0,8},{8,0},{16,24},{24,16},{1,9},{9,1},{17,25},{25,17},{2,10},{10... | collective-permute-start | bytes 1572872 | tf_op jit(solution)/shard_map/ppermute | solution.py:874
  676.4 61.9 %collective-permute-start.38 = (bf16[512,512]{1,0:T(8,128)(2,1)}, bf16[512,512]{1,0:T(8,128)(2,1)}, u32[]{:S(2)}, u32[]{:S(2)}) collective-permute-start(bf16[512,512]{1,0:T(8,128)(2,1)} %add_convert_fusion.10), channel_id=1, source_target_pairs={{0,4},{4,0},{1,5},{5,1},{2,6},{6,2},{3,7},{7,3},{8,12},{12,8},{9,1... | collective-permute-start | bytes 1572872 | tf_op jit(solution)/shard_map/ppermute | solution.py:874
  695.1 43.2 %collective-permute-start.41 = (bf16[512,512]{1,0:T(8,128)(2,1)}, bf16[512,512]{1,0:T(8,128)(2,1)}, u32[]{:S(2)}, u32[]{:S(2)}) collective-permute-start(bf16[512,512]{1,0:T(8,128)(2,1)} %slice.239), channel_id=1, source_target_pairs={{0,16},{8,24},{16,0},{24,8},{1,17},{9,25},{17,1},{25,9},{2,18},{10... | collective-permute-start | bytes 1572872 | tf_op jit(solution)/shard_map/ppermute | solution.py:874
  697.5 40.8 %collective-permute-start.42 = (bf16[512,512]{1,0:T(8,128)(2,1)}, bf16[512,512]{1,0:T(8,128)(2,1)}, u32[]{:S(2)}, u32[]{:S(2)}) collective-permute-start(bf16[512,512]{1,0:T(8,128)(2,1)} %slice.240), channel_id=1, source_target_pairs={{0,8},{8,0},{16,24},{24,16},{1,9},{9,1},{17,25},{25,17},{2,10},{10... | collective-permute-start | bytes 1572872 | tf_op jit(solution)/shard_map/ppermute | solution.py:874
  720.1 36.1 %collective-permute-start.44 = (bf16[512,512]{1,0:T(8,128)(2,1)S(1)}, bf16[512,512]{1,0:T(8,128)(2,1)S(1)}, u32[]{:S(2)}, u32[]{:S(2)}) collective-permute-start(bf16[512,512]{1,0:T(8,128)(2,1)S(1)} %add_convert_fusion.9), channel_id=1, source_target_pairs={{0,4},{4,0},{1,5},{5,1},{2,6},{6,2},{3,7},{7,3},{8,12},{12,8},{9,1... | collective-permute-start | bytes 1572872 | tf_op jit(solution)/shard_map/ppermute | solution.py:874
  (72 other events, 752.9 us)
Sparse Core Ops, SparseCore 0:
  16.2 52.5 all-gather.4
  80.6 50.9 all-gather.6
  133.4 87.5 all-gather.8
  222.7 87.5 all-gather.10
  423.4 84.5 reduce-scatter.14
  511.8 86.4 reduce-scatter.12
  600.5 54.2 reduce-scatter.10
  657.1 96.1 reduce-scatter.8

commit v4 on v3

--- a/solution.py
+++ b/solution.py
@@ -342,7 +342,7 @@
         out_specs=[pl.BlockSpec((blocks // 2, 1, rows, tile), lambda s, i: (0, s, 0, i))] * 2,
         out_shape=outs,
         compiler_params=params(),
-        cost_estimate=cost(2 * count * tokens * cols * width, outs),
+        cost_estimate=cost(2 * count * tokens * cols * width, outs, 0.02),
         name="unproj",
     )(part, *weights)
 
@@ -458,7 +458,7 @@
         out_shape=outs,
         scratch_shapes=[pltpu.VMEM((tokens, HD), F32)] * 2,
         compiler_params=params(),
-        cost_estimate=cost(16 * heads * tokens * tokens * HD, [query, kv, grad, *outs]),
+        cost_estimate=cost(16 * heads * tokens * tokens * HD, [query, kv, grad, *outs], 0.02),
         name="attend_back",
     )(scalars, query, kv, grad, log_total, *tables)
 

time: 805 us -> 805 us (level)
  transfers between devices with their start and end apart: 56 -> 56, of which waited for: 28 -> 28; matrix products, arithmetic and copies ran while one was open for 8% -> 9% of each run, Pallas kernels for 29% -> 29%
where the time goes in v4:
time: 805 us; the launch traced here: 792 us
  waiting for transfers between devices  393 us (49%)
  Pallas kernels  260 us (32%)
  other arithmetic  44.4 us (6%)
  local copies, waits for them, and re-layouts  41.1 us (5%)
  starting transfers between devices  38.9 us (5%)
  between operations  15.3 us (2%)
    ppermute x48, waiting for transfers between devices, swap(): return lax.ppermute(values, axis, [(i, i ^ bits) for i in range(size)])  377 us
    pallas_call x2, Pallas kernels, feed(): pl.pallas_call(functools.partial(feed_kernel, blocks, ready, [per] * halv...  48.2 us
    ppermute x48, starting transfers between devices, swap(): return lax.ppermute(values, axis, [(i, i ^ bits) for i in range(size)])  38.3 us
    pallas_call x2, Pallas kernels, weight_grad(): pl.pallas_call(functools.partial(weight_grad_kernel, len(lefts), halves),...  27.1 us
    pallas_call x2, Pallas kernels, norm_back(): pl.pallas_call(functools.partial(norm_back_kernel, streams, len(parts)),...  26.1 us
    pallas_call x3, Pallas kernels, unproj(): pl.pallas_call(unproj_kernel, grid=(count, width // tile), in_specs=[pl.B...  23.4 us
    pallas_call x1, Pallas kernels, attend_back(): pl.pallas_call(functools.partial(attend_back_kernel, blocks), grid=(heads...  18.3 us
    unnamed x105, local copies, waits for them, and re-layouts  17.5 us
  transfers between devices with their start and end apart: 56, of which 28 were waited for; matrix products, arithmetic and copies ran while one was open for 9% of the time, Pallas kernels for 29%

profile of v4, /device:TPU:0, one launch (start us, length us, event | category | flops | bytes accessed | tf_op | source)
XLA Modules:
  0.0 792.5 jit_solution(13576796625022775719)
XLA Ops:
  16.9 13.2 %front.1 = (bf16[1,256,2048]{2,1,0:T(8,128)(2,1)}, bf16[2,256,2048]{2,1,0:T(8,128)(2,1)}, f32[256,2048]{1,0:T(8,128)}) custom-call(bf16[8,256,2048]{2,1,0:T(8,128)(2,1)} %refs_3_.5, f32[256,32]{1,0:T(8,128)} %copy.80.mix_ref.refs_4_, f32[4,2048]{1,0:T(4,128)} %refs_5_.7, f32[4,2048]{1,0:T(4,128)} %refs_6_.2), custom_call_target="tpu_custom_call" | custom-call | flops 293601280 | bytes 109051904 | tf_op jit(solution)/shard_map/front/pallas_call | solution.py:85
  32.8 42.4 %collective-permute-done.5.refs_2_ = bf16[1,256,2048]{2,1,0:T(8,128)(2,1)} collective-permute-done((bf16[1,256,2048]{2,1,0:T(8,128)(2,1)}, bf16[1,256,2048]{2,1,0:T(8,128)(2,1)}, u32[]{:S(2)}, u32[]{:S(2)}) %collective-permute-start.5) | collective-permute-done | bytes 1048608 | tf_op jit(solution)/shard_map/ppermute | solution.py:874
  91.8 83.0 %collective-permute-done = bf16[512,2048]{1,0:T(8,128)(2,1)} collective-permute-done((bf16[512,2048]{1,0:T(8,128)(2,1)S(1)}, bf16[512,2048]{1,0:T(8,128)(2,1)}, u32[]{:S(2)}, u32[]{:S(2)}) %collective-permute-start) | collective-permute-done | bytes 2097184 | tf_op jit(solution)/shard_map/ppermute | solution.py:874
  178.3 6.8 qkv_proj.2.query_ref
  186.4 10.4 %qkv_proj.3.kv_ref = bf16[2,1024,512]{2,1,0:T(8,128)(2,1)} custom-call(bf16[2,256,2048]{2,1,0:T(8,128)(2,1)} %get-tuple-element.115.refs_0_.refs_4_, bf16[2,256,2048]{2,1,0:T(8,128)(2,1)} %collective-permute-done.7.refs_1_.refs_5_, bf16[2,256,2048]{2,1,0:T(8,128)(2,1)} %collective-permute-done.1.refs_2_.refs_6_, bf16[2,256,2048]{2,1,0:T(8,128)(2,1)} %copy-done.11, ...), custom_call_target="tpu_custom_call" | custom-call | flops 34359738368 | bytes 83886080 | tf_op jit(solution)/shard_map/qkv_proj/pallas_call | solution.py:270
  196.8 14.4 %attend.1 = (bf16[1,1024,512]{2,1,0:T(8,128)(2,1)}, f32[4,1,1024]{2,1,0:T(1,128)}) custom-call(s32[5]{0:T(128)} %pad_add_fusion.1.scalars, bf16[1,1024,512]{2,1,0:T(8,128)(2,1)} %qkv_proj.2.query_ref, bf16[2,1024,512]{2,1,0:T(8,128)(2,1)} %qkv_proj.3.kv_ref), custom_call_target="tpu_custom_call" | custom-call | flops 34359738368 | bytes 33685504 | tf_op jit(solution)/shard_map/attend/pallas_call | solution.py:382
  224.7 25.3 %collective-permute-done.10.refs_2_ = bf16[1,256,2048]{2,1,0:T(8,128)(2,1)S(1)} collective-permute-done((bf16[1,256,2048]{2,1,0:T(8,128)(2,1)S(1)}, bf16[1,256,2048]{2,1,0:T(8,128)(2,1)S(1)}, u32[]{:S(2)}, u32[]{:S(2)}) %collective-permute-start.10) | collective-permute-done | bytes 1048608 | tf_op jit(solution)/shard_map/ppermute | solution.py:874
  256.3 24.6 %collective-permute-done.12.refs_2_ = bf16[256,2048]{1,0:T(8,128)(2,1)S(1)} collective-permute-done((bf16[256,2048]{1,0:T(8,128)(2,1)}, bf16[256,2048]{1,0:T(8,128)(2,1)S(1)}, u32[]{:S(2)}, u32[]{:S(2)}) %collective-permute-start.12) | collective-permute-done | bytes 1048608 | tf_op jit(solution)/shard_map/ppermute | solution.py:874
  284.6 9.9 %expand.1 = (bf16[1024,1024]{1,0:T(8,128)(2,1)}, bf16[1024,1024]{1,0:T(8,128)(2,1)}) custom-call(bf16[256,2048]{1,0:T(8,128)(2,1)} %get-tuple-element.132.refs_0_, bf16[256,2048]{1,0:T(8,128)(2,1)} %copy-done.42, bf16[256,2048]{1,0:T(8,128)(2,1)} %copy-done.41, bf16[256,2048]{1,0:T(8,128)(2,1)} %copy-done.43, ...), custom_call_target="tpu_custom_call" | custom-call | flops 34359738368 | bytes 67108864 | tf_op jit(solution)/shard_map/expand/pallas_call | solution.py:596
  294.5 15.9 %all-gather.11.cloned.1.call-done.refs_5_.refs_8_.refs_9_ = bf16[2048,2048]{1,0:T(8,128)(2,1)} async-done(((bf16[512,2048]{1,0:T(8,128)(2,1)}), bf16[2048,2048]{1,0:T(8,128)(2,1)}) %all-gather.11.cloned.1.call-update) | async-done | bytes 8388624 | tf_op jit(solution)/shard_map/all_gather | solution.py:931
  310.4 21.4 %feed.1 = (bf16[1024,1024]{1,0:T(8,128)(2,1)}, bf16[1024,1024]{1,0:T(8,128)(2,1)}, bf16[2,1,256,2048]{3,2,1,0:T(8,128)(2,1)}, bf16[2,1,256,2048]{3,2,1,0:T(8,128)(2,1)}) custom-call(bf16[256,2048]{1,0:T(8,128)(2,1)} %get-tuple-element.132.refs_0_, bf16[256,2048]{1,0:T(8,128)(2,1)} %copy-done.42, bf16[256,2048]{1,0:T(8,128)(2,1)} %copy-done.41, ...), custom_call_target="tpu_custom_call" | custom-call | flops 103079215104 | bytes 100663296 | tf_op jit(solution)/shard_map/feed/pallas_call | solution.py:681
  342.2 21.7 %collective-permute-done.15.refs_2_ = bf16[1,256,2048]{2,1,0:T(8,128)(2,1)} collective-permute-done((bf16[1,256,2048]{2,1,0:T(8,128)(2,1)S(1)}, bf16[1,256,2048]{2,1,0:T(8,128)(2,1)}, u32[]{:S(2)}, u32[]{:S(2)}) %collective-permute-start.15) | collective-permute-done | bytes 1048608 | tf_op jit(solution)/shard_map/ppermute | solution.py:874
  363.9 10.9 %mixing.1 = (f32[256,2048]{1,0:T(8,128)}, f32[256,36]{1,0:T(8,128)}, f32[256,2048]{1,0:T(8,128)}, bf16[256,2048]{1,0:T(8,128)(2,1)}, f32[8,2048]{1,0:T(8,128)}, /*index=5*/f32[36,2048]{1,0:T(8,128)}, f32[36,36]{1,0:T(8,128)}) custom-call(bf16[2,1,256,2048]{3,2,1,0:T(8,128)(2,1)} %get-tuple-element.136.refs_0_, bf16[2,1,256,2048]{3,2,1,0:T(8,128)(2,1)} %copy-done.23, ...), custom_call_target="tpu_custom_call" | custom-call | flops 12582912000 | bytes 112271872 | tf_op jit(solution)/shard_map/mixing/pallas_call | solution.py:857
  382.5 21.1 %collective-permute-done.19.refs_2_ = bf16[256,2048]{1,0:T(8,128)(2,1)S(1)} collective-permute-done((bf16[256,2048]{1,0:T(8,128)(2,1)}, bf16[256,2048]{1,0:T(8,128)(2,1)S(1)}, u32[]{:S(2)}, u32[]{:S(2)}) %collective-permute-start.19) | collective-permute-done | bytes 1048608 | tf_op jit(solution)/shard_map/ppermute | solution.py:874
  407.2 13.6 %weight_grad.2 = bf16[4,2,512,1024]{3,2,1,0:T(8,128)(2,1)} custom-call(bf16[256,2048]{1,0:T(8,128)(2,1)} %get-tuple-element.151.refs_0_, bf16[256,2048]{1,0:T(8,128)(2,1)} %copy-done.44, bf16[256,2048]{1,0:T(8,128)(2,1)} %copy-done.45, bf16[256,2048]{1,0:T(8,128)(2,1)} %copy-done.46, bf16[1024,1024]{1,0:T(8,128)(2,1)} %get-tuple-element.134.refs_4_, ...), custom_call_target="tpu_custom_call" | custom-call | flops 68719476736 | bytes 134217728 | tf_op jit(solution)/shard_map/weight_grad/pallas_call | solution.py:715
  423.4 26.9 %feed_back.1 = (bf16[1024,1024]{1,0:T(8,128)(2,1)}, bf16[1024,1024]{1,0:T(8,128)(2,1)}, f32[1,1024]{1,0:T(1,128)}, f32[1,1024]{1,0:T(1,128)}, bf16[2,1,256,2048]...) custom-call(bf16[256,2048]{1,0:T(8,128)(2,1)} %get-tuple-element.151.refs_0_, bf16[256,2048]{1,0:T(8,128)(2,1)} %copy-done.44, ...), custom_call_target="tpu_custom_call" | custom-call | flops 137438953472 | bytes 100728832 | tf_op jit(solution)/shard_map/feed_back/pallas_call | solution.py:681
  460.3 13.5 %weight_grad.3 = bf16[4,2,512,1024]{3,2,1,0:T(8,128)(2,1)} custom-call(bf16[256,2048]{1,0:T(8,128)(2,1)} %get-tuple-element.132.refs_0_, bf16[256,2048]{1,0:T(8,128)(2,1)} %copy-done.42, bf16[256,2048]{1,0:T(8,128)(2,1)} %copy-done.41, bf16[256,2048]{1,0:T(8,128)(2,1)} %copy-done.43, bf16[1024,1024]{1,0:T(8,128)(2,1)} %get-tuple-element.159.refs_4_, ...), custom_call_target="tpu_custom_call" | custom-call | flops 68719476736 | bytes 134217728 | tf_op jit(solution)/shard_map/weight_grad/pallas_call | solution.py:715
  473.8 10.4 %collective-permute-done.25.refs_2_ = bf16[1,256,2048]{2,1,0:T(8,128)(2,1)S(1)} collective-permute-done((bf16[1,256,2048]{2,1,0:T(8,128)(2,1)}, bf16[1,256,2048]{2,1,0:T(8,128)(2,1)S(1)}, u32[]{:S(2)}, u32[]{:S(2)}) %collective-permute-start.25) | collective-permute-done | bytes 1048608 | tf_op jit(solution)/shard_map/ppermute | solution.py:874
  485.2 6.7 middle_back.1
  493.5 23.1 %collective-permute-done.27.refs_2_.refs_10_ = bf16[256,2048]{1,0:T(8,128)(2,1)S(1)} collective-permute-done((bf16[256,2048]{1,0:T(8,128)(2,1)}, bf16[256,2048]{1,0:T(8,128)(2,1)S(1)}, u32[]{:S(2)}, u32[]{:S(2)}) %collective-permute-start.27) | collective-permute-done | bytes 1048608 | tf_op jit(solution)/shard_map/ppermute | solution.py:874
  526.3 18.3 %attend_back.1 = (bf16[3,1024,512]{2,1,0:T(8,128)(2,1)}, f32[4,8,128]{2,1,0:T(8,128)}) custom-call(s32[5]{0:T(128)} %pad_add_fusion.1.scalars, bf16[1,1024,512]{2,1,0:T(8,128)(2,1)} %qkv_proj.2.query_ref, bf16[2,1024,512]{2,1,0:T(8,128)(2,1)} %qkv_proj.3.kv_ref, bf16[1024,512]{1,0:T(8,128)(2,1)} %proj.1.g_ref, f32[4,1,1024]{2,1,0:T(1,128)} %get-tuple-element.164.log_ref, ...), custom_call_target="tpu_custom_call" | custom-call | flops 171798688 | bytes 147128 | tf_op jit(solution)/shard_map/attend_back/pallas_call | solution.py:445
  550.8 11.3 %unproj.5 = (bf16[2,2,256,2048]{3,2,1,0:T(8,128)(2,1)}, bf16[2,2,256,2048]{3,2,1,0:T(8,128)(2,1)}) custom-call(bf16[3,1024,512]{2,1,0:T(8,128)(2,1)} %get-tuple-element.170.a_ref.refs_12_, bf16[2048,1024]{1,0:T(8,128)(2,1)} %all-gather.5.cloned.1.call-done.refs_4_.refs_0_, bf16[2048,1024]{1,0:T(8,128)(2,1)} %all-gather.7.cloned.1.call-done.refs_5_.refs_1_), custom_call_target="tpu_custom_call" | custom-call | flops 85899344 | bytes 167772 | tf_op jit(solution)/shard_map/unproj/pallas_call | solution.py:337
  580.4 16.1 %piece_grad.1 = (bf16[2048,512]{1,0:T(8,128)(2,1)}, bf16[2048,512]{1,0:T(8,128)(2,1)}, bf16[2048,512]{1,0:T(8,128)(2,1)}, bf16[2048,512]{1,0:T(8,128)(2,1)}) custom-call(s32[3,4]{1,0:T(4,128)} %pad_add_fusion.table, bf16[1,256,2048]{2,1,0:T(8,128)(2,1)} %get-tuple-element.119.refs_0_, bf16[1,256,2048]{2,1,0:T(8,128)(2,1)} %collective-permute-done.2.refs_1_, ...), custom_call_target="tpu_custom_call" | custom-call | flops 429496736 | bytes 1468006 | tf_op jit(solution)/shard_map/piece_grad/pallas_call | solution.py:773
  602.9 12.2 %norm_back.2 = (f32[1,256,2048]{2,1,0:T(8,128)}, f32[1,16,2048]{2,1,0:T(8,128)}) custom-call(bf16[2,1,256,2048]{3,2,1,0:T(8,128)(2,1)} %get-tuple-element.168.refs_0_, bf16[2,1,256,2048]{3,2,1,0:T(8,128)(2,1)} %collective-permute-done.29.refs_1_, bf16[1,256,2048]{2,1,0:T(8,128)(2,1)} %collective-permute-done.30.refs_2_, bf16[8,256,2048]{2,1,0:T(8,128)(2,1)} %refs_3_.5, ...), custom_call_target="tpu_custom_call" | custom-call | flops 1048576 | bytes 792985 | tf_op jit(solution)/shard_map/norm_back/pallas_call | solution.py:154
  615.1 7.8 collective-permute-done.32
  643.0 22.1 %collective-permute-done.35 = bf16[512,512]{1,0:T(8,128)(2,1)S(1)} collective-permute-done((bf16[512,512]{1,0:T(8,128)(2,1)S(1)}, bf16[512,512]{1,0:T(8,128)(2,1)S(1)}, u32[]{:S(2)}, u32[]{:S(2)}) %collective-permute-start.35) | collective-permute-done | bytes 524320 | tf_op jit(solution)/shard_map/ppermute | solution.py:874
  665.1 11.9 %collective-permute-done.36.refs_2_ = bf16[2,256,2048]{2,1,0:T(8,128)(2,1)} collective-permute-done((bf16[2,256,2048]{2,1,0:T(8,128)(2,1)}, bf16[2,256,2048]{2,1,0:T(8,128)(2,1)}, u32[]{:S(2)}, u32[]{:S(2)}) %collective-permute-start.36) | collective-permute-done | bytes 2097184 | tf_op jit(solution)/shard_map/ppermute | solution.py:874
  680.9 13.9 %norm_back.3 = (f32[2,256,2048]{2,1,0:T(8,128)}, f32[2,16,2048]{2,1,0:T(8,128)}) custom-call(bf16[2,2,256,2048]{3,2,1,0:T(8,128)(2,1)} %get-tuple-element.174.refs_0_, bf16[2,2,256,2048]{3,2,1,0:T(8,128)(2,1)} %collective-permute-done.31.refs_1_, bf16[2,256,2048]{2,1,0:T(8,128)(2,1)} %collective-permute-done.36.refs_2_, bf16[8,256,2048]{2,1,0:T(8,128)(2,1)} %refs_3_.5, ...), custom_call_target="tpu_custom_call" | custom-call | flops 2097152 | bytes 1166540 | tf_op jit(solution)/shard_map/norm_back/pallas_call | solution.py:154
  702.3 17.2 %stack_back.1 = (f32[8,256,2048]{2,1,0:T(8,128)}, f32[256,32]{1,0:T(8,128)}) custom-call(f32[1,256,2048]{2,1,0:T(8,128)} %get-tuple-element.197.refs_0_, f32[2,256,2048]{2,1,0:T(8,128)} %get-tuple-element.198.refs_1_, f32[256,2048]{1,0:T(8,128)} %get-tuple-element.199.refs_2_, bf16[8,256,2048]{2,1,0:T(8,128)(2,1)} %refs_3_.5, f32[256,32]{1,0:T(8,128)} %copy.80.mix_ref.refs_4_), custom_call_target="tpu_custom_call" | custom-call | flops 545259520 | bytes 268697600 | tf_op jit(solution)/shard_map/stack_back/pallas_call | solution.py:208
  723.5 15.8 %collective-permute-done.38 = bf16[512,512]{1,0:T(8,128)(2,1)} collective-permute-done((bf16[512,512]{1,0:T(8,128)(2,1)}, bf16[512,512]{1,0:T(8,128)(2,1)}, u32[]{:S(2)}, u32[]{:S(2)}) %collective-permute-start.38) | collective-permute-done | bytes 524320 | tf_op jit(solution)/shard_map/ppermute | solution.py:874
  741.8 14.3 %collective-permute-done.44 = bf16[512,512]{1,0:T(8,128)(2,1)S(1)} collective-permute-done((bf16[512,512]{1,0:T(8,128)(2,1)S(1)}, bf16[512,512]{1,0:T(8,128)(2,1)S(1)}, u32[]{:S(2)}, u32[]{:S(2)}) %collective-permute-start.44) | collective-permute-done | bytes 524320 | tf_op jit(solution)/shard_map/ppermute | solution.py:874
  766.0 10.5 %collective-permute-done.47 = f32[17,2048]{1,0:T(8,128)S(1)} collective-permute-done((f32[17,2048]{1,0:T(8,128)S(1)}, f32[17,2048]{1,0:T(8,128)S(1)}, u32[]{:S(2)}, u32[]{:S(2)}) %collective-permute-start.47) | collective-permute-done | bytes 139296 | tf_op jit(solution)/shard_map/ppermute | solution.py:874
  (297 shorter events, 190.6 us)
Async XLA Ops:
  7.2 171.1 %all-gather.5.cloned.1.call-start = ((), (), s32[]{:S(2)}) async-start(), calls=%async_computation.4 | async-start | bytes 5242880 | tf_op jit(solution)/shard_map/all_gather | solution.py:931
  16.1 162.3 %all-gather.7.cloned.1.call-start = ((), (), s32[]{:S(2)}) async-start(), calls=%async_computation.5 | async-start | bytes 5242880 | tf_op jit(solution)/shard_map/all_gather | solution.py:931
  30.0 45.2 %collective-permute-start.5 = (bf16[1,256,2048]{2,1,0:T(8,128)(2,1)}, bf16[1,256,2048]{2,1,0:T(8,128)(2,1)}, u32[]{:S(2)}, u32[]{:S(2)}) collective-permute-start(bf16[1,256,2048]{2,1,0:T(8,128)(2,1)} %get-tuple-element.119.refs_0_), channel_id=1, source_target_pairs={{0,2},{2,0},{1,3},{3,1},{4,6},{6,4},{5,7},{7,5},{8,10},{10,8},{9,1... | collective-permute-start | bytes 3145736 | tf_op jit(solution)/shard_map/ppermute | solution.py:874
  31.6 47.8 %collective-permute-start.4 = (bf16[512,1024]{1,0:T(8,128)(2,1)S(1)}, bf16[512,1024]{1,0:T(8,128)(2,1)S(1)}, u32[]{:S(2)}, u32[]{:S(2)}) collective-permute-start(bf16[512,1024]{1,0:T(8,128)(2,1)S(1)} %copy-done.4), channel_id=1, source_target_pairs={{0,4},{4,0},{1,5},{5,1},{2,6},{6,2},{3,7},{7,3},{8,12},{12,8},{9,1... | collective-permute-start | bytes 3145736 | tf_op jit(solution)/shard_map/ppermute | solution.py:874
  80.5 203.2 %all-gather.9.cloned.1.call-start = ((), (), s32[]{:S(2)}) async-start(), calls=%async_computation.6 | async-start | bytes 10485760 | tf_op jit(solution)/shard_map/all_gather | solution.py:931
  83.9 226.5 %all-gather.11.cloned.1.call-start = ((), (), s32[]{:S(2)}) async-start(), calls=%async_computation.7 | async-start | bytes 10485760 | tf_op jit(solution)/shard_map/all_gather | solution.py:931
  85.6 89.2 %collective-permute-start = (bf16[512,2048]{1,0:T(8,128)(2,1)S(1)}, bf16[512,2048]{1,0:T(8,128)(2,1)}, u32[]{:S(2)}, u32[]{:S(2)}) collective-permute-start(bf16[512,2048]{1,0:T(8,128)(2,1)S(1)} %copy-done), channel_id=1, source_target_pairs={{0,4},{4,0},{1,5},{5,1},{2,6},{6,2},{3,7},{7,3},{8,12},{12,8},{9,1... | collective-permute-start | bytes 6291464 | tf_op jit(solution)/shard_map/ppermute | solution.py:874
  85.9 91.2 %collective-permute-start.1 = (bf16[2,256,2048]{2,1,0:T(8,128)(2,1)}, bf16[2,256,2048]{2,1,0:T(8,128)(2,1)}, u32[]{:S(2)}, u32[]{:S(2)}) collective-permute-start(bf16[2,256,2048]{2,1,0:T(8,128)(2,1)} %get-tuple-element.115.refs_0_.refs_4_), channel_id=1, source_target_pairs={{0,2},{2,0},{1,3},{3,1},{4,6},{6,4},{5,7},{7,5},{8,10},{10,8},{9,1... | collective-permute-start | bytes 6291464 | tf_op jit(solution)/shard_map/ppermute | solution.py:874
  85.9 92.4 %collective-permute-start.2 = (bf16[1,256,2048]{2,1,0:T(8,128)(2,1)S(1)}, bf16[1,256,2048]{2,1,0:T(8,128)(2,1)}, u32[]{:S(2)}, u32[]{:S(2)}) collective-permute-start(bf16[1,256,2048]{2,1,0:T(8,128)(2,1)S(1)} %copy-done.19), channel_id=1, source_target_pairs={{0,1},{1,0},{2,3},{3,2},{4,5},{5,4},{6,7},{7,6},{8,9},{9,8},{10,11... | collective-permute-start | bytes 3145736 | tf_op jit(solution)/shard_map/ppermute | solution.py:874
  85.9 99.2 %collective-permute-start.7 = (bf16[2,256,2048]{2,1,0:T(8,128)(2,1)}, bf16[2,256,2048]{2,1,0:T(8,128)(2,1)}, u32[]{:S(2)}, u32[]{:S(2)}) collective-permute-start(bf16[2,256,2048]{2,1,0:T(8,128)(2,1)} %get-tuple-element.115.refs_0_.refs_4_), channel_id=1, source_target_pairs={{0,1},{1,0},{2,3},{3,2},{4,5},{5,4},{6,7},{7,6},{8,9},{9,8},{10,11... | collective-permute-start | bytes 6291464 | tf_op jit(solution)/shard_map/ppermute | solution.py:874
  87.1 91.2 %collective-permute-start.6 = (bf16[1,256,2048]{2,1,0:T(8,128)(2,1)}, bf16[1,256,2048]{2,1,0:T(8,128)(2,1)}, u32[]{:S(2)}, u32[]{:S(2)}) collective-permute-start(bf16[1,256,2048]{2,1,0:T(8,128)(2,1)} %collective-permute-done.5.refs_2_), channel_id=1, source_target_pairs={{0,1},{1,0},{2,3},{3,2},{4,5},{5,4},{6,7},{7,6},{8,9},{9,8},{10,11... | collective-permute-start | bytes 3145736 | tf_op jit(solution)/shard_map/ppermute | solution.py:874
  211.2 351.5 %reduce-scatter.15.cloned.1.call-start = ((), (), s32[]{:S(2)}) async-start(), calls=%async_computation.11 | async-start | bytes 10485760
  224.5 25.5 %collective-permute-start.10 = (bf16[1,256,2048]{2,1,0:T(8,128)(2,1)S(1)}, bf16[1,256,2048]{2,1,0:T(8,128)(2,1)S(1)}, u32[]{:S(2)}, u32[]{:S(2)}) collective-permute-start(bf16[1,256,2048]{2,1,0:T(8,128)(2,1)S(1)} %fusion.1), channel_id=1, source_target_pairs={{0,2},{2,0},{1,3},{3,1},{4,6},{6,4},{5,7},{7,5},{8,10},{10,8},{9,1... | collective-permute-start | bytes 3145736 | tf_op jit(solution)/shard_map/ppermute | solution.py:874
  256.3 25.3 %collective-permute-start.11 = (bf16[256,2048]{1,0:T(8,128)(2,1)}, bf16[256,2048]{1,0:T(8,128)(2,1)S(1)}, u32[]{:S(2)}, u32[]{:S(2)}) collective-permute-start(bf16[256,2048]{1,0:T(8,128)(2,1)} %get-tuple-element.132.refs_0_), channel_id=1, source_target_pairs={{0,1},{1,0},{2,3},{3,2},{4,5},{5,4},{6,7},{7,6},{8,9},{9,8},{10,11... | collective-permute-start | bytes 3145736 | tf_op jit(solution)/shard_map/ppermute | solution.py:874
  338.6 25.4 %collective-permute-start.15 = (bf16[1,256,2048]{2,1,0:T(8,128)(2,1)S(1)}, bf16[1,256,2048]{2,1,0:T(8,128)(2,1)}, u32[]{:S(2)}, u32[]{:S(2)}) collective-permute-start(bf16[1,256,2048]{2,1,0:T(8,128)(2,1)S(1)} %fusion.2), channel_id=1, source_target_pairs={{0,2},{2,0},{1,3},{3,1},{4,6},{6,4},{5,7},{7,5},{8,10},{10,8},{9,1... | collective-permute-start | bytes 3145736 | tf_op jit(solution)/shard_map/ppermute | solution.py:874
  378.2 25.4 %collective-permute-start.19 = (bf16[256,2048]{1,0:T(8,128)(2,1)}, bf16[256,2048]{1,0:T(8,128)(2,1)S(1)}, u32[]{:S(2)}, u32[]{:S(2)}) collective-permute-start(bf16[256,2048]{1,0:T(8,128)(2,1)} %get-tuple-element.151.refs_0_), channel_id=1, source_target_pairs={{0,2},{2,0},{1,3},{3,1},{4,6},{6,4},{5,7},{7,5},{8,10},{10,8},{9,1... | collective-permute-start | bytes 3145736 | tf_op jit(solution)/shard_map/ppermute | solution.py:874
  420.8 29.4 %collective-permute-start.22 = (f32[39,2048]{1,0:T(8,128)S(1)}, f32[39,2048]{1,0:T(8,128)S(1)}, u32[]{:S(2)}, u32[]{:S(2)}) collective-permute-start(f32[39,2048]{1,0:T(8,128)S(1)} %add.177), channel_id=1, source_target_pairs={{0,4},{4,0},{1,5},{5,1},{2,6},{6,2},{3,7},{7,3},{8,12},{12,8},{9,1... | collective-permute-start | bytes 958472 | tf_op jit(solution)/shard_map/ppermute | solution.py:874
  423.3 209.2 %reduce-scatter.13.cloned.1.call-start = ((), (), s32[]{:S(2)}) async-start(), calls=%async_computation.10 | async-start | bytes 10485760
  458.8 25.5 %collective-permute-start.25 = (bf16[1,256,2048]{2,1,0:T(8,128)(2,1)}, bf16[1,256,2048]{2,1,0:T(8,128)(2,1)S(1)}, u32[]{:S(2)}, u32[]{:S(2)}) collective-permute-start(bf16[1,256,2048]{2,1,0:T(8,128)(2,1)} %fusion.3), channel_id=1, source_target_pairs={{0,2},{2,0},{1,3},{3,1},{4,6},{6,4},{5,7},{7,5},{8,10},{10,8},{9,1... | collective-permute-start | bytes 3145736 | tf_op jit(solution)/shard_map/ppermute | solution.py:874
  485.2 293.9 %reduce-scatter.11.cloned.1.call-start = ((), (), s32[]{:S(2)}) async-start(), calls=%async_computation.9 | async-start | bytes 3145728 | tf_op jit(solution)/shard_map/reduce_scatter | solution.py:936
  516.7 28.0 %collective-permute-start.23 = (f32[39,2048]{1,0:T(8,128)S(1)}, f32[39,2048]{1,0:T(8,128)S(1)}, u32[]{:S(2)}, u32[]{:S(2)}) collective-permute-start(f32[39,2048]{1,0:T(8,128)S(1)} %add.178), channel_id=1, source_target_pairs={{0,2},{2,0},{1,3},{3,1},{4,6},{6,4},{5,7},{7,5},{8,10},{10,8},{9,1... | collective-permute-start | bytes 958472 | tf_op jit(solution)/shard_map/ppermute | solution.py:874
  562.7 219.7 %reduce-scatter.9.cloned.1.call-start = ((), (), s32[]{:S(2)}) async-start(), calls=%async_computation.8 | async-start | bytes 3145728 | tf_op jit(solution)/shard_map/reduce_scatter | solution.py:936
  574.3 28.6 %collective-permute-start.30 = (bf16[1,256,2048]{2,1,0:T(8,128)(2,1)S(1)}, bf16[1,256,2048]{2,1,0:T(8,128)(2,1)}, u32[]{:S(2)}, u32[]{:S(2)}) collective-permute-start(bf16[1,256,2048]{2,1,0:T(8,128)(2,1)S(1)} %fusion.4), channel_id=1, source_target_pairs={{0,2},{2,0},{1,3},{3,1},{4,6},{6,4},{5,7},{7,5},{8,10},{10,8},{9,1... | collective-permute-start | bytes 3145736 | tf_op jit(solution)/shard_map/ppermute | solution.py:874
  597.9 25.0 %collective-permute-start.32 = (bf16[1024,512]{1,0:T(8,128)(2,1)S(1)}, bf16[1024,512]{1,0:T(8,128)(2,1)S(1)}, u32[]{:S(2)}, u32[]{:S(2)}) collective-permute-start(bf16[1024,512]{1,0:T(8,128)(2,1)S(1)} %slice.195), channel_id=1, source_target_pairs={{0,8},{8,0},{16,24},{24,16},{1,9},{9,1},{17,25},{25,17},{2,10},{10... | collective-permute-start | bytes 3145736 | tf_op jit(solution)/shard_map/ppermute | solution.py:874
  601.6 75.4 %collective-permute-start.36 = (bf16[2,256,2048]{2,1,0:T(8,128)(2,1)}, bf16[2,256,2048]{2,1,0:T(8,128)(2,1)}, u32[]{:S(2)}, u32[]{:S(2)}) collective-permute-start(bf16[2,256,2048]{2,1,0:T(8,128)(2,1)} %fusion), channel_id=1, source_target_pairs={{0,2},{2,0},{1,3},{3,1},{4,6},{6,4},{5,7},{7,5},{8,10},{10,8},{9,1... | collective-permute-start | bytes 6291464 | tf_op jit(solution)/shard_map/ppermute | solution.py:874
  630.1 64.7 %collective-permute-start.39 = (bf16[1024,512]{1,0:T(8,128)(2,1)}, bf16[1024,512]{1,0:T(8,128)(2,1)}, u32[]{:S(2)}, u32[]{:S(2)}) collective-permute-start(bf16[1024,512]{1,0:T(8,128)(2,1)} %slice.211), channel_id=1, source_target_pairs={{0,8},{8,0},{16,24},{24,16},{1,9},{9,1},{17,25},{25,17},{2,10},{10... | collective-permute-start | bytes 3145736 | tf_op jit(solution)/shard_map/ppermute | solution.py:874
  631.9 62.9 %collective-permute-start.40 = (bf16[1024,512]{1,0:T(8,128)(2,1)}, bf16[1024,512]{1,0:T(8,128)(2,1)}, u32[]{:S(2)}, u32[]{:S(2)}) collective-permute-start(bf16[1024,512]{1,0:T(8,128)(2,1)} %slice.212), channel_id=1, source_target_pairs={{0,16},{8,24},{16,0},{24,8},{1,17},{9,25},{17,1},{25,9},{2,18},{10... | collective-permute-start | bytes 3145736 | tf_op jit(solution)/shard_map/ppermute | solution.py:874
  634.2 31.0 %collective-permute-start.35 = (bf16[512,512]{1,0:T(8,128)(2,1)S(1)}, bf16[512,512]{1,0:T(8,128)(2,1)S(1)}, u32[]{:S(2)}, u32[]{:S(2)}) collective-permute-start(bf16[512,512]{1,0:T(8,128)(2,1)S(1)} %slice.237), channel_id=1, source_target_pairs={{0,8},{8,0},{16,24},{24,16},{1,9},{9,1},{17,25},{25,17},{2,10},{10... | collective-permute-start | bytes 1572872 | tf_op jit(solution)/shard_map/ppermute | solution.py:874
  679.0 60.3 %collective-permute-start.38 = (bf16[512,512]{1,0:T(8,128)(2,1)}, bf16[512,512]{1,0:T(8,128)(2,1)}, u32[]{:S(2)}, u32[]{:S(2)}) collective-permute-start(bf16[512,512]{1,0:T(8,128)(2,1)} %add_convert_fusion.10), channel_id=1, source_target_pairs={{0,4},{4,0},{1,5},{5,1},{2,6},{6,2},{3,7},{7,3},{8,12},{12,8},{9,1... | collective-permute-start | bytes 1572872 | tf_op jit(solution)/shard_map/ppermute | solution.py:874
  697.3 42.0 %collective-permute-start.41 = (bf16[512,512]{1,0:T(8,128)(2,1)}, bf16[512,512]{1,0:T(8,128)(2,1)}, u32[]{:S(2)}, u32[]{:S(2)}) collective-permute-start(bf16[512,512]{1,0:T(8,128)(2,1)} %slice.239), channel_id=1, source_target_pairs={{0,16},{8,24},{16,0},{24,8},{1,17},{9,25},{17,1},{25,9},{2,18},{10... | collective-permute-start | bytes 1572872 | tf_op jit(solution)/shard_map/ppermute | solution.py:874
  699.7 39.6 %collective-permute-start.42 = (bf16[512,512]{1,0:T(8,128)(2,1)}, bf16[512,512]{1,0:T(8,128)(2,1)}, u32[]{:S(2)}, u32[]{:S(2)}) collective-permute-start(bf16[512,512]{1,0:T(8,128)(2,1)} %slice.240), channel_id=1, source_target_pairs={{0,8},{8,0},{16,24},{24,16},{1,9},{9,1},{17,25},{25,17},{2,10},{10... | collective-permute-start | bytes 1572872 | tf_op jit(solution)/shard_map/ppermute | solution.py:874
  722.3 33.8 %collective-permute-start.44 = (bf16[512,512]{1,0:T(8,128)(2,1)S(1)}, bf16[512,512]{1,0:T(8,128)(2,1)S(1)}, u32[]{:S(2)}, u32[]{:S(2)}) collective-permute-start(bf16[512,512]{1,0:T(8,128)(2,1)S(1)} %add_convert_fusion.9), channel_id=1, source_target_pairs={{0,4},{4,0},{1,5},{5,1},{2,6},{6,2},{3,7},{7,3},{8,12},{12,8},{9,1... | collective-permute-start | bytes 1572872 | tf_op jit(solution)/shard_map/ppermute | solution.py:874
  (72 other events, 780.4 us)
Sparse Core Ops, SparseCore 0:
  16.2 52.5 all-gather.4
  80.6 50.9 all-gather.6
  133.4 87.5 all-gather.8
  222.7 87.5 all-gather.10
  423.4 84.5 reduce-scatter.14
  511.8 86.4 reduce-scatter.12
  600.5 54.3 reduce-scatter.10
  657.2 94.9 reduce-scatter.8
